TPU v7x, 32 devices: a whole 2x2x4 slice. The times are simulated.
32 devices in a mesh: dp: 8 (over z, x), mp: 4 (over y, core).
Axes of the slice: x: 2, y: 2, z: 4, core: 2. Of those that a mesh axis runs over, the one named last changes fastest.
Arguments:
- layer_input: bfloat16 [4096, 1024], P(('dp', 'mp')), may hold values from -6 to 6
- first_gain: float32 [1024], replicated, may hold values from 0.25 to 1.75
- query_weight: bfloat16 [1024, 1024], P('dp', 'mp'), may hold values from -0.1875 to 0.1875
- key_matrix: bfloat16 [1024, 512], P('dp', 'mp'), may hold values from -0.1875 to 0.1875
- value_matrix: bfloat16 [1024, 512], P('dp', 'mp'), may hold values from -0.1875 to 0.1875
- output_weight: bfloat16 [1024, 1024], P('dp', 'mp'), may hold values from -1 to 1
- second_gain: float32 [1024], replicated, may hold values from 0.25 to 1.75
- gate_weight: bfloat16 [32, 1024, 512], P('dp'), may hold values from -0.1875 to 0.1875
- up_weight: bfloat16 [32, 1024, 512], P('dp'), may hold values from -0.1875 to 0.1875
- down_weight: bfloat16 [32, 512, 1024], P('dp'), may hold values from -1 to 1
- routes: int32 [4096, 8], P(('dp', 'mp')), may hold values from 0 to 31, all different within a row; in each aligned block of 128 rows (0 to 127, 128 to 255, ...) at most 40 rows name the same one
- combine: float32 [4096, 8], P(('dp', 'mp')), may hold values from 0.05 to 0.25
- upstream: bfloat16 [4096, 1024], P(('dp', 'mp')), may hold values from -6 to 6
Outputs:
- layer_output: bfloat16 [4096, 1024], P(('dp', 'mp'))
- input_grad: float32 [4096, 1024], P(('dp', 'mp'))
- first_gain_grad: float32 [1024], replicated
- second_gain_grad: float32 [1024], replicated
- query_grad: float32 [1024, 1024], P('dp', 'mp')
- key_grad: float32 [1024, 512], P('dp', 'mp')
- value_grad: float32 [1024, 512], P('dp', 'mp')
- output_weight_grad: float32 [1024, 1024], P('dp', 'mp')
- gate_grad: float32 [32, 1024, 512], P('dp')
- up_grad: float32 [32, 1024, 512], P('dp')
- down_grad: float32 [32, 512, 1024], P('dp')
Inputs may be any that keep to these rules, and one draw needn't show every extreme that they name: `routes`: each row names 8 different experts; in each aligned block of 128 rows (the rows of one device) no expert is named by more than 40 rows, a bound that some block reaches.
All inputs are finite; a program needn't handle non-finite values.
Results may differ from a plain program's by a relative error of at most 0.023.
Values may be sent and summed in bfloat16 or wider, within the bound.
No kernel may reach another device: no remote copies, remote signals or barrier semaphores. Data moves between devices by JAX's collectives and lax.ppermute only.
A program may use at most 192 MiB of HBM per device.

v0:
```python
import jax
import jax.numpy as jnp
from jax import lax
from jax.sharding import PartitionSpec as P

HEAD_SIZE = 64
EXPERTS = 32
FF = 512
SEQUENCE_TOKENS = 4096


epsilon = 1e-06
theta = 10000.0
masked = -1e30


def passed_along(value, axis, steps):
    count = lax.axis_size(axis)
    first, last = (max(0, -steps), min(count, count - steps))
    return lax.ppermute(value, axis, [(source, source + steps) for source in range(first, last)])


def contract(left, right, left_dim, right_dim):
    return lax.dot_general(
        left, right, (((left_dim,), (right_dim,)), ((), ())), preferred_element_type=jnp.float32
    )


def rotation(token_positions, depth):
    half = depth // 2
    freqs = theta ** (-jnp.arange(half, dtype=jnp.float32) * 2.0 / depth)
    angles = token_positions.astype(jnp.float32)[:, None] * freqs[None, :]
    return (jnp.cos(angles)[:, None, :], jnp.sin(angles)[:, None, :])


def apply_rotary(value_rows, cosine, sine):
    half = value_rows.shape[-1] // 2
    first = value_rows[..., :half]
    second = value_rows[..., half:]
    return jnp.concatenate(
        [first * cosine - second * sine, second * cosine + first * sine], axis=-1
    )


def block_scores(query_rows, keys_block, query_pos, key_pos, scale):
    scores = (
        jnp.einsum("thgd,nhd->hgtn", query_rows, keys_block, preferred_element_type=jnp.float32)
        * scale
    )
    allowed = (key_pos[None, :] <= query_pos[:, None]) & (key_pos[None, :] >= 0)
    return jnp.where(allowed, scores, masked)


def send_slots(payload):
    return lax.all_to_all(payload, "dp", split_axis=0, concat_axis=0, tiled=True)


def shards(
    layer_input,
    first_gain,
    query_weight,
    key_matrix,
    value_matrix,
    output_weight,
    second_gain,
    gate_weight,
    up_weight,
    down_weight,
    routes,
    combine,
    upstream,
):
    rows, width = layer_input.shape
    topk = routes.shape[1]
    most = max(2, 5 * rows * topk // (4 * EXPERTS))
    devices = lax.axis_size("dp")
    pieces_dev = gate_weight.shape[0]
    split = FF // gate_weight.shape[2]
    local_q = query_weight.shape[1] // HEAD_SIZE
    local_kv = key_matrix.shape[1] // HEAD_SIZE
    query_group = local_q // local_kv
    scale = HEAD_SIZE ** (-0.5)
    inputs_f = layer_input.astype(jnp.float32)
    first_scale = lax.rsqrt(jnp.mean(inputs_f * inputs_f, axis=-1, keepdims=True) + epsilon)
    first_hat = inputs_f * first_scale
    leading_norm = (first_hat * first_gain).astype(jnp.bfloat16)
    sequence_rows = lax.all_gather(leading_norm, "mp", axis=0, tiled=True)
    tokens = sequence_rows.shape[0]
    span = SEQUENCE_TOKENS // tokens
    full_query, full_key, full_value, full_out = (
        lax.all_gather(query_weight, "dp", axis=0, tiled=True),
        lax.all_gather(key_matrix, "dp", axis=0, tiled=True),
        lax.all_gather(value_matrix, "dp", axis=0, tiled=True),
        lax.all_gather(output_weight, "dp", axis=0, tiled=True),
    )
    unrotated_query = jnp.dot(sequence_rows, full_query, preferred_element_type=jnp.float32)
    unrotated_key = jnp.dot(sequence_rows, full_key, preferred_element_type=jnp.float32)
    values_own = (
        jnp.dot(sequence_rows, full_value, preferred_element_type=jnp.float32)
        .astype(jnp.bfloat16)
        .reshape(tokens, local_kv, HEAD_SIZE)
    )
    offset = lax.axis_index("dp") % span
    query_pos = offset * tokens + jnp.arange(tokens, dtype=jnp.int32)
    cosine, sine = rotation(query_pos, HEAD_SIZE)
    query_rows = apply_rotary(
        unrotated_query.reshape(tokens, local_q, HEAD_SIZE), cosine, sine
    ).astype(jnp.bfloat16)
    query_rows = query_rows.reshape(tokens, local_kv, query_group, HEAD_SIZE)
    keys_own = apply_rotary(
        unrotated_key.reshape(tokens, local_kv, HEAD_SIZE), cosine, sine
    ).astype(jnp.bfloat16)
    key_list = [keys_own]
    value_list = [values_own]
    for step in range(1, span):
        earlier_key, earlier_value = passed_along((keys_own, values_own), "dp", step)
        key_list.insert(0, earlier_key)
        value_list.insert(0, earlier_value)
    all_keys = jnp.concatenate(key_list, axis=0)
    all_values = jnp.concatenate(value_list, axis=0)
    first_key = (offset - span + 1) * tokens
    key_pos = first_key + jnp.arange(span * tokens, dtype=jnp.int32)
    key_block = min(512, span * tokens)
    block_count = span * tokens // key_block

    def block_live(lower):
        return first_key + lower + key_block > 0

    running_top = jnp.full((local_kv, query_group, tokens), masked, jnp.float32)
    running_total = jnp.zeros((local_kv, query_group, tokens), jnp.float32)
    for index in range(block_count):
        lower = index * key_block

        def stats_step(state, lower=lower):
            top_now, total_now = state
            scores = block_scores(
                query_rows,
                all_keys[lower : lower + key_block],
                query_pos,
                key_pos[lower : lower + key_block],
                scale,
            )
            new_top = jnp.maximum(top_now, jnp.max(scores, axis=-1))
            new_total = total_now * jnp.exp(top_now - new_top) + jnp.sum(
                jnp.exp(scores - new_top[..., None]), axis=-1
            )
            return (new_top, new_total)

        running_top, running_total = lax.cond(
            block_live(lower), stats_step, lambda state: state, (running_top, running_total)
        )
    logsum = running_top + jnp.log(running_total)
    attended = jnp.zeros((tokens, local_kv, query_group, HEAD_SIZE), jnp.float32)
    for index in range(block_count):
        lower = index * key_block

        def attend_step(total, lower=lower):
            scores = block_scores(
                query_rows,
                all_keys[lower : lower + key_block],
                query_pos,
                key_pos[lower : lower + key_block],
                scale,
            )
            probs = jnp.exp(scores - logsum[..., None]).astype(jnp.bfloat16)
            return total + jnp.einsum(
                "hgtn,nhd->thgd",
                probs,
                all_values[lower : lower + key_block],
                preferred_element_type=jnp.float32,
            )

        attended = lax.cond(block_live(lower), attend_step, lambda total: total, attended)
    attended_low = attended.reshape(tokens, local_q * HEAD_SIZE).astype(jnp.bfloat16)
    branch_part = contract(attended_low, full_out, 1, 1)
    branch = lax.psum_scatter(
        branch_part.astype(jnp.bfloat16), "mp", scatter_dimension=0, tiled=True
    ).astype(jnp.float32)
    middle = inputs_f + branch
    second_scale = lax.rsqrt(jnp.mean(middle * middle, axis=-1, keepdims=True) + epsilon)
    second_hat = middle * second_scale
    second_norm = (second_hat * second_gain).astype(jnp.bfloat16)
    chosen = jnp.sum(
        (routes[:, :, None] == jnp.arange(EXPERTS, dtype=jnp.int32)[None, None, :]).astype(
            jnp.int32
        ),
        axis=1,
    )
    before = jnp.cumsum(chosen, axis=0) - chosen
    rank = jnp.take_along_axis(before, routes, axis=1)
    slot = routes * most + rank
    pair = (
        jnp.full((EXPERTS * most,), rows * topk, jnp.int32)
        .at[slot.reshape(-1)]
        .set(jnp.arange(rows * topk, dtype=jnp.int32))
    )
    token_of = pair // topk
    padded_norm = jnp.concatenate([second_norm, jnp.zeros((1, width), jnp.bfloat16)], axis=0)
    gathered = padded_norm[token_of].reshape(EXPERTS, 1, most, width)
    dispatched = jnp.broadcast_to(gathered, (EXPERTS, split, most, width)).reshape(
        devices, pieces_dev, most, width
    )
    padded_up = jnp.concatenate([upstream, jnp.zeros((1, width), jnp.bfloat16)], axis=0)
    weights_flat = jnp.concatenate([combine.reshape(-1), jnp.zeros((1,), jnp.float32)], axis=0)
    slot_weight = weights_flat[pair]
    slot_grads = (padded_up[token_of].astype(jnp.float32) * slot_weight[:, None]).astype(
        jnp.bfloat16
    )
    slot_grads = jnp.broadcast_to(
        slot_grads.reshape(EXPERTS, 1, most, width), (EXPERTS, split, most, width)
    ).reshape(devices, pieces_dev, most, width)
    received = send_slots(dispatched)
    gate = jnp.einsum("spmd,pdf->spmf", received, gate_weight, preferred_element_type=jnp.float32)
    upper = jnp.einsum("spmd,pdf->spmf", received, up_weight, preferred_element_type=jnp.float32)
    sigmoid = jax.nn.sigmoid(gate)
    activated = gate * sigmoid
    hidden = (activated * upper).astype(jnp.bfloat16)
    produced = jnp.einsum(
        "spmf,pfd->spmd", hidden, down_weight, preferred_element_type=jnp.float32
    ).astype(jnp.bfloat16)
    returned = lax.all_to_all(produced, "dp", split_axis=0, concat_axis=0, tiled=True)
    merged = jnp.sum(returned.reshape(EXPERTS, split, most, width).astype(jnp.float32), axis=1)
    merged = merged.reshape(EXPERTS * most, width)
    mixture = jnp.sum(merged[slot] * combine[:, :, None], axis=1)
    layer_output = (middle + mixture).astype(jnp.bfloat16)
    upstream_f = upstream.astype(jnp.float32)
    received_grads = send_slots(slot_grads)
    hidden_grad = jnp.einsum(
        "spmd,pfd->spmf", received_grads, down_weight, preferred_element_type=jnp.float32
    )
    gate_low = (hidden_grad * upper * (sigmoid * (1.0 + gate * (1.0 - sigmoid)))).astype(
        jnp.bfloat16
    )
    upper_low = (hidden_grad * activated).astype(jnp.bfloat16)
    slot_input_grad = (
        jnp.einsum("spmf,pdf->spmd", gate_low, gate_weight, preferred_element_type=jnp.float32)
        + jnp.einsum("spmf,pdf->spmd", upper_low, up_weight, preferred_element_type=jnp.float32)
    ).astype(jnp.bfloat16)
    gate_sum = jnp.einsum("spmd,spmf->pdf", received, gate_low, preferred_element_type=jnp.float32)
    upper_sum = jnp.einsum(
        "spmd,spmf->pdf", received, upper_low, preferred_element_type=jnp.float32
    )
    down_sum = jnp.einsum(
        "spmf,spmd->pfd", hidden, received_grads, preferred_element_type=jnp.float32
    )
    gate_grad, up_grad, down_grad = (
        lax.psum(gate_sum.astype(jnp.bfloat16), "mp").astype(jnp.float32),
        lax.psum(upper_sum.astype(jnp.bfloat16), "mp").astype(jnp.float32),
        lax.psum(down_sum.astype(jnp.bfloat16), "mp").astype(jnp.float32),
    )
    back = lax.all_to_all(slot_input_grad, "dp", split_axis=0, concat_axis=0, tiled=True)
    back_merged = jnp.sum(back.reshape(EXPERTS, split, most, width).astype(jnp.float32), axis=1)
    back_merged = back_merged.reshape(EXPERTS * most, width)
    norm_two_grad = jnp.sum(back_merged[slot], axis=1)
    second_gain_part = jnp.sum(norm_two_grad * second_hat, axis=0)
    weighted_two = norm_two_grad * second_gain
    middle_grad = upstream_f + second_scale * (
        weighted_two - second_hat * jnp.mean(weighted_two * second_hat, axis=-1, keepdims=True)
    )
    branch_low = middle_grad.astype(jnp.bfloat16)
    branch_rows = lax.all_gather(branch_low, "mp", axis=0, tiled=True)
    full_query, full_key, full_value, full_out = (
        lax.all_gather(query_weight, "dp", axis=0, tiled=True),
        lax.all_gather(key_matrix, "dp", axis=0, tiled=True),
        lax.all_gather(value_matrix, "dp", axis=0, tiled=True),
        lax.all_gather(output_weight, "dp", axis=0, tiled=True),
    )
    attended_grad = jnp.dot(branch_rows, full_out, preferred_element_type=jnp.float32).astype(
        jnp.bfloat16
    )
    attended_grad4 = attended_grad.reshape(tokens, local_kv, query_group, HEAD_SIZE)
    delta = jnp.transpose(
        jnp.sum(attended_grad4.astype(jnp.float32) * attended, axis=-1), (1, 2, 0)
    )
    query_rot_grad = jnp.zeros((tokens, local_kv, query_group, HEAD_SIZE), jnp.float32)
    key_parts = []
    value_parts = []
    for index in range(block_count):
        lower = index * key_block

        def grad_step(query_total, lower=lower):
            keys_block = all_keys[lower : lower + key_block]
            values_block = all_values[lower : lower + key_block]
            scores = block_scores(
                query_rows, keys_block, query_pos, key_pos[lower : lower + key_block], scale
            )
            probs = jnp.exp(scores - logsum[..., None])
            prob_grad = jnp.einsum(
                "thgd,nhd->hgtn", attended_grad4, values_block, preferred_element_type=jnp.float32
            )
            score_grad = (probs * (prob_grad - delta[..., None])).astype(jnp.bfloat16)
            value_part = jnp.einsum(
                "hgtn,thgd->nhd",
                probs.astype(jnp.bfloat16),
                attended_grad4,
                preferred_element_type=jnp.float32,
            )
            query_next = query_total + jnp.einsum(
                "hgtn,nhd->thgd", score_grad, keys_block, preferred_element_type=jnp.float32
            )
            key_part = jnp.einsum(
                "hgtn,thgd->nhd", score_grad, query_rows, preferred_element_type=jnp.float32
            )
            return (query_next, key_part, value_part)

        def grad_skip(query_total):
            empty = jnp.zeros((key_block, local_kv, HEAD_SIZE), jnp.float32)
            return (query_total, empty, empty)

        query_rot_grad, key_part, value_part = lax.cond(
            block_live(lower), grad_step, grad_skip, query_rot_grad
        )
        key_parts.append(key_part)
        value_parts.append(value_part)
    key_all_grad = jnp.concatenate(key_parts, axis=0) * scale
    value_all_grad = jnp.concatenate(value_parts, axis=0)
    query_rot_grad = query_rot_grad * scale
    own_start = (span - 1) * tokens
    key_total = key_all_grad[own_start:]
    value_total = value_all_grad[own_start:]
    for step in range(1, span):
        start = (span - 1 - step) * tokens
        got_key, got_value = (
            passed_along(
                key_all_grad[start : start + tokens].astype(jnp.bfloat16), "dp", -step
            ).astype(jnp.float32),
            passed_along(
                value_all_grad[start : start + tokens].astype(jnp.bfloat16), "dp", -step
            ).astype(jnp.float32),
        )
        key_total = key_total + got_key
        value_total = value_total + got_value
    query_plain_grad = (
        apply_rotary(query_rot_grad.reshape(tokens, local_q, HEAD_SIZE), cosine, -sine)
        .astype(jnp.bfloat16)
        .reshape(tokens, local_q * HEAD_SIZE)
    )
    key_plain_grad = (
        apply_rotary(key_total, cosine, -sine)
        .astype(jnp.bfloat16)
        .reshape(tokens, local_kv * HEAD_SIZE)
    )
    value_plain_grad = value_total.astype(jnp.bfloat16).reshape(tokens, local_kv * HEAD_SIZE)
    input_part = (
        contract(query_plain_grad, full_query, 1, 1)
        + contract(key_plain_grad, full_key, 1, 1)
        + contract(value_plain_grad, full_value, 1, 1)
    )
    norm_one_grad = lax.psum_scatter(
        input_part.astype(jnp.bfloat16), "mp", scatter_dimension=0, tiled=True
    ).astype(jnp.float32)
    weight_block = lax.psum_scatter(
        jnp.concatenate(
            [
                contract(sequence_rows, query_plain_grad, 0, 0),
                contract(sequence_rows, key_plain_grad, 0, 0),
                contract(sequence_rows, value_plain_grad, 0, 0),
                contract(branch_rows, attended_low, 0, 0),
            ],
            axis=1,
        ),
        "dp",
        scatter_dimension=0,
        tiled=True,
    )
    query_cols = local_q * HEAD_SIZE
    kv_cols = local_kv * HEAD_SIZE
    query_grad = weight_block[:, :query_cols]
    key_grad = weight_block[:, query_cols : query_cols + kv_cols]
    value_grad = weight_block[:, query_cols + kv_cols : query_cols + 2 * kv_cols]
    output_weight_grad = weight_block[:, query_cols + 2 * kv_cols :]
    first_gain_part = jnp.sum(norm_one_grad * first_hat, axis=0)
    weighted_one = norm_one_grad * first_gain
    input_grad = middle_grad + first_scale * (
        weighted_one - first_hat * jnp.mean(weighted_one * first_hat, axis=-1, keepdims=True)
    )
    first_gain_grad, second_gain_grad = lax.psum((first_gain_part, second_gain_part), ("dp", "mp"))
    return (
        layer_output,
        input_grad,
        first_gain_grad,
        second_gain_grad,
        query_grad,
        key_grad,
        value_grad,
        output_weight_grad,
        gate_grad,
        up_grad,
        down_grad,
    )


def solution(mesh):
    in_specs = (
        P(("dp", "mp"), None),
        P(),
        P("dp", "mp"),
        P("dp", "mp"),
        P("dp", "mp"),
        P("dp", "mp"),
        P(),
        P("dp", None, None),
        P("dp", None, None),
        P("dp", None, None),
        P(("dp", "mp"), None),
        P(("dp", "mp"), None),
        P(("dp", "mp"), None),
    )
    out_specs = (
        P(("dp", "mp"), None),
        P(("dp", "mp"), None),
        P(),
        P(),
        P("dp", "mp"),
        P("dp", "mp"),
        P("dp", "mp"),
        P("dp", "mp"),
        P("dp", None, None),
        P("dp", None, None),
        P("dp", None, None),
    )
    return jax.shard_map(shards, mesh=mesh, in_specs=in_specs, out_specs=out_specs, check_vma=False)
```

profile of v0, /device:TPU:0, one launch (start us, length us, event | category | flops | bytes accessed | tf_op | source)
XLA Modules:
  0.0 844.7 jit_solution(3751684973854212432)
XLA Ops:
  10.3 32.8 %all_gather.23 = bf16[1024,128]{1,0:T(8,128)(2,1)S(1)} all-gather(bf16[128,128]{1,0:T(8,128)(2,1)} %param.64), channel_id=1, replica_groups=mesh['dp'=8,'mp'=4] {'dp'}, dimensions={0}, use_global_device_ids=true | all-gather | bytes 294912 | tf_op jit(solution)/shard_map/all_gather | solution.py:92
  43.1 31.1 %all_gather.25 = bf16[1024,128]{1,0:T(8,128)(2,1)S(1)} all-gather(bf16[128,128]{1,0:T(8,128)(2,1)} %param.65), channel_id=1, replica_groups=mesh['dp'=8,'mp'=4] {'dp'}, dimensions={0}, use_global_device_ids=true | all-gather | bytes 294912 | tf_op jit(solution)/shard_map/all_gather | solution.py:93
  75.1 31.8 %all_gather.24 = bf16[1024,256]{1,0:T(8,128)(2,1)S(1)} all-gather(bf16[128,256]{1,0:T(8,128)(2,1)} %param.63), channel_id=1, replica_groups=mesh['dp'=8,'mp'=4] {'dp'}, dimensions={0}, use_global_device_ids=true | all-gather | bytes 589824 | tf_op jit(solution)/shard_map/all_gather | solution.py:91
  106.9 31.9 %all_gather.26 = bf16[1024,256]{1,0:T(8,128)(2,1)S(1)} all-gather(bf16[128,256]{1,0:T(8,128)(2,1)} %param.66), channel_id=1, replica_groups=mesh['dp'=8,'mp'=4] {'dp'}, dimensions={0}, use_global_device_ids=true | all-gather | bytes 589824 | tf_op jit(solution)/shard_map/all_gather | solution.py:94
  140.8 6.0 collective-permute-start
  150.7 2.5 collective-permute-start.4
  156.8 3.1 collective-permute-start.6
  159.9 5.6 collective-permute-start.7
  165.5 1.9 collective-permute-start.8
  168.2 5.8 collective-permute-start.9
  174.3 1.9 collective-permute-start.10
  176.2 21.4 %collective-permute-start.11 = (bf16[512,2,64]{0,2,1:T(8,128)(2,1)S(1)}, bf16[512,2,64]{0,2,1:T(8,128)(2,1)}, u32[]{:S(2)}, u32[]{:S(2)}) collective-permute-start(bf16[512,2,64]{0,2,1:T(8,128)(2,1)S(1)} %bitcast.912), channel_id=1, source_target_pairs={{0,12},{4,16},{8,20},{12,24},{16,28},{1,13},{5,17},{9,21},{13,25},... | collective-permute-start | bytes 393224 | tf_op jit(solution)/shard_map/ppermute | solution.py:20
  197.7 4.1 conditional.31
  201.8 2.9 collective-permute-start.12
  204.7 6.2 collective-permute-start.13
  212.8 3.9 conditional.39
  219.5 7.1 gather_fusion.5
  227.0 4.3 scatter_custom_fusion
  231.4 21.3 %reduce-scatter.4.cloned.1.call-done = bf16[128,1024]{1,0:T(8,128)(2,1)} async-done(((bf16[512,1024]{1,0:T(8,128)(2,1)}), bf16[128,1024]{1,0:T(8,128)(2,1)}) %reduce-scatter.4.cloned.1.call-update) | async-done | bytes 262160 | tf_op jit(solution)/shard_map/reduce_scatter | solution.py:176
  254.9 5.1 gather_fusion
  260.0 5.5 all-to-all-start
  266.5 5.1 gather_fusion.2
  272.3 7.1 gather_fusion.3
  279.5 3.7 fusion.254
  283.2 41.8 %all-to-all-done = bf16[8,4,40,1024]{3,2,1,0:T(8,128)(2,1)S(1)} async-done(((bf16[8,4,40,1024]{3,2,1,0:T(8,128)(2,1)}), bf16[8,4,40,1024]{3,2,1,0:T(8,128)(2,1)S(1)}, u32[]{:S(2)}, u32[]{:S(2)}) %all-to-all-start) | async-done | bytes 2621472 | tf_op jit(solution)/shard_map/all_to_all | solution.py:55
  325.0 4.6 all-to-all-start.2
  329.6 5.4 fusion.257
  335.0 3.0 fusion.261
  338.0 50.6 %all-to-all-done.2 = bf16[8,4,40,1024]{3,2,1,0:T(8,128)(2,1)} async-done(((bf16[8,4,40,1024]{3,2,1,0:T(8,128)(2,1)}), bf16[8,4,40,1024]{3,2,1,0:T(8,128)(2,1)}, u32[]{:S(2)}, u32[]{:S(2)}) %all-to-all-start.2) | async-done | bytes 2621472 | tf_op jit(solution)/shard_map/all_to_all | solution.py:55
  388.6 8.2 fusion.270
  403.3 4.4 all-to-all-start.3
  408.3 5.7 bitcast_convert_fusion.2
  414.0 52.7 %all-to-all-done.3 = bf16[8,4,40,1024]{3,2,1,0:T(8,128)(2,1)} async-done(((bf16[8,4,40,1024]{3,2,1,0:T(8,128)(2,1)}), bf16[8,4,40,1024]{3,2,1,0:T(8,128)(2,1)}, u32[]{:S(2)}, u32[]{:S(2)}) %all-to-all-start.3) | async-done | bytes 2621472 | tf_op jit(solution)/shard_map/all_to_all | solution.py:251
  466.7 4.7 bitcast_convert_fusion.3
  471.5 8.8 %gather_fusion.4 = f32[1024,1024]{1,0:T(8,128)} fusion(f32[1280,1024]{1,0:T(8,128)} %bitcast_convert_fusion.3, s32[1024]{0:T(1024)S(1)} %broadcast_clamp_fusion), kind=kCustom, calls=%fused_computation.4 | custom fusion | bytes 8392704 | tf_op jit(solution)/shard_map/gather | solution.py:254
  480.3 3.3 bitcast_reduce_fusion
  485.5 5.8 bitcast_convert_fusion.1
  491.3 6.2 bitcast_convert_fusion
  497.5 2.9 all-gather.5.cloned.1.call-done
  500.4 2.4 multiply_reduce_fusion.1
  505.9 5.8 conditional.43
  514.2 4.7 conditional.46
  519.7 8.0 conditional.47
  521.7 2.5 fusion.237
  525.5 2.2 fusion.245
  542.4 40.7 %collective-permute-done.27 = bf16[512,2,64]{0,2,1:T(8,128)(2,1)S(1)} collective-permute-done((bf16[512,2,64]{0,2,1:T(8,128)(2,1)S(1)}, bf16[512,2,64]{0,2,1:T(8,128)(2,1)S(1)}, u32[]{:S(2)}, u32[]{:S(2)}) %collective-permute-start.27) | collective-permute-done | bytes 131104 | tf_op jit(solution)/shard_map/ppermute | solution.py:20
  585.8 4.3 collective-permute-done.22
  598.7 4.8 collective-permute-done.20
  607.2 6.6 collective-permute-done.18
  618.0 3.9 convert_bitcast_fusion
  623.7 10.0 %all-to-all-start.1 = ((bf16[8,4,40,1024]{3,2,1,0:T(8,128)(2,1)}), bf16[8,4,40,1024]{3,2,1,0:T(8,128)(2,1)}, u32[]{:S(2)}, u32[]{:S(2)}) async-start(bf16[8,4,40,1024]{3,2,1,0:T(8,128)(2,1)} %copy.277), calls=%async_computation.2 | async-start | bytes 5242880 | tf_op jit(solution)/shard_map/all_to_all | solution.py:221
  635.4 1.9 pad_maximum_fusion
  637.3 55.3 %all-to-all-done.1 = bf16[8,4,40,1024]{3,2,1,0:T(8,128)(2,1)} async-done(((bf16[8,4,40,1024]{3,2,1,0:T(8,128)(2,1)}), bf16[8,4,40,1024]{3,2,1,0:T(8,128)(2,1)}, u32[]{:S(2)}, u32[]{:S(2)}) %all-to-all-start.1) | async-done | bytes 2621472 | tf_op jit(solution)/shard_map/all_to_all | solution.py:221
  692.6 4.8 bitcast_convert_fusion.4
  697.4 8.9 %gather_fusion.1 = f32[1024,1024]{1,0:T(8,128)} fusion(f32[1280,1024]{1,0:T(8,128)} %bitcast_convert_fusion.4, s32[1024]{0:T(1024)S(1)} %broadcast_clamp_fusion), kind=kCustom, calls=%fused_computation.1 | custom fusion | bytes 8392704 | tf_op jit(solution)/shard_map/gather | solution.py:224
  706.3 3.4 fusion.267
  709.7 15.5 %all-reduce.6.cloned.1.call-done = (bf16[4,1024,512]{2,1,0:T(8,128)(2,1)}, bf16[4,1024,512]{2,1,0:T(8,128)(2,1)}, bf16[4,512,1024]{2,1,0:T(8,128)(2,1)}) async-done(((bf16[4,1024,512]{2,1,0:T(8,128)(2,1)}, bf16[4,1024,512]{2,1,0:T(8,128)(2,1)}, bf16[4,512,1024]{2,1,0:T(8,128)(2,1)}), (bf16[4,1024,512]{2,1,0:T(8,128)(2,1)}, bf16[4,1024,512]{2,1,0:T(8,128)(2,1)}, ...) | async-done | bytes 12582928 | tf_op jit(solution)/shard_map/psum | solution.py:247
  725.2 6.9 convert_element_type.391
  732.1 4.6 convert_element_type.393
  736.8 4.4 convert_element_type.395
  741.2 11.6 %reduce-scatter.6.cloned.1.call-done = bf16[128,1024]{1,0:T(8,128)(2,1)} async-done(((bf16[512,1024]{1,0:T(8,128)(2,1)}), bf16[128,1024]{1,0:T(8,128)(2,1)}) %reduce-scatter.6.cloned.1.call-update) | async-done | bytes 262160 | tf_op jit(solution)/shard_map/reduce_scatter | solution.py:349
  754.1 41.3 %all-reduce.2 = (f32[1024]{0:T(1024)}, f32[1024]{0:T(1024)}) all-reduce(f32[1024]{0:T(1024)S(1)} %get-tuple-element.861, f32[1024]{0:T(1024)S(1)} %get-tuple-element.859), channel_id=1, replica_groups=mesh['dp'=8,'mp'=4] {'dp','mp'}, use_global_device_ids=true, to_apply=%region_77.78 | all-reduce | flops 2048 | bytes 16384 | tf_op jit(solution)/shard_map/psum | solution.py:377
  795.4 2.2 fusion.294
  797.6 35.0 %reduce-scatter.8.cloned.1.call-done = f32[128,768]{0,1:T(8,128)} async-done(((f32[1024,768]{0,1:T(8,128)}), f32[128,768]{0,1:T(8,128)}) %reduce-scatter.8.cloned.1.call-update) | async-done | bytes 393232 | tf_op jit(solution)/shard_map/reduce_scatter | solution.py:352
  (368 shorter events, 91.3 us)
Async XLA Ops:
  7.2 131.6 %all-gather.3.cloned.1.call-start = ((), (), s32[]{:S(2)}) async-start(), calls=%async_computation.7 | async-start | bytes 1310720 | tf_op jit(solution)/shard_map/all_gather | solution.py:87
  10.1 242.6 %reduce-scatter.4.cloned.1.call-start = ((), (), s32[]{:S(2)}) async-start(), calls=%async_computation.8 | async-start | bytes 1310720 | tf_op jit(solution)/shard_map/reduce_scatter | solution.py:176
  43.1 124.5 %copy-start.24 = (bf16[1024,128]{1,0:T(8,128)(2,1)}, bf16[1024,128]{1,0:T(8,128)(2,1)S(1)}, u32[]{:S(2)}) copy-start(bf16[1024,128]{1,0:T(8,128)(2,1)S(1)} %all_gather.23) | copy-start | bytes 786436
  74.2 93.4 %copy-start.22 = (bf16[1024,128]{1,0:T(8,128)(2,1)}, bf16[1024,128]{1,0:T(8,128)(2,1)S(1)}, u32[]{:S(2)}) copy-start(bf16[1024,128]{1,0:T(8,128)(2,1)S(1)} %all_gather.25) | copy-start | bytes 786436
  75.1 92.5 %copy-start.26 = (f32[512,32]{0,1:T(8,128)}, f32[512,32]{0,1:T(8,128)S(1)}, u32[]{:S(2)}) copy-start(f32[512,32]{0,1:T(8,128)S(1)} %get-tuple-element.916) | copy-start | bytes 196612
  106.9 60.7 %copy-start.13 = (bf16[1024,256]{1,0:T(8,128)(2,1)}, bf16[1024,256]{1,0:T(8,128)(2,1)S(1)}, u32[]{:S(2)}) copy-start(bf16[1024,256]{1,0:T(8,128)(2,1)S(1)} %all_gather.24) | copy-start | bytes 1572868
  138.8 77.9 %copy-start.9 = (bf16[1024,256]{1,0:T(8,128)(2,1)}, bf16[1024,256]{1,0:T(8,128)(2,1)S(1)}, u32[]{:S(2)}) copy-start(bf16[1024,256]{1,0:T(8,128)(2,1)S(1)} %all_gather.26) | copy-start | bytes 1572868
  140.8 72.0 %copy-start.32 = (bf16[512,2,64]{0,2,1:T(8,128)(2,1)}, bf16[512,2,64]{0,2,1:T(8,128)(2,1)S(1)}, u32[]{:S(2)}) copy-start(bf16[512,2,64]{0,2,1:T(8,128)(2,1)S(1)} %pad_maximum_fusion.3) | copy-start | bytes 393220
  140.8 14.6 %collective-permute-start = (bf16[512,2,64]{0,2,1:T(8,128)(2,1)S(1)}, bf16[512,2,64]{0,2,1:T(8,128)(2,1)S(1)}, u32[]{:S(2)}, u32[]{:S(2)}) collective-permute-start(bf16[512,2,64]{0,2,1:T(8,128)(2,1)S(1)} %pad_maximum_fusion.3), channel_id=1, source_target_pairs={{0,28},{1,29},{2,30},{3,31}} | collective-permute-start | bytes 393224 | tf_op jit(solution)/shard_map/ppermute | solution.py:20
  146.8 9.9 %collective-permute-start.1 = (bf16[512,2,64]{0,2,1:T(8,128)(2,1)S(1)}, bf16[512,2,64]{0,2,1:T(8,128)(2,1)S(1)}, u32[]{:S(2)}, u32[]{:S(2)}) collective-permute-start(bf16[512,2,64]{0,2,1:T(8,128)(2,1)S(1)} %pad_maximum_fusion.3), channel_id=1, source_target_pairs={{0,24},{4,28},{1,25},{5,29},{2,26},{6,30},{3,27},{7,31}} | collective-permute-start | bytes 393224 | tf_op jit(solution)/shard_map/ppermute | solution.py:20
  148.1 11.8 %collective-permute-start.2 = (bf16[512,2,64]{0,2,1:T(8,128)(2,1)S(1)}, bf16[512,2,64]{0,2,1:T(8,128)(2,1)S(1)}, u32[]{:S(2)}, u32[]{:S(2)}) collective-permute-start(bf16[512,2,64]{0,2,1:T(8,128)(2,1)S(1)} %pad_maximum_fusion.3), channel_id=1, source_target_pairs={{0,20},{4,24},{8,28},{1,21},{5,25},{9,29},{2,22},{6,26},{10,30},{3... | collective-permute-start | bytes 393224 | tf_op jit(solution)/shard_map/ppermute | solution.py:20
  149.4 16.1 %collective-permute-start.3 = (bf16[512,2,64]{0,2,1:T(8,128)(2,1)S(1)}, bf16[512,2,64]{0,2,1:T(8,128)(2,1)S(1)}, u32[]{:S(2)}, u32[]{:S(2)}) collective-permute-start(bf16[512,2,64]{0,2,1:T(8,128)(2,1)S(1)} %pad_maximum_fusion.3), channel_id=1, source_target_pairs={{0,16},{4,20},{8,24},{12,28},{1,17},{5,21},{9,25},{13,29},{2,18},{... | collective-permute-start | bytes 393224 | tf_op jit(solution)/shard_map/ppermute | solution.py:20
  150.7 17.5 %collective-permute-start.4 = (bf16[512,2,64]{0,2,1:T(8,128)(2,1)S(1)}, bf16[512,2,64]{0,2,1:T(8,128)(2,1)S(1)}, u32[]{:S(2)}, u32[]{:S(2)}) collective-permute-start(bf16[512,2,64]{0,2,1:T(8,128)(2,1)S(1)} %pad_maximum_fusion.3), channel_id=1, source_target_pairs={{0,12},{4,16},{8,20},{12,24},{16,28},{1,13},{5,17},{9,21},{13,25},... | collective-permute-start | bytes 393224 | tf_op jit(solution)/shard_map/ppermute | solution.py:20
  155.4 57.4 %copy-start.75 = (bf16[512,128]{0,1:T(8,128)(2,1)}, bf16[512,128]{0,1:T(8,128)(2,1)S(1)}, u32[]{:S(2)}) copy-start(bf16[512,128]{0,1:T(8,128)(2,1)S(1)} %convolution_convert_fusion.2) | copy-start | bytes 393220
  155.4 56.2 %copy-start.71 = (bf16[512,2,64]{0,2,1:T(8,128)(2,1)}, bf16[512,2,64]{0,2,1:T(8,128)(2,1)S(1)}, u32[]{:S(2)}) copy-start(bf16[512,2,64]{0,2,1:T(8,128)(2,1)S(1)} %collective-permute-done) | copy-start | bytes 393220
  155.4 18.8 %collective-permute-start.5 = (bf16[512,2,64]{0,2,1:T(8,128)(2,1)S(1)}, bf16[512,2,64]{0,2,1:T(8,128)(2,1)S(1)}, u32[]{:S(2)}, u32[]{:S(2)}) collective-permute-start(bf16[512,2,64]{0,2,1:T(8,128)(2,1)S(1)} %pad_maximum_fusion.3), channel_id=1, source_target_pairs={{0,8},{4,12},{8,16},{12,20},{16,24},{20,28},{1,9},{5,13},{9,17},{1... | collective-permute-start | bytes 393224 | tf_op jit(solution)/shard_map/ppermute | solution.py:20
  156.7 55.0 %copy-start.69 = (bf16[512,2,64]{0,2,1:T(8,128)(2,1)}, bf16[512,2,64]{0,2,1:T(8,128)(2,1)S(1)}, u32[]{:S(2)}) copy-start(bf16[512,2,64]{0,2,1:T(8,128)(2,1)S(1)} %collective-permute-done.1) | copy-start | bytes 393220
  156.8 19.5 %collective-permute-start.6 = (bf16[512,2,64]{0,2,1:T(8,128)(2,1)S(1)}, bf16[512,2,64]{0,2,1:T(8,128)(2,1)S(1)}, u32[]{:S(2)}, u32[]{:S(2)}) collective-permute-start(bf16[512,2,64]{0,2,1:T(8,128)(2,1)S(1)} %pad_maximum_fusion.3), channel_id=1, source_target_pairs={{0,4},{4,8},{8,12},{12,16},{16,20},{20,24},{24,28},{1,5},{5,9},{9,... | collective-permute-start | bytes 393224 | tf_op jit(solution)/shard_map/ppermute | solution.py:20
  159.9 51.9 %copy-start.67 = (bf16[512,2,64]{0,2,1:T(8,128)(2,1)}, bf16[512,2,64]{0,2,1:T(8,128)(2,1)S(1)}, u32[]{:S(2)}) copy-start(bf16[512,2,64]{0,2,1:T(8,128)(2,1)S(1)} %collective-permute-done.2) | copy-start | bytes 393220
  159.9 41.9 %collective-permute-start.7 = (bf16[512,2,64]{0,2,1:T(8,128)(2,1)S(1)}, bf16[512,2,64]{0,2,1:T(8,128)(2,1)}, u32[]{:S(2)}, u32[]{:S(2)}) collective-permute-start(bf16[512,2,64]{0,2,1:T(8,128)(2,1)S(1)} %bitcast.908), channel_id=1, source_target_pairs={{0,28},{1,29},{2,30},{3,31}} | collective-permute-start | bytes 393224 | tf_op jit(solution)/shard_map/ppermute | solution.py:20
  165.5 46.7 %copy-start.65 = (bf16[512,2,64]{0,2,1:T(8,128)(2,1)}, bf16[512,2,64]{0,2,1:T(8,128)(2,1)S(1)}, u32[]{:S(2)}) copy-start(bf16[512,2,64]{0,2,1:T(8,128)(2,1)S(1)} %collective-permute-done.3) | copy-start | bytes 393220
  165.5 39.1 %collective-permute-start.8 = (bf16[512,2,64]{0,2,1:T(8,128)(2,1)S(1)}, bf16[512,2,64]{0,2,1:T(8,128)(2,1)}, u32[]{:S(2)}, u32[]{:S(2)}) collective-permute-start(bf16[512,2,64]{0,2,1:T(8,128)(2,1)S(1)} %bitcast.909), channel_id=1, source_target_pairs={{0,24},{4,28},{1,25},{5,29},{2,26},{6,30},{3,27},{7,31}} | collective-permute-start | bytes 393224 | tf_op jit(solution)/shard_map/ppermute | solution.py:20
  168.2 44.0 %copy-start.63 = (bf16[512,2,64]{0,2,1:T(8,128)(2,1)}, bf16[512,2,64]{0,2,1:T(8,128)(2,1)S(1)}, u32[]{:S(2)}) copy-start(bf16[512,2,64]{0,2,1:T(8,128)(2,1)S(1)} %collective-permute-done.4) | copy-start | bytes 393220
  168.2 43.5 %collective-permute-start.9 = (bf16[512,2,64]{0,2,1:T(8,128)(2,1)S(1)}, bf16[512,2,64]{0,2,1:T(8,128)(2,1)}, u32[]{:S(2)}, u32[]{:S(2)}) collective-permute-start(bf16[512,2,64]{0,2,1:T(8,128)(2,1)S(1)} %bitcast.910), channel_id=1, source_target_pairs={{0,20},{4,24},{8,28},{1,21},{5,25},{9,29},{2,22},{6,26},{10,30},{3... | collective-permute-start | bytes 393224 | tf_op jit(solution)/shard_map/ppermute | solution.py:20
  174.3 38.0 %copy-start.61 = (bf16[512,2,64]{0,2,1:T(8,128)(2,1)}, bf16[512,2,64]{0,2,1:T(8,128)(2,1)S(1)}, u32[]{:S(2)}) copy-start(bf16[512,2,64]{0,2,1:T(8,128)(2,1)S(1)} %collective-permute-done.5) | copy-start | bytes 393220
  174.3 37.9 %collective-permute-start.10 = (bf16[512,2,64]{0,2,1:T(8,128)(2,1)S(1)}, bf16[512,2,64]{0,2,1:T(8,128)(2,1)}, u32[]{:S(2)}, u32[]{:S(2)}) collective-permute-start(bf16[512,2,64]{0,2,1:T(8,128)(2,1)S(1)} %bitcast.911), channel_id=1, source_target_pairs={{0,16},{4,20},{8,24},{12,28},{1,17},{5,21},{9,25},{13,29},{2,18},{... | collective-permute-start | bytes 393224 | tf_op jit(solution)/shard_map/ppermute | solution.py:20
  176.2 36.5 %copy-start.59 = (bf16[512,2,64]{0,2,1:T(8,128)(2,1)}, bf16[512,2,64]{0,2,1:T(8,128)(2,1)S(1)}, u32[]{:S(2)}) copy-start(bf16[512,2,64]{0,2,1:T(8,128)(2,1)S(1)} %collective-permute-done.6) | copy-start | bytes 393220
  176.2 36.0 %collective-permute-start.11 = (bf16[512,2,64]{0,2,1:T(8,128)(2,1)S(1)}, bf16[512,2,64]{0,2,1:T(8,128)(2,1)}, u32[]{:S(2)}, u32[]{:S(2)}) collective-permute-start(bf16[512,2,64]{0,2,1:T(8,128)(2,1)S(1)} %bitcast.912), channel_id=1, source_target_pairs={{0,12},{4,16},{8,20},{12,24},{16,28},{1,13},{5,17},{9,21},{13,25},... | collective-permute-start | bytes 393224 | tf_op jit(solution)/shard_map/ppermute | solution.py:20
  201.8 10.5 %collective-permute-start.12 = (bf16[512,2,64]{0,2,1:T(8,128)(2,1)S(1)}, bf16[512,2,64]{0,2,1:T(8,128)(2,1)}, u32[]{:S(2)}, u32[]{:S(2)}) collective-permute-start(bf16[512,2,64]{0,2,1:T(8,128)(2,1)S(1)} %bitcast.913), channel_id=1, source_target_pairs={{0,8},{4,12},{8,16},{12,20},{16,24},{20,28},{1,9},{5,13},{9,17},{1... | collective-permute-start | bytes 393224 | tf_op jit(solution)/shard_map/ppermute | solution.py:20
  204.7 8.1 collective-permute-start.13
  219.5 33.2 %copy-start.4 = (bf16[128,1024]{1,0:T(8,128)(2,1)S(1)}, bf16[128,1024]{1,0:T(8,128)(2,1)}, u32[]{:S(2)}) copy-start(bf16[128,1024]{1,0:T(8,128)(2,1)} %param.61) | copy-start | bytes 786436
  219.5 34.3 %copy-start.77 = (f32[1024]{0:T(1024)S(1)}, f32[1024]{0:T(1024)}, u32[]{:S(2)}) copy-start(f32[1024]{0:T(1024)} %param.67) | copy-start | bytes 12292
  253.8 230.1 %copy-start.81 = (f32[128]{0:T(128)}, f32[128]{0:T(128)S(1)}, u32[]{:S(2)}) copy-start(f32[128]{0:T(128)S(1)} %add_rsqrt_fusion) | copy-start | bytes 1540
  260.0 65.0 %all-to-all-start = ((bf16[8,4,40,1024]{3,2,1,0:T(8,128)(2,1)}), bf16[8,4,40,1024]{3,2,1,0:T(8,128)(2,1)S(1)}, u32[]{:S(2)}, u32[]{:S(2)}) async-start(bf16[8,4,40,1024]{3,2,1,0:T(8,128)(2,1)} %bitcast.893), calls=%async_computation.1 | async-start | bytes 5242880 | tf_op jit(solution)/shard_map/all_to_all | solution.py:55
  325.0 63.6 %all-to-all-start.2 = ((bf16[8,4,40,1024]{3,2,1,0:T(8,128)(2,1)}), bf16[8,4,40,1024]{3,2,1,0:T(8,128)(2,1)}, u32[]{:S(2)}, u32[]{:S(2)}) async-start(bf16[8,4,40,1024]{3,2,1,0:T(8,128)(2,1)} %fusion.254), calls=%async_computation.3 | async-start | bytes 5242880 | tf_op jit(solution)/shard_map/all_to_all | solution.py:55
  403.3 63.4 %all-to-all-start.3 = ((bf16[8,4,40,1024]{3,2,1,0:T(8,128)(2,1)}), bf16[8,4,40,1024]{3,2,1,0:T(8,128)(2,1)}, u32[]{:S(2)}, u32[]{:S(2)}) async-start(bf16[8,4,40,1024]{3,2,1,0:T(8,128)(2,1)} %copy.282), calls=%async_computation.4 | async-start | bytes 5242880 | tf_op jit(solution)/shard_map/all_to_all | solution.py:251
  407.8 92.6 %all-gather.5.cloned.1.call-start = ((), (), s32[]{:S(2)}) async-start(), calls=%async_computation.9 | async-start | bytes 1310720 | tf_op jit(solution)/shard_map/all_gather | solution.py:261
  485.4 239.8 %all-reduce.6.cloned.1.call-start = ((), (), s32[]{:S(2)}) async-start(), calls=%async_computation.12 | async-start | bytes 25165824 | tf_op jit(solution)/shard_map/psum | solution.py:247
  497.5 255.4 %reduce-scatter.6.cloned.1.call-start = ((), (), s32[]{:S(2)}) async-start(), calls=%async_computation.10 | async-start | bytes 1310720 | tf_op jit(solution)/shard_map/reduce_scatter | solution.py:349
  527.8 57.9 %copy-start.49 = (f32[512,2,64]{0,2,1:T(8,128)S(1)}, f32[512,2,64]{0,2,1:T(8,128)}, u32[]{:S(2)}) copy-start(f32[512,2,64]{0,2,1:T(8,128)} %copy-done.48) | copy-start | bytes 786436
  527.8 58.0 %copy-start.53 = (f32[512,2,64]{0,2,1:T(8,128)S(1)}, f32[512,2,64]{0,2,1:T(8,128)}, u32[]{:S(2)}) copy-start(f32[512,2,64]{0,2,1:T(8,128)} %copy-done.52) | copy-start | bytes 786436
  528.9 54.2 %collective-permute-start.27 = (bf16[512,2,64]{0,2,1:T(8,128)(2,1)S(1)}, bf16[512,2,64]{0,2,1:T(8,128)(2,1)S(1)}, u32[]{:S(2)}, u32[]{:S(2)}) collective-permute-start(bf16[512,2,64]{0,2,1:T(8,128)(2,1)S(1)} %convert_element_type.385), channel_id=1, source_target_pairs={{28,0},{29,1},{30,2},{31,3}} | collective-permute-start | bytes 393224 | tf_op jit(solution)/shard_map/ppermute | solution.py:20
  531.2 53.2 %collective-permute-start.26 = (bf16[512,2,64]{0,2,1:T(8,128)(2,1)S(1)}, bf16[512,2,64]{0,2,1:T(8,128)(2,1)S(1)}, u32[]{:S(2)}, u32[]{:S(2)}) collective-permute-start(bf16[512,2,64]{0,2,1:T(8,128)(2,1)S(1)} %convert_element_type.383), channel_id=1, source_target_pairs={{24,0},{28,4},{25,1},{29,5},{26,2},{30,6},{27,3},{31,7}} | collective-permute-start | bytes 393224 | tf_op jit(solution)/shard_map/ppermute | solution.py:20
  533.4 52.4 %collective-permute-start.25 = (bf16[512,2,64]{0,2,1:T(8,128)(2,1)S(1)}, bf16[512,2,64]{0,2,1:T(8,128)(2,1)S(1)}, u32[]{:S(2)}, u32[]{:S(2)}) collective-permute-start(bf16[512,2,64]{0,2,1:T(8,128)(2,1)S(1)} %convert_element_type.381), channel_id=1, source_target_pairs={{20,0},{24,4},{28,8},{21,1},{25,5},{29,9},{22,2},{26,6},{30,10},{2... | collective-permute-start | bytes 393224 | tf_op jit(solution)/shard_map/ppermute | solution.py:20
  535.7 50.1 %collective-permute-start.24 = (bf16[512,2,64]{0,2,1:T(8,128)(2,1)S(1)}, bf16[512,2,64]{0,2,1:T(8,128)(2,1)S(1)}, u32[]{:S(2)}, u32[]{:S(2)}) collective-permute-start(bf16[512,2,64]{0,2,1:T(8,128)(2,1)S(1)} %convert_element_type.379), channel_id=1, source_target_pairs={{16,0},{20,4},{24,8},{28,12},{17,1},{21,5},{25,9},{29,13},{18,2},{... | collective-permute-start | bytes 393224 | tf_op jit(solution)/shard_map/ppermute | solution.py:20
  538.0 47.8 %collective-permute-start.23 = (bf16[512,2,64]{0,2,1:T(8,128)(2,1)S(1)}, bf16[512,2,64]{0,2,1:T(8,128)(2,1)S(1)}, u32[]{:S(2)}, u32[]{:S(2)}) collective-permute-start(bf16[512,2,64]{0,2,1:T(8,128)(2,1)S(1)} %convert_element_type.377), channel_id=1, source_target_pairs={{12,0},{16,4},{20,8},{24,12},{28,16},{13,1},{17,5},{21,9},{25,13},... | collective-permute-start | bytes 393224 | tf_op jit(solution)/shard_map/ppermute | solution.py:20
  583.1 7.0 collective-permute-start.22
  584.4 7.0 collective-permute-start.21
  591.9 24.1 %copy-start.25 = (bf16[1024,128]{1,0:T(8,128)(2,1)S(1)}, bf16[1024,128]{1,0:T(8,128)(2,1)}, u32[]{:S(2)}) copy-start(bf16[1024,128]{1,0:T(8,128)(2,1)} %copy-done.24) | copy-start | bytes 786436
  592.0 11.6 %collective-permute-start.20 = (bf16[512,2,64]{0,2,1:T(8,128)(2,1)S(1)}, bf16[512,2,64]{0,2,1:T(8,128)(2,1)S(1)}, u32[]{:S(2)}, u32[]{:S(2)}) collective-permute-start(bf16[512,2,64]{0,2,1:T(8,128)(2,1)S(1)} %get-tuple-element.892), channel_id=1, source_target_pairs={{28,0},{29,1},{30,2},{31,3}} | collective-permute-start | bytes 393224 | tf_op jit(solution)/shard_map/ppermute | solution.py:20
  593.3 11.9 %collective-permute-start.19 = (bf16[512,2,64]{0,2,1:T(8,128)(2,1)S(1)}, bf16[512,2,64]{0,2,1:T(8,128)(2,1)S(1)}, u32[]{:S(2)}, u32[]{:S(2)}) collective-permute-start(bf16[512,2,64]{0,2,1:T(8,128)(2,1)S(1)} %get-tuple-element.893), channel_id=1, source_target_pairs={{24,0},{28,4},{25,1},{29,5},{26,2},{30,6},{27,3},{31,7}} | collective-permute-start | bytes 393224 | tf_op jit(solution)/shard_map/ppermute | solution.py:20
  594.7 21.8 %copy-start.23 = (bf16[1024,128]{1,0:T(8,128)(2,1)S(1)}, bf16[1024,128]{1,0:T(8,128)(2,1)}, u32[]{:S(2)}) copy-start(bf16[1024,128]{1,0:T(8,128)(2,1)} %copy-done.22) | copy-start | bytes 786436
  594.7 19.1 %collective-permute-start.18 = (bf16[512,2,64]{0,2,1:T(8,128)(2,1)S(1)}, bf16[512,2,64]{0,2,1:T(8,128)(2,1)S(1)}, u32[]{:S(2)}, u32[]{:S(2)}) collective-permute-start(bf16[512,2,64]{0,2,1:T(8,128)(2,1)S(1)} %get-tuple-element.894), channel_id=1, source_target_pairs={{20,0},{24,4},{28,8},{21,1},{25,5},{29,9},{22,2},{26,6},{30,10},{2... | collective-permute-start | bytes 393224 | tf_op jit(solution)/shard_map/ppermute | solution.py:20
  596.1 19.6 %collective-permute-start.17 = (bf16[512,2,64]{0,2,1:T(8,128)(2,1)S(1)}, bf16[512,2,64]{0,2,1:T(8,128)(2,1)S(1)}, u32[]{:S(2)}, u32[]{:S(2)}) collective-permute-start(bf16[512,2,64]{0,2,1:T(8,128)(2,1)S(1)} %get-tuple-element.895), channel_id=1, source_target_pairs={{16,0},{20,4},{24,8},{28,12},{17,1},{21,5},{25,9},{29,13},{18,2},{... | collective-permute-start | bytes 393224 | tf_op jit(solution)/shard_map/ppermute | solution.py:20
  597.4 18.3 %collective-permute-start.16 = (bf16[512,2,64]{0,2,1:T(8,128)(2,1)S(1)}, bf16[512,2,64]{0,2,1:T(8,128)(2,1)S(1)}, u32[]{:S(2)}, u32[]{:S(2)}) collective-permute-start(bf16[512,2,64]{0,2,1:T(8,128)(2,1)S(1)} %get-tuple-element.896), channel_id=1, source_target_pairs={{12,0},{16,4},{20,8},{24,12},{28,16},{13,1},{17,5},{21,9},{25,13},... | collective-permute-start | bytes 393224 | tf_op jit(solution)/shard_map/ppermute | solution.py:20
  603.6 12.2 %collective-permute-start.15 = (bf16[512,2,64]{0,2,1:T(8,128)(2,1)S(1)}, bf16[512,2,64]{0,2,1:T(8,128)(2,1)S(1)}, u32[]{:S(2)}, u32[]{:S(2)}) collective-permute-start(bf16[512,2,64]{0,2,1:T(8,128)(2,1)S(1)} %get-tuple-element.897), channel_id=1, source_target_pairs={{8,0},{12,4},{16,8},{20,12},{24,16},{28,20},{9,1},{13,5},{17,9},{2... | collective-permute-start | bytes 393224 | tf_op jit(solution)/shard_map/ppermute | solution.py:20
  605.1 10.6 %collective-permute-start.14 = (bf16[512,2,64]{0,2,1:T(8,128)(2,1)S(1)}, bf16[512,2,64]{0,2,1:T(8,128)(2,1)S(1)}, u32[]{:S(2)}, u32[]{:S(2)}) collective-permute-start(bf16[512,2,64]{0,2,1:T(8,128)(2,1)S(1)} %get-tuple-element.891), channel_id=1, source_target_pairs={{4,0},{8,4},{12,8},{16,12},{20,16},{24,20},{28,24},{5,1},{9,5},{13... | collective-permute-start | bytes 393224 | tf_op jit(solution)/shard_map/ppermute | solution.py:20
  623.7 68.9 %all-to-all-start.1 = ((bf16[8,4,40,1024]{3,2,1,0:T(8,128)(2,1)}), bf16[8,4,40,1024]{3,2,1,0:T(8,128)(2,1)}, u32[]{:S(2)}, u32[]{:S(2)}) async-start(bf16[8,4,40,1024]{3,2,1,0:T(8,128)(2,1)} %copy.277), calls=%async_computation.2 | async-start | bytes 5242880 | tf_op jit(solution)/shard_map/all_to_all | solution.py:221
  633.7 198.8 %reduce-scatter.8.cloned.1.call-start = ((), (), s32[]{:S(2)}) async-start(), calls=%async_computation.11 | async-start | bytes 3538944 | tf_op jit(solution)/shard_map/reduce_scatter | solution.py:352
  736.7 58.6 %copy-start.7 = (f32[128,1024]{1,0:T(8,128)S(1)}, f32[128,1024]{1,0:T(8,128)}, u32[]{:S(2)}) copy-start(f32[128,1024]{1,0:T(8,128)} %copy-done.6) | copy-start | bytes 1572868
  736.8 58.6 %copy-start.21 = (bf16[128,1024]{1,0:T(8,128)(2,1)S(1)}, bf16[128,1024]{1,0:T(8,128)(2,1)}, u32[]{:S(2)}) copy-start(bf16[128,1024]{1,0:T(8,128)(2,1)} %param.73) | copy-start | bytes 786436
  736.8 58.6 %copy-start.78 = (f32[1024]{0:T(1024)S(1)}, f32[1024]{0:T(1024)}, u32[]{:S(2)}) copy-start(f32[1024]{0:T(1024)} %param.67) | copy-start | bytes 12292
  736.8 58.6 %copy-start.82 = (f32[128]{0:T(128)S(1)}, f32[128]{0:T(128)}, u32[]{:S(2)}) copy-start(f32[128]{0:T(128)} %copy-done.81) | copy-start | bytes 1540
  736.8 58.6 %copy-start.90 = (f32[128]{0:T(128)S(1)}, f32[128]{0:T(128)}, u32[]{:S(2)}) copy-start(f32[128]{0:T(128)} %copy-done.89) | copy-start | bytes 1540
  (57 other events, 285.1 us)
Sparse Core Ops, SparseCore 0:
  10.3 19.4 all-gather.2
  219.1 33.5 reduce-scatter.3
  485.5 14.8 all-gather.4
  503.8 221.3 all-reduce.5
  727.7 25.0 reduce-scatter.5
  756.3 76.2 reduce-scatter.7
where the time goes:
time: 856 us; the launch traced here: 845 us
  waiting for transfers between devices  347 us (41%)
  blocking collectives  169 us (20%)
  starting transfers between devices  106 us (12%)
  local copies, waits for them, and re-layouts  70.6 us (8%)
  matrix products  63.3 us (7%)
  other arithmetic  58.7 us (7%)
  between operations  16.2 us (2%)
  loops' own time  13.7 us (2%)
    all_to_all x2, waiting for transfers between devices, send_slots(): lax.all_to_all(payload, 'dp', split_axis=0, concat_axis=0, tiled=True)  92.4 us
    ppermute x28, starting transfers between devices, passed_along(): lax.ppermute(value, axis, [(source, source + steps) for source in range(f...  81.1 us
    ppermute x28, waiting for transfers between devices, passed_along(): lax.ppermute(value, axis, [(source, source + steps) for source in range(f...  60.4 us
    all_to_all x1, waiting for transfers between devices, shards(): lax.all_to_all(produced, 'dp', split_axis=0, concat_axis=0, tiled=True)  55.3 us
    all_to_all x1, waiting for transfers between devices, shards(): lax.all_to_all(slot_input_grad, 'dp', split_axis=0, concat_axis=0, tiled=...  52.7 us
    psum x1, blocking collectives, shards(): lax.psum((first_gain_part, second_gain_part), ('dp', 'mp'))  41.3 us
    reduce_scatter x1, waiting for transfers between devices, shards(): lax.psum_scatter(jnp.concatenate([contract(sequence_rows, query_plain_gra...  35 us
    all_gather x1, blocking collectives, shards(): lax.all_gather(key_matrix, 'dp', axis=0, tiled=True)  32.8 us
  transfers between devices with their start and end apart: 38, of which 17 were waited for; matrix products, arithmetic and copies ran while one was open for 16% of the time, Pallas kernels for 0%

commit v1 on v0

--- a/solution.py
+++ b/solution.py
@@ -1,6 +1,8 @@
 import jax
 import jax.numpy as jnp
 from jax import lax
+from jax.experimental import pallas as pl
+from jax.experimental.pallas import tpu as pltpu
 from jax.sharding import PartitionSpec as P
 
 HEAD_SIZE = 64
@@ -12,6 +14,8 @@
 epsilon = 1e-06
 theta = 10000.0
 masked = -1e30
+vmem_bytes = 56 * 2**20
+vmem_small = 20 * 2**20
 
 
 def passed_along(value, axis, steps):
@@ -390,6 +394,1054 @@
     )
 
 
+def xor_gather(value, axis):
+    count = lax.axis_size(axis)
+    chunks = [value] + [None] * (count - 1)
+    order = sorted(range(1, count), key=lambda r: (bin(r).count("1"), -(r & -r)))
+    for r in order:
+        low = r & -r
+        chunks[r] = lax.ppermute(chunks[r ^ low], axis, [(i, i ^ low) for i in range(count)])
+    return chunks
+
+
+def xor_scatter(chunks, axis):
+    count = lax.axis_size(axis)
+    pending = [[chunk] for chunk in chunks]
+    order = sorted(range(1, count), key=lambda r: (-bin(r).count("1"), r & -r))
+    for r in order:
+        low = r & -r
+        total = add_parts(pending[r])
+        pending[r ^ low].append(
+            lax.ppermute(total, axis, [(i, i ^ low) for i in range(count)])
+        )
+    return pending[0]
+
+
+def add_parts(parts):
+    if len(parts) == 1:
+        return parts[0]
+    return sum_parts(parts).astype(parts[0].dtype)
+
+
+def sum_parts(parts):
+    total = parts[0].astype(jnp.float32)
+    for part in parts[1:]:
+        total = total + part.astype(jnp.float32)
+    return total
+
+
+def butterfly_sum(value, axis):
+    count = lax.axis_size(axis)
+    bit = 1
+    while bit < count:
+        value = value + lax.ppermute(value, axis, [(i, i ^ bit) for i in range(count)])
+        bit *= 2
+    return value
+
+
+def dot_nn(left, right):
+    return lax.dot_general(
+        left, right, (((1,), (0,)), ((), ())), preferred_element_type=jnp.float32
+    )
+
+
+def dot_nt(left, right):
+    return lax.dot_general(
+        left, right, (((1,), (1,)), ((), ())), preferred_element_type=jnp.float32
+    )
+
+
+def dot_tn(left, right):
+    return lax.dot_general(
+        left, right, (((0,), (0,)), ((), ())), preferred_element_type=jnp.float32
+    )
+
+
+def low(value):
+    return value.astype(jnp.bfloat16)
+
+
+def wide(value):
+    return value.astype(jnp.float32)
+
+
+def call(body, outs, operands, scalars, flops, scratch=(), grid=None, in_specs=None,
+         out_specs=None, transcendentals=0, aliases=None):
+    memory = vmem_small if grid is None else vmem_bytes
+    size = sum(x.size * x.dtype.itemsize for x in operands)
+    size += sum(x.size * x.dtype.itemsize for x in outs)
+    if grid is None:
+        in_specs = [pl.BlockSpec(memory_space=pltpu.SMEM)] * len(scalars)
+        in_specs += [pl.BlockSpec(memory_space=pltpu.VMEM)] * len(operands)
+        layout = {
+            "in_specs": in_specs,
+            "out_specs": [pl.BlockSpec(memory_space=pltpu.VMEM)] * len(outs),
+            "scratch_shapes": list(scratch),
+        }
+    else:
+        layout = {
+            "grid_spec": pltpu.PrefetchScalarGridSpec(
+                num_scalar_prefetch=len(scalars),
+                grid=grid,
+                in_specs=in_specs,
+                out_specs=out_specs,
+                scratch_shapes=list(scratch),
+            )
+        }
+    return pl.pallas_call(
+        body,
+        out_shape=list(outs),
+        input_output_aliases=aliases or {},
+        compiler_params=pltpu.CompilerParams(vmem_limit_bytes=memory),
+        cost_estimate=pl.CostEstimate(
+            flops=int(flops // 256), bytes_accessed=int(size // 256), transcendentals=0
+        ),
+        **layout,
+    )(*scalars, *operands)
+
+
+def shape(dims, dtype):
+    return jax.ShapeDtypeStruct(tuple(dims), dtype)
+
+
+def column(index, me, width):
+    return pl.ds(pl.multiple_of((index ^ me) * width, width), width)
+
+
+def first_norm_rows(layer_input, gain, me, count):
+    rows, width = layer_input.shape
+    chunk = width // count
+
+    def body(me_ref, x_ref, gain_ref, out_ref):
+        x = wide(x_ref[...])
+        scale = lax.rsqrt(jnp.mean(x * x, axis=-1, keepdims=True) + epsilon)
+        normed = low(x * scale * gain_ref[...])
+        for r in range(count):
+            out_ref[:, column(r, me_ref[0], chunk)] = normed[:, r * chunk : (r + 1) * chunk]
+
+    return call(
+        body, [shape((rows, width), jnp.bfloat16)], [layer_input, gain], [me], 4 * rows * width
+    )[0]
+
+
+def rope_rows(block, cosine, sine):
+    half = HEAD_SIZE // 2
+    first, second = block[:half], block[half:]
+    return jnp.concatenate(
+        [first * cosine - second * sine, second * cosine + first * sine], axis=0
+    )
+
+
+def padded_heads(blocks, group):
+    heads = len(blocks)
+    kv = heads // group
+    empty = jnp.zeros_like(blocks[0])
+    columns = []
+    for head, block in enumerate(blocks):
+        parts = [block if k == head // group else empty for k in range(kv)]
+        columns.append(jnp.concatenate(parts, axis=0))
+    return jnp.concatenate(columns, axis=1)
+
+
+def project(x_chunks, w_chunks, cosine, sine, local_q, local_kv):
+    w_chunks, w_cols = w_chunks
+    tokens = sum(x.shape[0] for x in x_chunks)
+    width = x_chunks[0].shape[1]
+    cols = w_cols.stop - w_cols.start
+    kv_rows = local_kv * HEAD_SIZE
+    group = local_q // local_kv
+    nx, nw = len(x_chunks), len(w_chunks)
+
+    def body(*refs):
+        x_refs, w_refs = refs[:nx], refs[nx : nx + nw]
+        cos_ref, sin_ref, q_ref, kv_ref = refs[nx + nw :]
+        weight = jnp.concatenate([w[:, w_cols] for w in w_refs], axis=0)
+        rows = jnp.concatenate([x[...] for x in x_refs], axis=0)
+        plain = dot_nn(rows, weight).T
+        cosine, sine = cos_ref[...], sin_ref[...]
+        blocks = [
+            low(rope_rows(plain[h * HEAD_SIZE : (h + 1) * HEAD_SIZE], cosine, sine))
+            for h in range(local_q + local_kv)
+        ]
+        scale = jnp.bfloat16(HEAD_SIZE ** (-0.5))
+        q_ref[...] = padded_heads([b * scale for b in blocks[:local_q]], group)
+        for h in range(local_kv):
+            kv_ref[h * HEAD_SIZE : (h + 1) * HEAD_SIZE, :] = blocks[local_q + h]
+        kv_ref[kv_rows:, :] = low(plain[local_q * HEAD_SIZE + kv_rows :])
+
+    return call(
+        body,
+        [
+            shape((kv_rows, local_q * tokens), jnp.bfloat16),
+            shape((2 * kv_rows, tokens), jnp.bfloat16),
+        ],
+        [*x_chunks, *w_chunks, cosine, sine],
+        [],
+        2 * tokens * width * cols,
+    )
+
+
+def attention_part(offset, state, queries, kv_chunks, numbers, key_pos, query_pos, local_q):
+    kv_rows, all_rows = queries.shape
+    tokens = all_rows // local_q
+    n = len(kv_chunks)
+    first = state is None
+
+    def body(off_ref, *refs):
+        if not first:
+            before_ref, refs = refs[0], refs[1:]
+        q_ref, kv_refs = refs[0], refs[1 : 1 + n]
+        kpos_ref, qpos_ref, state_ref = refs[1 + n :]
+        off = off_ref[0]
+        if not first:
+            state_ref[...] = before_ref[...]
+        top_at, total_at = slice(kv_rows, kv_rows + 1), slice(kv_rows + 1, kv_rows + 2)
+        for index, r in enumerate(numbers):
+
+            def block(index=index, r=r):
+                keys = kv_refs[index][:kv_rows, :].T
+                values = kv_refs[index][kv_rows:, :]
+
+                def head(h, _):
+                    cols = pl.ds(pl.multiple_of(h * tokens, tokens), tokens)
+                    scores = dot_nn(keys, q_ref[:, cols])
+                    if r == 0:
+                        scores = jnp.where(kpos_ref[...] <= qpos_ref[...], scores, masked)
+                        top = jnp.max(scores, axis=0, keepdims=True)
+                        probs = jnp.exp(scores - top)
+                        state_ref[total_at, cols] = jnp.sum(probs, axis=0, keepdims=True)
+                        state_ref[:kv_rows, cols] = dot_nn(values, low(probs))
+                    else:
+                        before = state_ref[top_at, cols]
+                        top = jnp.maximum(before, jnp.max(scores, axis=0, keepdims=True))
+                        probs = jnp.exp(scores - top)
+                        alpha = jnp.exp(before - top)
+                        state_ref[total_at, cols] = state_ref[total_at, cols] * alpha + jnp.sum(
+                            probs, axis=0, keepdims=True
+                        )
+                        state_ref[:kv_rows, cols] = state_ref[:kv_rows, cols] * alpha + dot_nn(
+                            values, low(probs)
+                        )
+                    state_ref[top_at, cols] = top
+                    return 0
+
+                lax.fori_loop(0, local_q, head, 0)
+
+            if r == 0:
+                block()
+            else:
+                pl.when((r ^ off) < off)(block)
+
+    operands = [queries, *kv_chunks, key_pos, query_pos]
+    return call(
+        body,
+        [shape((kv_rows + 8, all_rows), jnp.float32)],
+        operands if first else [state, *operands],
+        [offset],
+        4 * all_rows * tokens * n * kv_rows,
+        transcendentals=all_rows * tokens * n,
+        aliases=None if first else {1: 0},
+    )
+
+
+def attention_end(state, out_chunks, local_q, kv_rows, pieces):
+    out_chunks, w_cols = out_chunks
+    all_rows = state.shape[1]
+    tokens = all_rows // local_q
+    group = local_q // (kv_rows // HEAD_SIZE)
+    nw = len(out_chunks)
+    width = nw * out_chunks[0].shape[0]
+
+    def body(state_ref, *refs):
+        w_refs = refs[:nw]
+        att_ref, lse_ref = refs[nw : nw + 2]
+        branch_refs = refs[nw + 2 :]
+        total = state_ref[kv_rows + 1 : kv_rows + 2, :]
+        lse_ref[...] = state_ref[kv_rows : kv_rows + 1, :] + jnp.log(total)
+        for h in range(local_q):
+            rows = slice((h // group) * HEAD_SIZE, (h // group + 1) * HEAD_SIZE)
+            cols = slice(h * tokens, (h + 1) * tokens)
+            att_ref[h * HEAD_SIZE : (h + 1) * HEAD_SIZE, :] = state_ref[rows, cols] / total[:, cols]
+        attended = low(att_ref[...].T)
+        weight = jnp.concatenate([w[:, w_cols] for w in w_refs], axis=0)
+        part = tokens // pieces
+        for m in range(pieces):
+            branch_refs[m][...] = low(dot_nt(attended[m * part : (m + 1) * part], weight))
+
+    f32 = jnp.float32
+    outs = [shape((local_q * HEAD_SIZE, tokens), f32), shape((1, all_rows), f32)]
+    outs += [shape((tokens // pieces, width), jnp.bfloat16)] * pieces
+    return call(
+        body, outs, [state, *out_chunks], [], 2 * tokens * width * local_q * HEAD_SIZE
+    )
+
+
+def middle_rows(me, layer_input, branch_parts, gain, count):
+    rows, width = layer_input.shape
+    chunk = width // count
+    n = len(branch_parts)
+
+    def body(me_ref, x_ref, gain_ref, *refs):
+        branch = sum_parts([b[...] for b in refs[:n]])
+        middle_ref, norm_ref = refs[n:]
+        for r in range(count):
+            at = column(r, me_ref[0], chunk)
+            middle_ref[:, at] = wide(x_ref[:, at]) + branch[:, r * chunk : (r + 1) * chunk]
+        middle = middle_ref[...]
+        scale = lax.rsqrt(jnp.mean(middle * middle, axis=-1, keepdims=True) + epsilon)
+        norm_ref[...] = low(middle * scale * gain_ref[...])
+
+    return call(
+        body,
+        [shape((rows, width), jnp.float32), shape((rows, width), jnp.bfloat16)],
+        [layer_input, gain, *branch_parts],
+        [me],
+        6 * rows * width,
+    )
+
+
+def routing_tables(chosen, payloads, cols, experts_all, most, pieces):
+    count, rows = len(payloads), payloads[0].shape[0]
+    tokens = cols.stop - cols.start
+
+    def body(chosen_ref, *refs):
+        out_ref, wide_ref = refs[count:]
+        for source in range(count):
+            wide_ref[source * rows : (source + 1) * rows, :] = wide(refs[source][:, cols])
+        for k in range(pieces):
+            for source in range(count):
+                at = slice(source * tokens, (source + 1) * tokens)
+                lines = [
+                    wide_ref[pl.ds(source * rows + kind * experts_all + chosen_ref[k], 1), :]
+                    for kind in range(4)
+                ]
+                place = jnp.where(lines[0] >= 0, lines[0] + source % 2 * most, -1.0)
+                out_ref[k, 0:1, at] = place
+                out_ref[k, 1:2, at] = lines[1] + (lines[2] + lines[3])
+
+    return call(
+        body,
+        [shape((pieces, 2, count * tokens), jnp.float32)],
+        list(payloads),
+        [chosen],
+        count * rows * tokens,
+        scratch=[pltpu.VMEM((count * rows, tokens), jnp.float32)],
+    )[0]
+
+
+def stacked(chunks):
+    count = len(chunks)
+
+    def body(*refs):
+        for k in range(count):
+            refs[count][k] = refs[k][...]
+
+    outs = [shape((count,) + chunks[0].shape, chunks[0].dtype)]
+    return call(body, outs, list(chunks), [], chunks[0].size)[0]
+
+
+def experts(selected, norms, gathered, tables, gate_w, up_w, down_w, most, pieces, whole):
+    rows, width = gathered.shape[1:]
+    count = selected.shape[0] - 1 - pieces
+    half = pieces // 2
+    nn = len(norms)
+    ff = gate_w.shape[2]
+    pair = 2 * rows
+    taken = 2 * most
+    pairs = count // 2
+    slots = count * most
+
+    def body(sel_ref, *refs):
+        n_refs, u_refs = refs[:nn], refs[nn : nn + count]
+        refs = refs[nn + count :]
+        table_ref, g_ref, up_ref, d_ref = refs[:4]
+        rest = refs[4:]
+        keep_ref, send_ref, rest = *rest[:2], rest[2:]
+        if whole:
+            mix_refs, dx_refs = rest[:count], rest[count : 2 * count]
+            xs, gs, ys, ds = rest[2 * count :]
+        else:
+            xs, gs = rest
+        p = pl.program_id(0)
+
+        def chosen(q):
+            at = slice(q * pair, (q + 1) * pair)
+            line = lax.broadcasted_iota(jnp.int32, (taken, pair), 0).astype(jnp.float32)
+            return [line == table_ref[k, 0:1, at] for k in range(pieces)]
+
+        def weighted(q, picks):
+            at = slice(q * pair, (q + 1) * pair)
+            return [jnp.where(c, table_ref[k, 1:2, at], 0.0) for k, c in enumerate(picks)]
+
+        def norm_pair(q):
+            if nn == 1:
+                return n_refs[0][2 * q : 2 * q + 2].reshape(pair, width)
+            return jnp.concatenate([n_refs[2 * q][...], n_refs[2 * q + 1][...]], axis=0)
+
+        @pl.when(p == 0)
+        def _():
+            for q in range(pairs):
+                picks = chosen(q)
+                factor = jnp.sum(
+                    jnp.concatenate(weighted(q, picks), axis=0), axis=1, keepdims=True
+                )
+                pick = jnp.concatenate([low(c.astype(jnp.float32)) for c in picks], axis=0)
+                here = dot_nn(pick, norm_pair(q))
+                grads = dot_nn(
+                    pick,
+                    jnp.concatenate(
+                        [u_refs[2 * q][0], u_refs[2 * q + 1][0]], axis=0
+                    ),
+                )
+                grads = grads * factor
+                for k in range(pieces):
+                    part = slice(k * taken, (k + 1) * taken)
+                    xs[k, q * taken : (q + 1) * taken, :] = low(here[part])
+                    gs[k, q * taken : (q + 1) * taken, :] = low(grads[part])
+
+        x, produced_grad = xs[p], gs[p]
+        gate_weight, up_weight, down_weight = g_ref[0], up_ref[0], d_ref[0]
+        gate = dot_nn(x, gate_weight)
+        upper = dot_nn(x, up_weight)
+        sigmoid = jax.nn.sigmoid(gate)
+        activated = gate * sigmoid
+        hidden = low(activated * upper)
+        hidden_grad = dot_nt(produced_grad, down_weight)
+        gate_low = low(hidden_grad * upper * (sigmoid * (1.0 + gate * (1.0 - sigmoid))))
+        upper_low = low(hidden_grad * activated)
+
+        def store(ref):
+            ref[0, :, :width] = x
+            ref[0, :, width : 2 * width] = produced_grad
+            for k, field in enumerate((hidden, gate_low, upper_low)):
+                ref[0, :, 2 * width + k * ff : 2 * width + (k + 1) * ff] = field
+
+        pl.when(p < half)(lambda: store(keep_ref))
+        pl.when(p >= half)(lambda: store(send_ref))
+        if whole:
+            ys[p] = low(dot_nn(hidden, down_weight))
+            ds[p] = low(dot_nt(gate_low, gate_weight) + dot_nt(upper_low, up_weight))
+
+            @pl.when(p == pieces - 1)
+            def _():
+                for q in range(pairs):
+                    picks = chosen(q)
+                    pick = jnp.concatenate([c.astype(jnp.float32) for c in picks], axis=0)
+                    scaled = jnp.concatenate(weighted(q, picks), axis=0)
+                    at = slice(q * taken, (q + 1) * taken)
+                    outs = jnp.concatenate([ys[k, at, :] for k in range(pieces)], axis=0)
+                    grads = jnp.concatenate([ds[k, at, :] for k in range(pieces)], axis=0)
+                    mixed = low(dot_tn(low(scaled), outs))
+                    back = low(dot_tn(low(pick), grads))
+                    for s in range(2):
+                        part = slice(s * rows, (s + 1) * rows)
+                        mix_refs[2 * q + s][...] = mixed[part]
+                        dx_refs[2 * q + s][...] = back[part]
+
+    def weight_block(a, b):
+        return pl.BlockSpec((1, a, b), lambda p, sel: (sel[count + 1 + p], 0, 0))
+
+    def fixed(dims):
+        return pl.BlockSpec(tuple(dims), lambda p, sel: (0,) * len(dims))
+
+    bf = jnp.bfloat16
+    fields = (slots, 2 * width + 3 * ff)
+    scratch = [pltpu.VMEM((pieces, slots, width), bf)] * 2
+    outs = [shape((half,) + fields, bf)] * 2
+    out_specs = [
+        pl.BlockSpec((1,) + fields, lambda p, sel: (jnp.minimum(p, half - 1), 0, 0)),
+        pl.BlockSpec((1,) + fields, lambda p, sel: (jnp.maximum(p - half, 0), 0, 0)),
+    ]
+    if whole:
+        outs += [shape((rows, width), bf)] * (2 * count)
+        out_specs += [fixed((rows, width))] * (2 * count)
+        scratch += [pltpu.VMEM((pieces, slots, width), bf)] * 2
+    blocks = [
+        pl.BlockSpec((1,) + gathered.shape[1:], lambda p, sel, r=r: (sel[r], 0, 0))
+        for r in range(count)
+    ]
+    return call(
+        body,
+        outs,
+        [*norms, *([gathered] * count), tables, gate_w, up_w, down_w],
+        [selected],
+        pieces * slots * width * ff * 2 * (6 if whole else 3),
+        scratch=scratch,
+        grid=(pieces,),
+        in_specs=[fixed(n.shape) for n in norms]
+        + blocks
+        + [fixed(tables.shape)]
+        + [weight_block(width, ff), weight_block(width, ff), weight_block(ff, width)],
+        out_specs=out_specs,
+    )
+
+
+def expert_weight_grads(places, groups, totals, pieces_dev, ff):
+    n = len(groups)
+    _, slots, cols = groups[0].shape
+    width = (cols - 3 * ff) // 2
+    edges = [0, width, 2 * width, 2 * width + ff, 2 * width + 2 * ff, cols]
+    given = len(totals)
+
+    def body(places_ref, *refs):
+        refs = refs[given:]
+        fields = [
+            jnp.concatenate([r[0, :, edges[f] : edges[f + 1]] for r in refs[:n]], axis=0)
+            for f in range(5)
+        ]
+        wide_refs, low_ref = refs[n : n + 3], refs[n + 3]
+        x, produced_grad, hidden, gate_low, upper_low = fields
+        for k, (left, right) in enumerate(
+            [(x, gate_low), (x, upper_low), (hidden, produced_grad)]
+        ):
+            total = dot_tn(left, right)
+            wide_refs[k][0] = total
+            store_packed(low_ref, k, low(total), ff)
+
+    dims = [(width, ff), (width, ff), (ff, width)]
+    return call(
+        body,
+        [shape((pieces_dev,) + d, jnp.float32) for d in dims]
+        + [shape((1, 3 * width, ff), jnp.bfloat16)],
+        [*totals, *groups],
+        [places],
+        6 * n * slots * width * ff,
+        grid=(1,),
+        in_specs=[pl.BlockSpec(memory_space=pl.ANY)] * given
+        + [pl.BlockSpec((1, slots, cols), lambda p, at: (at[1], 0, 0))] * n,
+        out_specs=[pl.BlockSpec((1,) + d, lambda p, at: (at[0], 0, 0)) for d in dims]
+        + [pl.BlockSpec((1, 3 * width, ff), lambda p, at: (0, 0, 0))],
+        aliases={1 + k: k for k in range(given)},
+    )
+
+
+def store_packed(ref, k, value, ff):
+    rows, cols = value.shape
+    start = k * rows * cols // ff
+    for cut in range(cols // ff):
+        at = slice(start + cut * rows, start + (cut + 1) * rows)
+        ref[0, at, :] = value[:, cut * ff : (cut + 1) * ff]
+
+
+def fill_piece(place, totals, received):
+    n = len(totals)
+    ff = received.shape[2]
+
+    def body(place_ref, *refs):
+        packed, outs = refs[n], refs[n + 1 :]
+        start = 0
+        for out in outs:
+            _, rows, cols = out.shape
+            for cut in range(cols // ff):
+                out[0, :, cut * ff : (cut + 1) * ff] = wide(packed[0, start : start + rows, :])
+                start += rows
+
+    return call(
+        body,
+        [shape(t.shape, t.dtype) for t in totals],
+        [*totals, received],
+        [place],
+        received.size,
+        grid=(1,),
+        in_specs=[pl.BlockSpec(memory_space=pl.ANY)] * n
+        + [pl.BlockSpec(received.shape, lambda p, at: (0, 0, 0))],
+        out_specs=[pl.BlockSpec((1,) + t.shape[1:], lambda p, at: (at[0], 0, 0)) for t in totals],
+        aliases={1 + k: k for k in range(n)},
+    )
+
+
+def middle_backward(me, parts, middle, gain, upstream, count):
+    rows, width = middle.shape
+    chunk = width // count
+    n = len(parts)
+
+    def body(me_ref, middle_ref, gain_ref, up_ref, *refs):
+        grad = sum_parts([b[...] for b in refs[:n]])
+        out_ref, low_ref, sum_ref = refs[n:]
+        middle = middle_ref[...]
+        scale = lax.rsqrt(jnp.mean(middle * middle, axis=-1, keepdims=True) + epsilon)
+        hat = middle * scale
+        sum_ref[...] = jnp.sum(grad * hat, axis=0, keepdims=True)
+        weighted = grad * gain_ref[...]
+        total = wide(up_ref[...]) + scale * (
+            weighted - hat * jnp.mean(weighted * hat, axis=-1, keepdims=True)
+        )
+        out_ref[...] = total
+        rounded = low(total)
+        for r in range(count):
+            low_ref[:, column(r, me_ref[0], chunk)] = rounded[:, r * chunk : (r + 1) * chunk]
+
+    return call(
+        body,
+        [
+            shape((rows, width), jnp.float32),
+            shape((rows, width), jnp.bfloat16),
+            shape((1, width), jnp.float32),
+        ],
+        [middle, gain, upstream, *parts],
+        [me],
+        12 * rows * width,
+    )
+
+
+def attention_backward_start(queries, attended, branch_chunks, out_chunks, local_q):
+    out_chunks, w_cols = out_chunks
+    kv_rows, all_rows = queries.shape
+    tokens = all_rows // local_q
+    group = local_q // (kv_rows // HEAD_SIZE)
+    nb, nw = len(branch_chunks), len(out_chunks)
+    width = branch_chunks[0].shape[1]
+
+    def body(q_ref, att_ref, *refs):
+        b_refs, w_refs = refs[:nb], refs[nb : nb + nw]
+        qn_ref, dot_ref, don_ref, delta_ref = refs[nb + nw :]
+        branch = jnp.concatenate([b[...] for b in b_refs], axis=0)
+        weight = jnp.concatenate([w[:, w_cols] for w in w_refs], axis=0)
+        grad = low(dot_nn(branch, weight).T)
+        blocks = [grad[h * HEAD_SIZE : (h + 1) * HEAD_SIZE] for h in range(local_q)]
+        dot_ref[...] = padded_heads(blocks, group)
+        for h in range(local_q):
+            cols = slice(h * tokens, (h + 1) * tokens)
+            attended_h = att_ref[h * HEAD_SIZE : (h + 1) * HEAD_SIZE, :]
+            delta_ref[:, cols] = jnp.sum(wide(blocks[h]) * attended_h, axis=0, keepdims=True)
+            qn_ref[cols, :] = q_ref[:, cols].T
+            don_ref[cols, :] = dot_ref[:, cols].T
+
+    bf = jnp.bfloat16
+    return call(
+        body,
+        [
+            shape((all_rows, kv_rows), bf),
+            shape((kv_rows, all_rows), bf),
+            shape((all_rows, kv_rows), bf),
+            shape((1, all_rows), jnp.float32),
+        ],
+        [queries, attended, *branch_chunks, *out_chunks],
+        [],
+        2 * tokens * width * local_q * HEAD_SIZE,
+    )
+
+
+def attention_backward_part(offset, total, queries, kv_chunks, extras, numbers, key_pos, query_pos,
+                            lse, started, local_q, rotation_table=()):
+    kv_rows, all_rows = queries.shape
+    tokens = all_rows // local_q
+    group = local_q // (kv_rows // HEAD_SIZE)
+    n = len(kv_chunks)
+    first, final = total is None, len(rotation_table) > 0
+    extra_rows, width = extras[0].shape
+    cuts = width // tokens
+    kv_end = 2 * kv_rows
+
+    def body(off_ref, *refs):
+        if not first:
+            before_ref, refs = refs[0], refs[1:]
+        extra_refs, refs = refs[:n], refs[n:]
+        q_ref, kv_refs = refs[0], refs[1 : 1 + n]
+        kpos_ref, qpos_ref, lse_ref = refs[1 + n : 4 + n]
+        qn_ref, dot_ref, don_ref, delta_ref = refs[4 + n : 8 + n]
+        refs = refs[8 + n :]
+        if final:
+            cos_ref, sin_ref, dq_out = refs[:3]
+            kv_outs = refs[3 : 3 + n]
+            dq_ref, dk_ref, dv_ref = refs[3 + n :]
+        else:
+            dq_ref, kv_outs = refs[0], refs[1 : 1 + n]
+            dk_ref, dv_ref = refs[1 + n :]
+        off = off_ref[0]
+        dq_ref[...] = jnp.zeros_like(dq_ref) if first else before_ref[...]
+        for index, r in enumerate(numbers):
+
+            def block(index=index, r=r):
+                keys_t = kv_refs[index][:kv_rows, :]
+                keys = keys_t.T
+                values = kv_refs[index][kv_rows:, :].T
+                dk_ref[...] = jnp.zeros_like(dk_ref)
+                dv_ref[...] = jnp.zeros_like(dv_ref)
+
+                def head(h, _):
+                    cols = pl.ds(pl.multiple_of(h * tokens, tokens), tokens)
+                    scores = dot_nn(keys, q_ref[:, cols])
+                    probs = jnp.exp(scores - lse_ref[:, cols])
+                    if r == 0:
+                        probs = jnp.where(kpos_ref[...] <= qpos_ref[...], probs, 0.0)
+                    prob_grad = dot_nn(values, dot_ref[:, cols])
+                    score_grad = low(probs * (prob_grad - delta_ref[:, cols]))
+                    dv_ref[...] += dot_nn(low(probs), don_ref[cols, :])
+                    dk_ref[...] += dot_nn(score_grad, qn_ref[cols, :])
+                    dq_ref[:, cols] += dot_nn(keys_t, score_grad)
+                    return 0
+
+                lax.fori_loop(0, local_q, head, 0)
+                kv_outs[index][:kv_rows, :] = low(dk_ref[...].T)
+                kv_outs[index][kv_rows:kv_end, :] = low(dv_ref[...].T)
+
+            for cut in range(cuts):
+                at = slice(kv_end + cut * extra_rows, kv_end + (cut + 1) * extra_rows)
+                kv_outs[index][at, :] = extra_refs[index][:, cut * tokens : (cut + 1) * tokens]
+
+            if r == 0:
+                block()
+            else:
+                live = (r ^ off) < off
+                pl.when(live)(block)
+
+                @pl.when(jnp.logical_not(live))
+                def _(index=index):
+                    kv_outs[index][:kv_end, :] = jnp.zeros((kv_end, tokens), jnp.bfloat16)
+
+        if not final:
+            return
+        cosine, sine = cos_ref[...], -sin_ref[...]
+        for h in range(local_q):
+            rows = slice((h // group) * HEAD_SIZE, (h // group + 1) * HEAD_SIZE)
+            cols = slice(h * tokens, (h + 1) * tokens)
+            part = dq_ref[rows, cols] * (HEAD_SIZE ** (-0.5))
+            dq_out[h * HEAD_SIZE : (h + 1) * HEAD_SIZE, :] = low(rope_rows(part, cosine, sine))
+
+    bf, f32 = jnp.bfloat16, jnp.float32
+    operands = [*extras, queries, *kv_chunks, key_pos, query_pos, lse, *started, *rotation_table]
+    operands = operands if first else [total, *operands]
+    outs = [shape((local_q * HEAD_SIZE, tokens), bf) if final else shape((kv_rows, all_rows), f32)]
+    scratch = [pltpu.VMEM((kv_rows, all_rows), f32)] if final else []
+    scratch += [pltpu.VMEM((tokens, kv_rows), f32)] * 2
+    return call(
+        body,
+        outs + [shape((kv_end + cuts * extra_rows, tokens), bf)] * n,
+        operands,
+        [offset],
+        10 * all_rows * tokens * n * kv_rows,
+        scratch=scratch,
+        transcendentals=all_rows * tokens * n,
+        aliases={1: 0} if not first and not final else None,
+    )
+
+
+def row_grads(me, pairs, count):
+    tokens = pairs[0][1].shape[1]
+    width = pairs[0][0][0].shape[1]
+    cols = sum(columns.shape[0] for _, columns in pairs)
+    chunk = width // count
+    counts = [len(x_chunks) + 1 for x_chunks, _ in pairs]
+
+    def body(me_ref, *refs):
+        out_ref, refs, left = refs[-1], list(refs[:-1]), 0
+        for n in counts:
+            mine, refs = refs[:n], refs[n:]
+            x = jnp.concatenate([r[...] for r in mine[:-1]], axis=0)
+            total = low(dot_tn(x, low(mine[-1][...]).T))
+            right = left + total.shape[1]
+            for r in range(count):
+                part = total[r * chunk : (r + 1) * chunk]
+                out_ref[pl.ds(r ^ me_ref[0], 1), :, left:right] = part[None]
+            left = right
+
+    operands = [x for x_chunks, columns in pairs for x in (*x_chunks, columns)]
+    outs = [shape((count, chunk, cols), jnp.bfloat16)]
+    return call(body, outs, operands, [me], 2 * tokens * width * cols)[0]
+
+
+def input_parts(me, kv_parts, middle, query_grad, x_chunks, w_chunks, cosine, sine, gain, local_kv, count):
+    w_chunks, w_cols = w_chunks
+    n, nx, nw = len(kv_parts), len(x_chunks), len(w_chunks)
+    rows, width = x_chunks[0].shape
+    tokens = query_grad.shape[1]
+    kv_rows = local_kv * HEAD_SIZE
+    chunk = width // count
+
+    def body(*refs):
+        me_ref = refs[0]
+        parts = refs[1 : 1 + n]
+        middle_ref = refs[1 + n]
+        refs = refs[1:]
+        dq_ref = refs[1 + n]
+        x_refs = refs[2 + n : 2 + n + nx]
+        w_refs = refs[2 + n + nx : 2 + n + nx + nw]
+        cos_ref, sin_ref, gain_ref = refs[2 + n + nx + nw : 5 + n + nx + nw]
+        outs = refs[5 + n + nx + nw :]
+        in_refs, grad_ref, sum_ref, out_ref = outs[:nx], *outs[nx:]
+        total = sum_parts([p[...] for p in parts])
+        cosine, sine = cos_ref[...], -sin_ref[...]
+        blocks = [
+            low(rope_rows(total[h * HEAD_SIZE : (h + 1) * HEAD_SIZE], cosine, sine))
+            for h in range(local_kv)
+        ]
+        for cut in range(width // tokens):
+            at = slice(cut * tokens, (cut + 1) * tokens)
+            mixed = total[2 * kv_rows + cut * rows : 2 * kv_rows + (cut + 1) * rows]
+            out_ref[:, at] = low(middle_ref[:, at] + mixed)
+        values = low(total[kv_rows : 2 * kv_rows])
+        columns = jnp.concatenate([dq_ref[...], *blocks, values], axis=0).T
+        weight = jnp.concatenate([w[:, w_cols] for w in w_refs], axis=0)
+        sums = jnp.zeros((1, width), jnp.float32)
+        for m in range(nx):
+            part = dot_nt(columns[m * rows : (m + 1) * rows], weight)
+            in_refs[m][...] = low(part)
+            sums = sums + jnp.sum(part * wide(x_refs[m][...]), axis=0, keepdims=True)
+        for r in range(count):
+            at = column(r, me_ref[0], chunk)
+            sum_ref[:, at] = sums[:, r * chunk : (r + 1) * chunk] / gain_ref[:, at]
+        x = jnp.concatenate([x[...] for x in x_refs], axis=0)
+        grads = dot_tn(x, columns[:, -2 * kv_rows :])
+        for r in range(count):
+            grad_ref[pl.ds(r ^ me_ref[0], 1)] = low(grads[r * chunk : (r + 1) * chunk])[None]
+
+    return call(
+        body,
+        [shape((rows, width), jnp.bfloat16)] * nx
+        + [shape((count, chunk, 2 * kv_rows), jnp.bfloat16)]
+        + [shape((1, width), jnp.float32), shape((rows, width), jnp.bfloat16)],
+        [*kv_parts, middle, query_grad, *x_chunks, *w_chunks, cosine, sine, gain],
+        [me],
+        4 * tokens * width * w_chunks[0].shape[1],
+    )
+
+
+def input_backward(me, parts, layer_input, gain, middle_grad, count):
+    rows, width = layer_input.shape
+    chunk = width // count
+    n = len(parts)
+
+    def body(me_ref, x_ref, gain_ref, middle_ref, *refs):
+        part = sum_parts([p[...] for p in refs[:n]])
+        out_ref = refs[n]
+        for r in range(count):
+            out_ref[:, column(r, me_ref[0], chunk)] = part[:, r * chunk : (r + 1) * chunk]
+        grad = out_ref[...]
+        x = wide(x_ref[...])
+        scale = lax.rsqrt(jnp.mean(x * x, axis=-1, keepdims=True) + epsilon)
+        hat = x * scale
+        weighted = grad * gain_ref[...]
+        out_ref[...] = middle_ref[...] + scale * (
+            weighted - hat * jnp.mean(weighted * hat, axis=-1, keepdims=True)
+        )
+
+    return call(
+        body,
+        [shape((rows, width), jnp.float32)],
+        [layer_input, gain, middle_grad, *parts],
+        [me],
+        10 * rows * width,
+    )[0]
+
+
+def exchange_sum(chunks):
+    received = lax.all_to_all(chunks, "dp", split_axis=0, concat_axis=0, tiled=True)
+    return jnp.sum(received.astype(jnp.float32), axis=0)
+
+
+def after(value, *others):
+    return lax.optimization_barrier((value, *others))[0]
+
+
+def layer_shards(
+    layer_input,
+    first_gain,
+    query_weight,
+    key_matrix,
+    value_matrix,
+    output_weight,
+    second_gain,
+    gate_weight,
+    up_weight,
+    down_weight,
+    routes,
+    combine,
+    upstream,
+):
+    rows, width = layer_input.shape
+    topk = routes.shape[1]
+    most = max(2, 5 * rows * topk // (4 * EXPERTS))
+    devices = lax.axis_size("dp")
+    groups = lax.axis_size("mp")
+    pieces_dev = gate_weight.shape[0]
+    split = FF // gate_weight.shape[2]
+    local_q = query_weight.shape[1] // HEAD_SIZE
+    local_kv = key_matrix.shape[1] // HEAD_SIZE
+    tokens = rows * groups
+    span = SEQUENCE_TOKENS // tokens
+    if span != devices or pieces_dev % 2 or groups % 2:
+        return shards(
+            layer_input, first_gain, query_weight, key_matrix, value_matrix, output_weight,
+            second_gain, gate_weight, up_weight, down_weight, routes, combine, upstream,
+        )
+    dp_at, mp_at = lax.axis_index("dp"), lax.axis_index("mp")
+    me = jnp.full((1,), dp_at, jnp.int32)
+    offset = jnp.full((1,), dp_at % span, jnp.int32)
+    gain_one, gain_two = first_gain.reshape(1, width), second_gain.reshape(1, width)
+
+    chunk_at = jnp.arange(groups, dtype=jnp.int32) ^ mp_at
+    inside = (chunk_at[:, None] * rows + jnp.arange(rows, dtype=jnp.int32)[None, :]).reshape(tokens)
+    positions = (dp_at % span) * tokens + inside
+    freqs = theta ** (-jnp.arange(HEAD_SIZE // 2, dtype=jnp.float32) * 2.0 / HEAD_SIZE)
+    angles = freqs[:, None] * positions.astype(jnp.float32)[None, :]
+    cosine, sine = jnp.cos(angles), jnp.sin(angles)
+
+    numbers = jnp.arange(EXPERTS, dtype=jnp.int32)
+    equal = routes.T[None, :, :] == numbers[:, None, None]
+    match = jnp.sum(equal.astype(jnp.float32), axis=1)
+    weight_table = jnp.sum(jnp.where(equal, combine.T[None, :, :], 0.0), axis=1)
+    line = jnp.arange(rows, dtype=jnp.int32)
+    earlier = (line[:, None] < line[None, :]).astype(jnp.bfloat16)
+    rank = jnp.dot(match.astype(jnp.bfloat16), earlier, preferred_element_type=jnp.float32)
+    terms = [low(jnp.where(match > 0, rank, -1.0))]
+    rest = weight_table
+    for _ in range(3):
+        term = lax.reduce_precision(rest, 8, 7)
+        terms.append(low(term))
+        rest = rest - term
+    table = jnp.stack(terms, axis=0)
+    expert_at = (dp_at * pieces_dev + jnp.arange(pieces_dev, dtype=jnp.int32)) // split
+    halves = pieces_dev // 2
+    first_piece = (mp_at % 2) * halves
+    order = (first_piece + jnp.arange(pieces_dev, dtype=jnp.int32)) % pieces_dev
+    experts_order = jnp.take(expert_at, order)
+
+    dp_order = jnp.arange(devices, dtype=jnp.int32) ^ dp_at
+
+    selected = jnp.concatenate([dp_order, me, order])
+
+    normed = first_norm_rows(layer_input, gain_one, me, devices)
+    weight_cols = [w.shape[1] for w in (query_weight, key_matrix, value_matrix)]
+    qkv_cols = sum(weight_cols)
+    out_rows, out_cols = output_weight.shape
+    payload = [query_weight, key_matrix, value_matrix, output_weight, table.reshape(out_rows, -1)]
+    payloads = xor_gather(jnp.concatenate(payload, axis=1), "dp")
+    qkv_chunks = (payloads, slice(0, qkv_cols))
+    out_chunks = (payloads, slice(qkv_cols, qkv_cols + out_cols))
+    tables = routing_tables(
+        experts_order, payloads, slice(qkv_cols + out_cols, payloads[0].shape[1]), EXPERTS, most,
+        pieces_dev,
+    )
+    x_chunks = xor_gather(normed, "mp")
+    queries, kv_own = project(x_chunks, qkv_chunks, cosine, sine, local_q, local_kv)
+    key_pos, query_pos = inside.reshape(tokens, 1), inside.reshape(1, tokens)
+    kv_chunks, state, done = [kv_own] + [None] * (devices - 1), None, []
+    forward_order = [(0,)] + [(r, r + 1) for r in range(1, devices - 1, 2)] + [(devices - 1,)]
+
+    def attend(numbers, state):
+        return attention_part(
+            offset, state, queries, [kv_chunks[r] for r in numbers], numbers, key_pos, query_pos,
+            local_q,
+        )[0]
+
+    for r in sorted(range(1, devices), key=lambda r: (bin(r).count("1"), -(r & -r))):
+        near = r & -r
+        source = kv_chunks[r ^ near]
+        hops = bin(r).count("1") - 1
+        if r > devices // 2 and hops > 0:
+            while len(done) < hops:
+                done.append(attend(forward_order[len(done)], state))
+                state = done[-1]
+            source = after(source, done[hops - 1])
+        kv_chunks[r] = lax.ppermute(source, "dp", [(i, i ^ near) for i in range(devices)])
+    for numbers in forward_order[len(done) :]:
+        state = attend(numbers, state)
+    gathered = lax.all_gather(after(upstream, kv_chunks[-1]), "dp", axis=0, tiled=False)
+    attended, lse, *branch_chunks = attention_end(state, out_chunks, local_q, kv_own.shape[0] // 2, groups)
+
+    middle, second_norm = middle_rows(
+        me, layer_input, xor_scatter(branch_chunks, "mp"), gain_two, devices
+    )
+    norm_chunks = xor_gather(second_norm, "dp")
+    far_pairs = [[(i, i ^ g) for i in range(groups)] for g in range(2, groups, 2)]
+    gathered_far = [lax.ppermute(after(gathered, second_norm), "mp", pairs) for pairs in far_pairs]
+    expert_weights = (gate_weight, up_weight, down_weight)
+    own = experts(
+        selected, norm_chunks, gathered, tables,
+        *expert_weights, most, pieces_dev, True,
+    )
+    mixture_chunks, back_chunks = own[2 : 2 + devices], own[2 + devices :]
+    swap = [(i, i ^ 1) for i in range(groups)]
+    fields = [own[0], lax.ppermute(own[1], "mp", swap)]
+    back_parts = xor_scatter(back_chunks, "dp")
+    middle_grad, branch_low, second_sum = middle_backward(
+        me, back_parts, middle, gain_two, upstream, devices
+    )
+
+    branch_rows = xor_gather(branch_low, "mp")
+    norm_here = after(stacked(norm_chunks), branch_rows[-1], *gathered_far)
+    far_groups = [
+        (rows_far, *[lax.ppermute(v, "mp", pairs) for v in (norm_here, tables)])
+        for rows_far, pairs in zip(gathered_far, far_pairs)
+    ]
+    started = attention_backward_start(queries, attended, branch_rows, out_chunks, local_q)
+    backward = sorted(range(devices), key=lambda r: (-bin(r).count("1"), -r))
+    backward_order = [tuple(backward[i : i + 2]) for i in range(0, devices - 2, 2)]
+    backward_order += [(r,) for r in backward[-2:]]
+    total, pending, arrived = None, [[] for _ in range(devices)], []
+    for numbers in backward_order:
+        last = numbers is backward_order[-1]
+        if len(arrived) > 1 and arrived[-2]:
+            total = after(total, *arrived[-2])
+        total, *parts = attention_backward_part(
+            offset, total, queries, [kv_chunks[r] for r in numbers],
+            [mixture_chunks[r] for r in numbers], numbers, key_pos, query_pos, lse, started, local_q,
+            (cosine, sine) if last else (),
+        )
+        for r, part in zip(numbers, parts):
+            pending[r].append(part)
+        arrived.append([])
+        for r in numbers:
+            near = r & -r
+            if r:
+                came = lax.ppermute(
+                    add_parts(pending[r]), "dp", [(i, i ^ near) for i in range(devices)]
+                )
+                pending[r ^ near].append(came)
+                arrived[-1].append(came)
+    query_plain, kv_parts = total, pending[0]
+    rows_grad = exchange_sum(
+        row_grads(me, [(x_chunks, query_plain), (branch_rows, attended)], devices)
+    )
+    query_cols = local_q * HEAD_SIZE
+    query_grad, out_grad = rows_grad[:, :query_cols], rows_grad[:, query_cols:]
+
+    for rows_far, norm_far, tables_far in far_groups:
+        kept, sent = experts(
+            selected, [after(norm_far, query_plain)], rows_far, tables_far, *expert_weights,
+            most, pieces_dev, False,
+        )
+        fields += [kept, lax.ppermute(sent, "mp", swap)]
+        kv_parts[0] = after(kv_parts[0], kept)
+    outs = input_parts(
+        me, kv_parts, middle, query_plain, x_chunks, qkv_chunks, cosine, sine, gain_one, local_kv,
+        devices,
+    )
+    in_chunks, (kv_weights, first_sum, layer_output) = outs[:groups], outs[groups:]
+    fields[0] = after(fields[0], first_sum)
+    totals, received = [], []
+    for i in range(halves):
+        places = jnp.stack([first_piece + i, jnp.int32(i)])
+        grads = expert_weight_grads(places, fields, totals, pieces_dev, FF // split)
+        totals = grads[:3]
+        received.append(lax.ppermute(grads[3], "mp", swap))
+    for i in range(halves):
+        place = jnp.full((1,), halves - first_piece + i, jnp.int32)
+        totals = fill_piece(place, totals, received[i])
+    gate_grad, up_grad, down_grad = totals
+    in_parts = xor_scatter(in_chunks, "mp")
+    kv_grad = exchange_sum(kv_weights)
+    kv_cols = local_kv * HEAD_SIZE
+    input_grad = input_backward(me, in_parts, layer_input, gain_one, middle_grad, devices)
+    gains = butterfly_sum(jnp.concatenate([first_sum, second_sum], axis=0), "mp")
+    gains = butterfly_sum(after(gains, in_parts[-1]), "dp")
+    first_gain_grad, second_gain_grad = gains[0], gains[1]
+    return (
+        layer_output,
+        input_grad,
+        first_gain_grad,
+        second_gain_grad,
+        query_grad,
+        kv_grad[:, :kv_cols],
+        kv_grad[:, kv_cols:],
+        out_grad,
+        gate_grad,
+        up_grad,
+        down_grad,
+    )
+
+
 def solution(mesh):
     in_specs = (
         P(("dp", "mp"), None),
@@ -419,4 +1471,5 @@
         P("dp", None, None),
         P("dp", None, None),
     )
-    return jax.shard_map(shards, mesh=mesh, in_specs=in_specs, out_specs=out_specs, check_vma=False)
+    return jax.shard_map(
+        layer_shards, mesh=mesh, in_specs=in_specs, out_specs=out_specs, check_vma=False)

time: 856 us -> 423 us (0.49)
  waiting for transfers between devices: 347 us -> 158 us
  blocking collectives: 169 us -> 0 us
  Pallas kernels: 0 us -> 96.4 us
  matrix products: 63.3 us -> 0.14 us
  other arithmetic: 58.7 us -> 8.2 us
  local copies, waits for them, and re-layouts: 70.6 us -> 31.1 us
  loops' own time: 13.7 us -> 0 us
    all_to_all x4 -> x2, waiting for transfers between devices: 200 us -> 0.01 us  [exchange_sum(): lax.all_to_all(chunks, 'dp', split_axis=0, concat_axis=0, tiled=True)]
    all_gather x4 -> x0, blocking collectives: 128 us -> none  [the longest x1 32.8 us: shards(): lax.all_gather(key_matrix, 'dp', axis=0, tiled=True)]
    ppermute x28 -> x59, waiting for transfers between devices: 60.4 us -> 158 us  [the longest x20 56.8 us: xor_gather(): lax.ppermute(chunks[r ^ low], axis, [(i, i ^ low) for i in range(count)])]
    pallas_call x0 -> x27, Pallas kernels: none -> 96.4 us  [call(): pl.pallas_call(body, out_shape=list(outs), input_output_aliases=aliases o...]
    reduce_scatter x3 -> x0, waiting for transfers between devices: 67.9 us -> none  [the longest x1 35 us: shards(): lax.psum_scatter(jnp.concatenate([contract(sequence_rows, query_plain_gra...]
    dot_general x28 -> x1, matrix products: 63.3 us -> 0.14 us  [layer_shards(): jnp.dot(match.astype(jnp.bfloat16), earlier, preferred_element_type=jnp.f...]
    gather x10 -> x1, local copies, waits for them, and re-layouts: 42.3 us -> 0.64 us  [layer_shards(): experts_order = jnp.take(expert_at, order)]
    psum x1 -> x0, blocking collectives: 41.3 us -> none  [shards(): lax.psum((first_gain_part, second_gain_part), ('dp', 'mp'))]
  transfers between devices with their start and end apart: 38 -> 62, of which waited for: 17 -> 34; matrix products, arithmetic and copies ran while one was open for 16% -> 2% of each run, Pallas kernels for 0% -> 22%
where the time goes in v1:
time: 423 us; the launch traced here: 416 us
  waiting for transfers between devices  158 us (37%)
  starting transfers between devices  106 us (25%)
  Pallas kernels  96.4 us (23%)
  local copies, waits for them, and re-layouts  31.1 us (7%)
  between operations  15.3 us (4%)
  other arithmetic  8.2 us (2%)
    pallas_call x27, Pallas kernels, call(): pl.pallas_call(body, out_shape=list(outs), input_output_aliases=aliases o...  96.4 us
    ppermute x20, waiting for transfers between devices, xor_gather(): lax.ppermute(chunks[r ^ low], axis, [(i, i ^ low) for i in range(count)])  56.8 us
    ppermute x7, waiting for transfers between devices, layer_shards(): lax.ppermute(add_parts(pending[r]), 'dp', [(i, i ^ near) for i in range(d...  34.4 us
    ppermute x13, waiting for transfers between devices, xor_scatter(): lax.ppermute(total, axis, [(i, i ^ low) for i in range(count)])  32 us
    ppermute x7, waiting for transfers between devices, layer_shards(): lax.ppermute(source, 'dp', [(i, i ^ near) for i in range(devices)])  30 us
    ppermute x20, starting transfers between devices, xor_gather(): lax.ppermute(chunks[r ^ low], axis, [(i, i ^ low) for i in range(count)])  28.5 us
    unnamed x172, local copies, waits for them, and re-layouts  28.3 us
    ppermute x7, starting transfers between devices, layer_shards(): lax.ppermute(add_parts(pending[r]), 'dp', [(i, i ^ near) for i in range(d...  21 us
  transfers between devices with their start and end apart: 62, of which 34 were waited for; matrix products, arithmetic and copies ran while one was open for 2% of the time, Pallas kernels for 22%

profile of v1, /device:TPU:0, one launch (start us, length us, event | category | flops | bytes accessed | tf_op | source)
XLA Modules:
  0.0 416.0 jit_solution(10495575007215628480)
XLA Ops:
  11.4 4.1 collective-permute-start.6
  15.5 1.6 collective-permute-start.4
  20.4 1.6 collective-permute-start.1
  22.0 4.1 collective-permute-done.6.refs_8_.refs_4_.refs_15_
  28.9 4.0 collective-permute-done.8.refs_10_.refs_6_.refs_17_
  35.4 4.9 %collective-permute-done.5.refs_7_.refs_3_.refs_14_ = bf16[128,896]{1,0:T(8,128)(2,1)S(1)} collective-permute-done((bf16[128,896]{1,0:T(8,128)(2,1)S(1)}, bf16[128,896]{1,0:T(8,128)(2,1)S(1)}, u32[]{:S(2)}, u32[]{:S(2)}) %collective-permute-start.5) | collective-permute-done | bytes 229408 | tf_op jit(solution)/shard_map/ppermute | solution.py:403
  40.3 3.6 collective-permute-done.9.refs_11_.refs_7_.refs_18_
  43.9 1.6 shard_map.213
  45.5 3.4 collective-permute-start.13
  50.9 3.7 shard_map.214.refs_0_
  54.6 5.6 %collective-permute-done.13.refs_3_.refs_4_ = bf16[256,512]{1,0:T(8,128)(2,1)} collective-permute-done((bf16[256,512]{1,0:T(8,128)(2,1)}, bf16[256,512]{1,0:T(8,128)(2,1)}, u32[]{:S(2)}, u32[]{:S(2)}) %collective-permute-start.13) | collective-permute-done | bytes 262176 | tf_op jit(solution)/shard_map/ppermute | solution.py:1337
  62.3 6.3 %collective-permute-done.15.refs_3_.refs_4_ = bf16[256,512]{1,0:T(8,128)(2,1)S(1)} collective-permute-done((bf16[256,512]{1,0:T(8,128)(2,1)}, bf16[256,512]{1,0:T(8,128)(2,1)S(1)}, u32[]{:S(2)}, u32[]{:S(2)}) %collective-permute-start.15) | collective-permute-done | bytes 262176 | tf_op jit(solution)/shard_map/ppermute | solution.py:1337
  68.6 1.5 collective-permute-start.16
  70.8 5.1 %collective-permute-done.16.refs_2_.refs_3_ = bf16[256,512]{1,0:T(8,128)(2,1)S(1)} collective-permute-done((bf16[256,512]{1,0:T(8,128)(2,1)S(1)}, bf16[256,512]{1,0:T(8,128)(2,1)S(1)}, u32[]{:S(2)}, u32[]{:S(2)}) %collective-permute-start.16) | collective-permute-done | bytes 262176 | tf_op jit(solution)/shard_map/ppermute | solution.py:1337
  76.6 1.6 collective-permute-start.12
  78.7 7.7 %collective-permute-done.12.refs_2_.refs_5_ = bf16[256,512]{1,0:T(8,128)(2,1)S(1)} collective-permute-done((bf16[256,512]{1,0:T(8,128)(2,1)}, bf16[256,512]{1,0:T(8,128)(2,1)S(1)}, u32[]{:S(2)}, u32[]{:S(2)}) %collective-permute-start.12) | collective-permute-done | bytes 262176 | tf_op jit(solution)/shard_map/ppermute | solution.py:1337
  87.7 4.0 collective-permute-done.14.refs_2_.refs_4_
  96.9 1.6 collective-permute-start.19
  98.5 6.8 %collective-permute-done.19.refs_2_ = bf16[128,1024]{1,0:T(8,128)(2,1)S(1)} collective-permute-done((bf16[128,1024]{1,0:T(8,128)(2,1)S(1)}, bf16[128,1024]{1,0:T(8,128)(2,1)S(1)}, u32[]{:S(2)}, u32[]{:S(2)}) %collective-permute-start.19) | collective-permute-done | bytes 262176 | tf_op jit(solution)/shard_map/ppermute | solution.py:415
  106.6 5.5 %collective-permute-start.23 = (bf16[128,1024]{1,0:T(8,128)(2,1)S(1)}, bf16[128,1024]{1,0:T(8,128)(2,1)S(1)}, u32[]{:S(2)}, u32[]{:S(2)}) collective-permute-start(bf16[128,1024]{1,0:T(8,128)(2,1)S(1)} %get-tuple-element.102.refs_0_), channel_id=1, source_target_pairs={{0,16},{4,20},{8,24},{12,28},{16,0},{20,4},{24,8},{28,12},{1,17},{... | collective-permute-start | bytes 786440 | tf_op jit(solution)/shard_map/ppermute | solution.py:403
  112.1 3.8 collective-permute-start.21
  115.9 17.2 %collective-permute-done.23.refs_4_ = bf16[128,1024]{1,0:T(8,128)(2,1)S(1)} collective-permute-done((bf16[128,1024]{1,0:T(8,128)(2,1)S(1)}, bf16[128,1024]{1,0:T(8,128)(2,1)S(1)}, u32[]{:S(2)}, u32[]{:S(2)}) %collective-permute-start.23) | collective-permute-done | bytes 262176 | tf_op jit(solution)/shard_map/ppermute | solution.py:403
  133.8 1.5 collective-permute-start.20
  137.3 4.0 collective-permute-done.25.refs_6_
  141.3 1.5 collective-permute-start.26
  142.9 1.5 collective-permute-start.41
  147.2 1.6 collective-permute-done.24.refs_5_
  148.8 5.6 %collective-permute-done.22.refs_3_ = bf16[128,1024]{1,0:T(8,128)(2,1)} collective-permute-done((bf16[128,1024]{1,0:T(8,128)(2,1)S(1)}, bf16[128,1024]{1,0:T(8,128)(2,1)}, u32[]{:S(2)}, u32[]{:S(2)}) %collective-permute-start.22) | collective-permute-done | bytes 262176 | tf_op jit(solution)/shard_map/ppermute | solution.py:403
  154.4 4.5 %collective-permute-done.26.refs_7_ = bf16[128,1024]{1,0:T(8,128)(2,1)} collective-permute-done((bf16[128,1024]{1,0:T(8,128)(2,1)}, bf16[128,1024]{1,0:T(8,128)(2,1)}, u32[]{:S(2)}, u32[]{:S(2)}) %collective-permute-start.26) | collective-permute-done | bytes 262176 | tf_op jit(solution)/shard_map/ppermute | solution.py:403
  158.9 23.2 %shard_map.222 = (bf16[2,320,3584]{2,1,0:T(8,128)(2,1)}, bf16[2,320,3584]{2,1,0:T(8,128)(2,1)}, bf16[128,1024]{1,0:T(8,128)(2,1)}, bf16[128,1024]{1,0:T(8,128)(2...) custom-call(s32[13]{0:T(128)} %pad_add_fusion.sel_ref, ...), custom_call_target="tpu_custom_call" | custom-call | flops 31457280 | bytes 175232 | tf_op jit(solution)/shard_map/pallas_call | solution.py:491
  182.1 1.6 collective-permute-start.31
  185.7 5.9 %collective-permute-done.31 = bf16[128,1024]{1,0:T(8,128)(2,1)S(1)} collective-permute-done((bf16[128,1024]{1,0:T(8,128)(2,1)}, bf16[128,1024]{1,0:T(8,128)(2,1)S(1)}, u32[]{:S(2)}, u32[]{:S(2)}) %collective-permute-start.31) | collective-permute-done | bytes 262176 | tf_op jit(solution)/shard_map/ppermute | solution.py:415
  192.7 1.8 collective-permute-start.32
  194.5 1.5 collective-permute-start.27
  198.3 1.8 collective-permute-start.29
  200.1 2.8 collective-permute-done.30
  204.0 2.0 collective-permute-start.33
  206.6 8.4 %collective-permute-done.33.refs_3_ = bf16[128,1024]{1,0:T(8,128)(2,1)S(1)} collective-permute-done((bf16[128,1024]{1,0:T(8,128)(2,1)S(1)}, bf16[128,1024]{1,0:T(8,128)(2,1)S(1)}, u32[]{:S(2)}, u32[]{:S(2)}) %collective-permute-start.33) | collective-permute-done | bytes 262176 | tf_op jit(solution)/shard_map/ppermute | solution.py:415
  218.6 4.9 %collective-permute-done.35.refs_2_.refs_7_ = bf16[128,1024]{1,0:T(8,128)(2,1)S(1)} collective-permute-done((bf16[128,1024]{1,0:T(8,128)(2,1)S(1)}, bf16[128,1024]{1,0:T(8,128)(2,1)S(1)}, u32[]{:S(2)}, u32[]{:S(2)}) %collective-permute-start.35) | collective-permute-done | bytes 262176 | tf_op jit(solution)/shard_map/ppermute | solution.py:403
  223.5 1.5 collective-permute-done.36.refs_3_.refs_8_
  226.2 1.7 collective-permute-start.37
  229.4 1.6 collective-permute-start.42
  230.9 9.4 %collective-permute-done.37 = bf16[512,512]{1,0:T(8,128)(2,1)S(1)} collective-permute-done((bf16[512,512]{1,0:T(8,128)(2,1)S(1)}, bf16[512,512]{1,0:T(8,128)(2,1)S(1)}, u32[]{:S(2)}, u32[]{:S(2)}) %collective-permute-start.37) | collective-permute-done | bytes 524320 | tf_op jit(solution)/shard_map/ppermute | solution.py:1388
  240.8 1.7 collective-permute-start.39
  242.9 10.7 %collective-permute-done.38 = bf16[512,512]{1,0:T(8,128)(2,1)S(1)} collective-permute-done((bf16[512,512]{1,0:T(8,128)(2,1)S(1)}, bf16[512,512]{1,0:T(8,128)(2,1)S(1)}, u32[]{:S(2)}, u32[]{:S(2)}) %collective-permute-start.38) | collective-permute-done | bytes 524320 | tf_op jit(solution)/shard_map/ppermute | solution.py:1388
  255.9 12.9 %collective-permute-start.40 = (bf16[512,512]{1,0:T(8,128)(2,1)S(1)}, bf16[512,512]{1,0:T(8,128)(2,1)S(1)}, u32[]{:S(2)}, u32[]{:S(2)}) collective-permute-start(bf16[512,512]{1,0:T(8,128)(2,1)S(1)} %add_convert_fusion.1), channel_id=1, source_target_pairs={{0,16},{4,20},{8,24},{12,28},{16,0},{20,4},{24,8},{28,12},{1,17},{... | collective-permute-start | bytes 1572872 | tf_op jit(solution)/shard_map/ppermute | solution.py:1388
  268.9 3.5 collective-permute-start.44
  274.9 13.5 %collective-permute-done.40.refs_1_ = bf16[512,512]{1,0:T(8,128)(2,1)S(1)} collective-permute-done((bf16[512,512]{1,0:T(8,128)(2,1)S(1)}, bf16[512,512]{1,0:T(8,128)(2,1)S(1)}, u32[]{:S(2)}, u32[]{:S(2)}) %collective-permute-start.40) | collective-permute-done | bytes 524320 | tf_op jit(solution)/shard_map/ppermute | solution.py:1388
  289.2 5.1 %shard_map.230 = (bf16[256,512]{1,0:T(8,128)(2,1)S(1)}, bf16[512,512]{1,0:T(8,128)(2,1)S(1)}) custom-call(s32[1]{0:T(128)} %bitcast.1.off_ref, f32[128,2048]{1,0:T(8,128)S(1)} %get-tuple-element.141.refs_0_, bf16[128,1024]{1,0:T(8,128)(2,1)S(1)} %copy-done.74, bf16[128,2048]{1,0:T(8,128)(2,1)S(1)} %get-tuple-element.94.refs_0_.refs_1_.q_ref.refs_2_.refs_3_, ...), custom_call_target="tpu_custom_call" | custom-call | flops 5242880 | bytes 18000 | tf_op jit(solution)/shard_map/pallas_call | solution.py:491
  297.7 15.3 %shard_map.231 = (bf16[2,320,3584]{2,1,0:T(8,128)(2,1)}, bf16[2,320,3584]{2,1,0:T(8,128)(2,1)}) custom-call(s32[13]{0:T(128)} %pad_add_fusion.sel_ref, bf16[8,128,1024]{2,1,0:T(8,128)(2,1)} %copy-done.82, bf16[8,128,1024]{2,1,0:T(8,128)(2,1)} %copy-done.81, bf16[8,128,1024]{2,1,0:T(8,128)(2,1)} %copy-done.81, bf16[8,128,1024]{2,1,0:T(8,128)(2,1)} %copy-done.81, ...), custom_call_target="tpu_custom_call" | custom-call | flops 15728640 | bytes 158848 | tf_op jit(solution)/shard_map/pallas_call | solution.py:491
  318.6 1.8 shard_map.234
  320.5 14.5 %all-to-all-start = ((bf16[8,128,512]{2,1,0:T(8,128)(2,1)}), bf16[8,128,512]{2,1,0:T(8,128)(2,1)}, u32[]{:S(2)}, u32[]{:S(2)}) async-start(bf16[8,128,512]{2,1,0:T(8,128)(2,1)} %shard_map.234), calls=%async_computation | async-start | bytes 2097152 | tf_op jit(solution)/shard_map/all_to_all | solution.py:1229
  342.1 3.8 shard_map.232
  345.9 11.0 %shard_map.235 = (f32[4,1024,512]{2,1,0:T(8,128)}, f32[4,1024,512]{2,1,0:T(8,128)}, f32[4,512,1024]{2,1,0:T(8,128)}, bf16[1,3072,512]{2,1,0:T(8,128)(2,1)}) custom-call(s32[2]{0:T(128)} %pad_add_fusion.2.places_ref, bf16[2,320,3584]{2,1,0:T(8,128)(2,1)} %get-tuple-element.160.refs_0_.refs_3_, bf16[2,320,3584]{2,1,0:T(8,128)(2,1)} %collective-permute-done.55.refs_1_.refs_4_, ...), custom_call_target="tpu_custom_call" | custom-call | flops 15728640 | bytes 182272 | tf_op jit(solution)/shard_map/pallas_call | solution.py:491
  356.9 11.1 %shard_map.236 = (f32[4,1024,512]{2,1,0:T(8,128)}, f32[4,1024,512]{2,1,0:T(8,128)}, f32[4,512,1024]{2,1,0:T(8,128)}, bf16[1,3072,512]{2,1,0:T(8,128)(2,1)}) custom-call(s32[2]{0:T(128)} %pad_add_fusion.1.places_ref, f32[4,1024,512]{2,1,0:T(8,128)} %get-tuple-element.163.refs_0_, ...), custom_call_target="tpu_custom_call", output_to_operand_aliasing={{0}: (1, {}), {1}: (2, {}), {2}: (3, {})} | custom-call | flops 15728640 | bytes 280576 | tf_op jit(solution)/shard_map/pallas_call | solution.py:491
  369.2 5.2 %collective-permute-done.48 = bf16[128,1024]{1,0:T(8,128)(2,1)S(1)} collective-permute-done((bf16[128,1024]{1,0:T(8,128)(2,1)S(1)}, bf16[128,1024]{1,0:T(8,128)(2,1)S(1)}, u32[]{:S(2)}, u32[]{:S(2)}) %collective-permute-start.48) | collective-permute-done | bytes 262176 | tf_op jit(solution)/shard_map/ppermute | solution.py:415
  374.5 1.5 collective-permute-start.49
  376.0 6.0 %all-to-all-start.1 = ((bf16[8,128,256]{2,1,0:T(8,128)(2,1)}), bf16[8,128,256]{2,1,0:T(8,128)(2,1)S(1)}, u32[]{:S(2)}, u32[]{:S(2)}) async-start(bf16[8,128,256]{2,1,0:T(8,128)(2,1)} %get-tuple-element.158), calls=%async_computation.1 | async-start | bytes 1048576 | tf_op jit(solution)/shard_map/all_to_all | solution.py:1229
  382.7 3.1 collective-permute-done.51
  385.8 2.1 collective-permute-start.52
  389.6 2.0 collective-permute-start.53
  393.3 2.7 collective-permute-start.54
  399.2 4.7 %shard_map.237 = (f32[4,1024,512]{2,1,0:T(8,128)}, f32[4,1024,512]{2,1,0:T(8,128)}, f32[4,512,1024]{2,1,0:T(8,128)}) custom-call(s32[1]{0:T(128)} %bitcast.17.place_ref, f32[4,1024,512]{2,1,0:T(8,128)} %get-tuple-element.166.refs_0_, f32[4,1024,512]{2,1,0:T(8,128)} %get-tuple-element.167.refs_1_, ...), custom_call_target="tpu_custom_call", output_to_operand_aliasing={{0}: (1, {}), {1}: (2, {}), {2}: (3, {})} | custom-call | flops 6144 | bytes 208896 | tf_op jit(solution)/shard_map/pallas_call | solution.py:491
  404.0 4.7 %shard_map.238 = (f32[4,1024,512]{2,1,0:T(8,128)}, f32[4,1024,512]{2,1,0:T(8,128)}, f32[4,512,1024]{2,1,0:T(8,128)}) custom-call(s32[1]{0:T(128)} %bitcast.16.place_ref, f32[4,1024,512]{2,1,0:T(8,128)} %get-tuple-element.170.refs_0_, f32[4,1024,512]{2,1,0:T(8,128)} %get-tuple-element.171.refs_1_, ...), custom_call_target="tpu_custom_call", output_to_operand_aliasing={{0}: (1, {}), {1}: (2, {}), {2}: (3, {})} | custom-call | flops 6144 | bytes 208896 | tf_op jit(solution)/shard_map/pallas_call | solution.py:491
  (299 shorter events, 76.2 us)
Async XLA Ops:
  7.2 135.7 %all-gather.3.cloned.1.call-start = ((), (), s32[]{:S(2)}) async-start(), calls=%async_computation.2 | async-start | bytes 2359296 | tf_op jit(solution)/shard_map/all_gather | solution.py:1340
  11.4 14.7 %collective-permute-start.6 = (bf16[128,896]{1,0:T(8,128)(2,1)S(1)}, bf16[128,896]{1,0:T(8,128)(2,1)S(1)}, u32[]{:S(2)}, u32[]{:S(2)}) collective-permute-start(bf16[128,896]{1,0:T(8,128)(2,1)S(1)} %constant_dynamic-update-slice_fusion.refs_4_.refs_0_.refs_11_), channel_id=1, source_target_pairs={{0,16},{4,20},{8,24},{12,28},{16,0},{20,4},{24,8},{28,12},{1,17},{... | collective-permute-start | bytes 688136 | tf_op jit(solution)/shard_map/ppermute | solution.py:403
  15.5 11.3 %collective-permute-start.4 = (bf16[128,896]{1,0:T(8,128)(2,1)S(1)}, bf16[128,896]{1,0:T(8,128)(2,1)S(1)}, u32[]{:S(2)}, u32[]{:S(2)}) collective-permute-start(bf16[128,896]{1,0:T(8,128)(2,1)S(1)} %constant_dynamic-update-slice_fusion.refs_4_.refs_0_.refs_11_), channel_id=1, source_target_pairs={{0,8},{4,12},{8,0},{12,4},{16,24},{20,28},{24,16},{28,20},{1,9},{5... | collective-permute-start | bytes 688136 | tf_op jit(solution)/shard_map/ppermute | solution.py:403
  17.1 11.2 %collective-permute-start.3 = (bf16[128,896]{1,0:T(8,128)(2,1)S(1)}, bf16[128,896]{1,0:T(8,128)(2,1)S(1)}, u32[]{:S(2)}, u32[]{:S(2)}) collective-permute-start(bf16[128,896]{1,0:T(8,128)(2,1)S(1)} %constant_dynamic-update-slice_fusion.refs_4_.refs_0_.refs_11_), channel_id=1, source_target_pairs={{0,4},{4,0},{8,12},{12,8},{16,20},{20,16},{24,28},{28,24},{1,5},{5... | collective-permute-start | bytes 688136 | tf_op jit(solution)/shard_map/ppermute | solution.py:403
  20.4 8.4 %collective-permute-start.1 = (bf16[128,1024]{1,0:T(8,128)(2,1)S(1)}, bf16[128,1024]{1,0:T(8,128)(2,1)S(1)}, u32[]{:S(2)}, u32[]{:S(2)}) collective-permute-start(bf16[128,1024]{1,0:T(8,128)(2,1)S(1)} %shard_map.212.refs_0_.refs_7_), channel_id=1, source_target_pairs={{0,2},{1,3},{2,0},{3,1},{4,6},{5,7},{6,4},{7,5},{8,10},{9,11},{10,... | collective-permute-start | bytes 786440 | tf_op jit(solution)/shard_map/ppermute | solution.py:403
  22.0 12.5 %collective-permute-start = (bf16[128,1024]{1,0:T(8,128)(2,1)S(1)}, bf16[128,1024]{1,0:T(8,128)(2,1)S(1)}, u32[]{:S(2)}, u32[]{:S(2)}) collective-permute-start(bf16[128,1024]{1,0:T(8,128)(2,1)S(1)} %shard_map.212.refs_0_.refs_7_), channel_id=1, source_target_pairs={{0,1},{1,0},{2,3},{3,2},{4,5},{5,4},{6,7},{7,6},{8,9},{9,8},{10,11... | collective-permute-start | bytes 786440 | tf_op jit(solution)/shard_map/ppermute | solution.py:403
  26.1 6.7 %collective-permute-start.8 = (bf16[128,896]{1,0:T(8,128)(2,1)S(1)}, bf16[128,896]{1,0:T(8,128)(2,1)S(1)}, u32[]{:S(2)}, u32[]{:S(2)}) collective-permute-start(bf16[128,896]{1,0:T(8,128)(2,1)S(1)} %collective-permute-done.6.refs_8_.refs_4_.refs_15_), channel_id=1, source_target_pairs={{0,8},{4,12},{8,0},{12,4},{16,24},{20,28},{24,16},{28,20},{1,9},{5... | collective-permute-start | bytes 688136 | tf_op jit(solution)/shard_map/ppermute | solution.py:403
  26.8 8.5 %collective-permute-start.7 = (bf16[128,896]{1,0:T(8,128)(2,1)S(1)}, bf16[128,896]{1,0:T(8,128)(2,1)S(1)}, u32[]{:S(2)}, u32[]{:S(2)}) collective-permute-start(bf16[128,896]{1,0:T(8,128)(2,1)S(1)} %collective-permute-done.6.refs_8_.refs_4_.refs_15_), channel_id=1, source_target_pairs={{0,4},{4,0},{8,12},{12,8},{16,20},{20,16},{24,28},{28,24},{1,5},{5... | collective-permute-start | bytes 688136 | tf_op jit(solution)/shard_map/ppermute | solution.py:403
  28.3 11.9 %collective-permute-start.5 = (bf16[128,896]{1,0:T(8,128)(2,1)S(1)}, bf16[128,896]{1,0:T(8,128)(2,1)S(1)}, u32[]{:S(2)}, u32[]{:S(2)}) collective-permute-start(bf16[128,896]{1,0:T(8,128)(2,1)S(1)} %collective-permute-done.4.refs_6_.refs_2_.refs_13_), channel_id=1, source_target_pairs={{0,4},{4,0},{8,12},{12,8},{16,20},{20,16},{24,28},{28,24},{1,5},{5... | collective-permute-start | bytes 688136 | tf_op jit(solution)/shard_map/ppermute | solution.py:403
  28.9 11.4 %collective-permute-start.2 = (bf16[128,1024]{1,0:T(8,128)(2,1)S(1)}, bf16[128,1024]{1,0:T(8,128)(2,1)S(1)}, u32[]{:S(2)}, u32[]{:S(2)}) collective-permute-start(bf16[128,1024]{1,0:T(8,128)(2,1)S(1)} %collective-permute-done.1.refs_2_.refs_9_), channel_id=1, source_target_pairs={{0,1},{1,0},{2,3},{3,2},{4,5},{5,4},{6,7},{7,6},{8,9},{9,8},{10,11... | collective-permute-start | bytes 786440 | tf_op jit(solution)/shard_map/ppermute | solution.py:403
  32.9 11.1 %collective-permute-start.9 = (bf16[128,896]{1,0:T(8,128)(2,1)S(1)}, bf16[128,896]{1,0:T(8,128)(2,1)S(1)}, u32[]{:S(2)}, u32[]{:S(2)}) collective-permute-start(bf16[128,896]{1,0:T(8,128)(2,1)S(1)} %collective-permute-done.8.refs_10_.refs_6_.refs_17_), channel_id=1, source_target_pairs={{0,4},{4,0},{8,12},{12,8},{16,20},{20,16},{24,28},{28,24},{1,5},{5... | collective-permute-start | bytes 688136 | tf_op jit(solution)/shard_map/ppermute | solution.py:403
  45.5 14.7 %collective-permute-start.13 = (bf16[256,512]{1,0:T(8,128)(2,1)}, bf16[256,512]{1,0:T(8,128)(2,1)}, u32[]{:S(2)}, u32[]{:S(2)}) collective-permute-start(bf16[256,512]{1,0:T(8,128)(2,1)} %get-tuple-element.95.refs_1_.refs_3_), channel_id=1, source_target_pairs={{0,16},{4,20},{8,24},{12,28},{16,0},{20,4},{24,8},{28,12},{1,17},{... | collective-permute-start | bytes 786440 | tf_op jit(solution)/shard_map/ppermute | solution.py:1337
  49.1 12.5 %collective-permute-start.11 = (bf16[256,512]{1,0:T(8,128)(2,1)}, bf16[256,512]{1,0:T(8,128)(2,1)S(1)}, u32[]{:S(2)}, u32[]{:S(2)}) collective-permute-start(bf16[256,512]{1,0:T(8,128)(2,1)} %get-tuple-element.95.refs_1_.refs_3_), channel_id=1, source_target_pairs={{0,8},{4,12},{8,0},{12,4},{16,24},{20,28},{24,16},{28,20},{1,9},{5... | collective-permute-start | bytes 786440 | tf_op jit(solution)/shard_map/ppermute | solution.py:1337
  49.4 12.2 %collective-permute-start.10 = (bf16[256,512]{1,0:T(8,128)(2,1)}, bf16[256,512]{1,0:T(8,128)(2,1)S(1)}, u32[]{:S(2)}, u32[]{:S(2)}) collective-permute-start(bf16[256,512]{1,0:T(8,128)(2,1)} %get-tuple-element.95.refs_1_.refs_3_), channel_id=1, source_target_pairs={{0,4},{4,0},{8,12},{12,8},{16,20},{20,16},{24,28},{28,24},{1,5},{5... | collective-permute-start | bytes 786440 | tf_op jit(solution)/shard_map/ppermute | solution.py:1337
  60.3 8.3 %collective-permute-start.15 = (bf16[256,512]{1,0:T(8,128)(2,1)}, bf16[256,512]{1,0:T(8,128)(2,1)S(1)}, u32[]{:S(2)}, u32[]{:S(2)}) collective-permute-start(bf16[256,512]{1,0:T(8,128)(2,1)} %collective-permute-done.13.refs_3_.refs_4_), channel_id=1, source_target_pairs={{0,8},{4,12},{8,0},{12,4},{16,24},{20,28},{24,16},{28,20},{1,9},{5... | collective-permute-start | bytes 786440 | tf_op jit(solution)/shard_map/ppermute | solution.py:1337
  68.6 7.3 %collective-permute-start.16 = (bf16[256,512]{1,0:T(8,128)(2,1)S(1)}, bf16[256,512]{1,0:T(8,128)(2,1)S(1)}, u32[]{:S(2)}, u32[]{:S(2)}) collective-permute-start(bf16[256,512]{1,0:T(8,128)(2,1)S(1)} %collective-permute-done.15.refs_3_.refs_4_), channel_id=1, source_target_pairs={{0,4},{4,0},{8,12},{12,8},{16,20},{20,16},{24,28},{28,24},{1,5},{5... | collective-permute-start | bytes 786440 | tf_op jit(solution)/shard_map/ppermute | solution.py:1337
  76.6 9.8 %collective-permute-start.12 = (bf16[256,512]{1,0:T(8,128)(2,1)}, bf16[256,512]{1,0:T(8,128)(2,1)S(1)}, u32[]{:S(2)}, u32[]{:S(2)}) collective-permute-start(bf16[256,512]{1,0:T(8,128)(2,1)} %copy-done.33), channel_id=1, source_target_pairs={{0,4},{4,0},{8,12},{12,8},{16,20},{20,16},{24,28},{28,24},{1,5},{5... | collective-permute-start | bytes 786440 | tf_op jit(solution)/shard_map/ppermute | solution.py:1337
  78.2 13.5 %collective-permute-start.14 = (bf16[256,512]{1,0:T(8,128)(2,1)}, bf16[256,512]{1,0:T(8,128)(2,1)S(1)}, u32[]{:S(2)}, u32[]{:S(2)}) collective-permute-start(bf16[256,512]{1,0:T(8,128)(2,1)} %collective-permute-done.13.refs_3_.refs_4_), channel_id=1, source_target_pairs={{0,4},{4,0},{8,12},{12,8},{16,20},{20,16},{24,28},{28,24},{1,5},{5... | collective-permute-start | bytes 786440 | tf_op jit(solution)/shard_map/ppermute | solution.py:1337
  95.3 1.5 collective-permute-start.18
  95.3 3.2 collective-permute-start.17
  96.9 8.4 %collective-permute-start.19 = (bf16[128,1024]{1,0:T(8,128)(2,1)S(1)}, bf16[128,1024]{1,0:T(8,128)(2,1)S(1)}, u32[]{:S(2)}, u32[]{:S(2)}) collective-permute-start(bf16[128,1024]{1,0:T(8,128)(2,1)S(1)} %add_convert_fusion.7), channel_id=1, source_target_pairs={{0,2},{1,3},{2,0},{3,1},{4,6},{5,7},{6,4},{7,5},{8,10},{9,11},{10,... | collective-permute-start | bytes 786440 | tf_op jit(solution)/shard_map/ppermute | solution.py:415
  106.6 26.6 %collective-permute-start.23 = (bf16[128,1024]{1,0:T(8,128)(2,1)S(1)}, bf16[128,1024]{1,0:T(8,128)(2,1)S(1)}, u32[]{:S(2)}, u32[]{:S(2)}) collective-permute-start(bf16[128,1024]{1,0:T(8,128)(2,1)S(1)} %get-tuple-element.102.refs_0_), channel_id=1, source_target_pairs={{0,16},{4,20},{8,24},{12,28},{16,0},{20,4},{24,8},{28,12},{1,17},{... | collective-permute-start | bytes 786440 | tf_op jit(solution)/shard_map/ppermute | solution.py:403
  112.1 23.8 %collective-permute-start.21 = (bf16[128,1024]{1,0:T(8,128)(2,1)S(1)}, bf16[128,1024]{1,0:T(8,128)(2,1)S(1)}, u32[]{:S(2)}, u32[]{:S(2)}) collective-permute-start(bf16[128,1024]{1,0:T(8,128)(2,1)S(1)} %get-tuple-element.102.refs_0_), channel_id=1, source_target_pairs={{0,8},{4,12},{8,0},{12,4},{16,24},{20,28},{24,16},{28,20},{1,9},{5... | collective-permute-start | bytes 786440 | tf_op jit(solution)/shard_map/ppermute | solution.py:403
  133.1 8.2 %collective-permute-start.25 = (bf16[128,1024]{1,0:T(8,128)(2,1)S(1)}, bf16[128,1024]{1,0:T(8,128)(2,1)}, u32[]{:S(2)}, u32[]{:S(2)}) collective-permute-start(bf16[128,1024]{1,0:T(8,128)(2,1)S(1)} %collective-permute-done.23.refs_4_), channel_id=1, source_target_pairs={{0,8},{4,12},{8,0},{12,4},{16,24},{20,28},{24,16},{28,20},{1,9},{5... | collective-permute-start | bytes 786440 | tf_op jit(solution)/shard_map/ppermute | solution.py:403
  133.8 13.4 %collective-permute-start.20 = (bf16[128,1024]{1,0:T(8,128)(2,1)S(1)}, bf16[128,1024]{1,0:T(8,128)(2,1)}, u32[]{:S(2)}, u32[]{:S(2)}) collective-permute-start(bf16[128,1024]{1,0:T(8,128)(2,1)S(1)} %get-tuple-element.102.refs_0_), channel_id=1, source_target_pairs={{0,4},{4,0},{8,12},{12,8},{16,20},{20,16},{24,28},{28,24},{1,5},{5... | collective-permute-start | bytes 786440 | tf_op jit(solution)/shard_map/ppermute | solution.py:403
  135.3 13.4 %collective-permute-start.24 = (bf16[128,1024]{1,0:T(8,128)(2,1)S(1)}, bf16[128,1024]{1,0:T(8,128)(2,1)}, u32[]{:S(2)}, u32[]{:S(2)}) collective-permute-start(bf16[128,1024]{1,0:T(8,128)(2,1)S(1)} %collective-permute-done.23.refs_4_), channel_id=1, source_target_pairs={{0,4},{4,0},{8,12},{12,8},{16,20},{20,16},{24,28},{28,24},{1,5},{5... | collective-permute-start | bytes 786440 | tf_op jit(solution)/shard_map/ppermute | solution.py:403
  135.9 18.5 %collective-permute-start.22 = (bf16[128,1024]{1,0:T(8,128)(2,1)S(1)}, bf16[128,1024]{1,0:T(8,128)(2,1)}, u32[]{:S(2)}, u32[]{:S(2)}) collective-permute-start(bf16[128,1024]{1,0:T(8,128)(2,1)S(1)} %collective-permute-done.21.refs_2_), channel_id=1, source_target_pairs={{0,4},{4,0},{8,12},{12,8},{16,20},{20,16},{24,28},{28,24},{1,5},{5... | collective-permute-start | bytes 786440 | tf_op jit(solution)/shard_map/ppermute | solution.py:403
  141.3 17.6 %collective-permute-start.26 = (bf16[128,1024]{1,0:T(8,128)(2,1)}, bf16[128,1024]{1,0:T(8,128)(2,1)}, u32[]{:S(2)}, u32[]{:S(2)}) collective-permute-start(bf16[128,1024]{1,0:T(8,128)(2,1)} %collective-permute-done.25.refs_6_), channel_id=1, source_target_pairs={{0,4},{4,0},{8,12},{12,8},{16,20},{20,16},{24,28},{28,24},{1,5},{5... | collective-permute-start | bytes 786440 | tf_op jit(solution)/shard_map/ppermute | solution.py:403
  142.9 86.5 %collective-permute-start.41 = (bf16[8,128,1024]{2,1,0:T(8,128)(2,1)}, bf16[8,128,1024]{2,1,0:T(8,128)(2,1)S(1)}, u32[]{:S(2)}, u32[]{:S(2)}) collective-permute-start(bf16[8,128,1024]{2,1,0:T(8,128)(2,1)} %bitcast.45), channel_id=1, source_target_pairs={{0,2},{1,3},{2,0},{3,1},{4,6},{5,7},{6,4},{7,5},{8,10},{9,11},{10,... | collective-permute-start | bytes 6291464 | tf_op jit(solution)/shard_map/ppermute | solution.py:1348
  147.2 67.8 %copy-start.19 = (f32[128,1024]{1,0:T(8,128)S(1)}, f32[128,1024]{1,0:T(8,128)}, u32[]{:S(2)}) copy-start(f32[128,1024]{1,0:T(8,128)} %copy-done.18) | copy-start | bytes 1572868
  147.2 67.8 %copy-start.45 = (bf16[128,1024]{1,0:T(8,128)(2,1)S(1)}, bf16[128,1024]{1,0:T(8,128)(2,1)}, u32[]{:S(2)}) copy-start(bf16[128,1024]{1,0:T(8,128)(2,1)} %up_ref.1) | copy-start | bytes 786436
  182.1 9.5 %collective-permute-start.31 = (bf16[128,1024]{1,0:T(8,128)(2,1)}, bf16[128,1024]{1,0:T(8,128)(2,1)S(1)}, u32[]{:S(2)}, u32[]{:S(2)}) collective-permute-start(bf16[128,1024]{1,0:T(8,128)(2,1)} %get-tuple-element.116), channel_id=1, source_target_pairs={{0,4},{4,0},{8,12},{12,8},{16,20},{20,16},{24,28},{28,24},{1,5},{5... | collective-permute-start | bytes 786440 | tf_op jit(solution)/shard_map/ppermute | solution.py:415
  183.7 13.6 %collective-permute-start.28 = (bf16[128,1024]{1,0:T(8,128)(2,1)}, bf16[128,1024]{1,0:T(8,128)(2,1)S(1)}, u32[]{:S(2)}, u32[]{:S(2)}) collective-permute-start(bf16[128,1024]{1,0:T(8,128)(2,1)} %get-tuple-element.112), channel_id=1, source_target_pairs={{0,4},{4,0},{8,12},{12,8},{16,20},{20,16},{24,28},{28,24},{1,5},{5... | collective-permute-start | bytes 786440 | tf_op jit(solution)/shard_map/ppermute | solution.py:415
  184.2 18.7 %collective-permute-start.30 = (bf16[128,1024]{1,0:T(8,128)(2,1)}, bf16[128,1024]{1,0:T(8,128)(2,1)S(1)}, u32[]{:S(2)}, u32[]{:S(2)}) collective-permute-start(bf16[128,1024]{1,0:T(8,128)(2,1)} %get-tuple-element.114), channel_id=1, source_target_pairs={{0,4},{4,0},{8,12},{12,8},{16,20},{20,16},{24,28},{28,24},{1,5},{5... | collective-permute-start | bytes 786440 | tf_op jit(solution)/shard_map/ppermute | solution.py:415
  192.7 10.2 %collective-permute-start.32 = (bf16[128,1024]{1,0:T(8,128)(2,1)S(1)}, bf16[128,1024]{1,0:T(8,128)(2,1)S(1)}, u32[]{:S(2)}, u32[]{:S(2)}) collective-permute-start(bf16[128,1024]{1,0:T(8,128)(2,1)S(1)} %add_convert_fusion.5), channel_id=1, source_target_pairs={{0,8},{4,12},{8,0},{12,4},{16,24},{20,28},{24,16},{28,20},{1,9},{5... | collective-permute-start | bytes 786440 | tf_op jit(solution)/shard_map/ppermute | solution.py:415
  194.5 12.1 %collective-permute-start.27 = (bf16[128,1024]{1,0:T(8,128)(2,1)}, bf16[128,1024]{1,0:T(8,128)(2,1)S(1)}, u32[]{:S(2)}, u32[]{:S(2)}) collective-permute-start(bf16[128,1024]{1,0:T(8,128)(2,1)} %get-tuple-element.110), channel_id=1, source_target_pairs={{0,4},{4,0},{8,12},{12,8},{16,20},{20,16},{24,28},{28,24},{1,5},{5... | collective-permute-start | bytes 786440 | tf_op jit(solution)/shard_map/ppermute | solution.py:415
  198.3 8.2 %collective-permute-start.29 = (bf16[128,1024]{1,0:T(8,128)(2,1)S(1)}, bf16[128,1024]{1,0:T(8,128)(2,1)S(1)}, u32[]{:S(2)}, u32[]{:S(2)}) collective-permute-start(bf16[128,1024]{1,0:T(8,128)(2,1)S(1)} %add_convert_fusion.6), channel_id=1, source_target_pairs={{0,8},{4,12},{8,0},{12,4},{16,24},{20,28},{24,16},{28,20},{1,9},{5... | collective-permute-start | bytes 786440 | tf_op jit(solution)/shard_map/ppermute | solution.py:415
  204.0 11.0 %collective-permute-start.33 = (bf16[128,1024]{1,0:T(8,128)(2,1)S(1)}, bf16[128,1024]{1,0:T(8,128)(2,1)S(1)}, u32[]{:S(2)}, u32[]{:S(2)}) collective-permute-start(bf16[128,1024]{1,0:T(8,128)(2,1)S(1)} %add_convert_fusion.4), channel_id=1, source_target_pairs={{0,16},{4,20},{8,24},{12,28},{16,0},{20,4},{24,8},{28,12},{1,17},{... | collective-permute-start | bytes 786440 | tf_op jit(solution)/shard_map/ppermute | solution.py:415
  217.1 6.4 %collective-permute-start.35 = (bf16[128,1024]{1,0:T(8,128)(2,1)S(1)}, bf16[128,1024]{1,0:T(8,128)(2,1)S(1)}, u32[]{:S(2)}, u32[]{:S(2)}) collective-permute-start(bf16[128,1024]{1,0:T(8,128)(2,1)S(1)} %get-tuple-element.117.refs_0_.refs_5_), channel_id=1, source_target_pairs={{0,2},{1,3},{2,0},{3,1},{4,6},{5,7},{6,4},{7,5},{8,10},{9,11},{10,... | collective-permute-start | bytes 786440 | tf_op jit(solution)/shard_map/ppermute | solution.py:403
  218.6 4.9 %collective-permute-start.34 = (bf16[128,1024]{1,0:T(8,128)(2,1)S(1)}, bf16[128,1024]{1,0:T(8,128)(2,1)S(1)}, u32[]{:S(2)}, u32[]{:S(2)}) collective-permute-start(bf16[128,1024]{1,0:T(8,128)(2,1)S(1)} %get-tuple-element.117.refs_0_.refs_5_), channel_id=1, source_target_pairs={{0,1},{1,0},{2,3},{3,2},{4,5},{5,4},{6,7},{7,6},{8,9},{9,8},{10,11... | collective-permute-start | bytes 786440 | tf_op jit(solution)/shard_map/ppermute | solution.py:403
  223.5 1.5 collective-permute-start.36
  226.2 14.0 %collective-permute-start.37 = (bf16[512,512]{1,0:T(8,128)(2,1)S(1)}, bf16[512,512]{1,0:T(8,128)(2,1)S(1)}, u32[]{:S(2)}, u32[]{:S(2)}) collective-permute-start(bf16[512,512]{1,0:T(8,128)(2,1)S(1)} %get-tuple-element.123), channel_id=1, source_target_pairs={{0,4},{4,0},{8,12},{12,8},{16,20},{20,16},{24,28},{28,24},{1,5},{5... | collective-permute-start | bytes 1572872 | tf_op jit(solution)/shard_map/ppermute | solution.py:1388
  229.4 66.4 %collective-permute-start.42 = (bf16[8,128,1024]{2,1,0:T(8,128)(2,1)S(1)}, bf16[8,128,1024]{2,1,0:T(8,128)(2,1)S(1)}, u32[]{:S(2)}, u32[]{:S(2)}) collective-permute-start(bf16[8,128,1024]{2,1,0:T(8,128)(2,1)S(1)} %shard_map.228), channel_id=1, source_target_pairs={{0,2},{1,3},{2,0},{3,1},{4,6},{5,7},{6,4},{7,5},{8,10},{9,11},{10,... | collective-permute-start | bytes 6291464 | tf_op jit(solution)/shard_map/ppermute | solution.py:1365
  240.4 13.2 %collective-permute-start.38 = (bf16[512,512]{1,0:T(8,128)(2,1)S(1)}, bf16[512,512]{1,0:T(8,128)(2,1)S(1)}, u32[]{:S(2)}, u32[]{:S(2)}) collective-permute-start(bf16[512,512]{1,0:T(8,128)(2,1)S(1)} %add_convert_fusion.2), channel_id=1, source_target_pairs={{0,8},{4,12},{8,0},{12,4},{16,24},{20,28},{24,16},{28,20},{1,9},{5... | collective-permute-start | bytes 1572872 | tf_op jit(solution)/shard_map/ppermute | solution.py:1388
  240.8 14.9 %collective-permute-start.39 = (bf16[512,512]{1,0:T(8,128)(2,1)S(1)}, bf16[512,512]{1,0:T(8,128)(2,1)S(1)}, u32[]{:S(2)}, u32[]{:S(2)}) collective-permute-start(bf16[512,512]{1,0:T(8,128)(2,1)S(1)} %get-tuple-element.127), channel_id=1, source_target_pairs={{0,4},{4,0},{8,12},{12,8},{16,20},{20,16},{24,28},{28,24},{1,5},{5... | collective-permute-start | bytes 1572872 | tf_op jit(solution)/shard_map/ppermute | solution.py:1388
  242.5 26.3 %collective-permute-start.43 = (bf16[512,512]{1,0:T(8,128)(2,1)S(1)}, bf16[512,512]{1,0:T(8,128)(2,1)S(1)}, u32[]{:S(2)}, u32[]{:S(2)}) collective-permute-start(bf16[512,512]{1,0:T(8,128)(2,1)S(1)} %get-tuple-element.136), channel_id=1, source_target_pairs={{0,4},{4,0},{8,12},{12,8},{16,20},{20,16},{24,28},{28,24},{1,5},{5... | collective-permute-start | bytes 1572872 | tf_op jit(solution)/shard_map/ppermute | solution.py:1388
  255.9 32.4 %collective-permute-start.40 = (bf16[512,512]{1,0:T(8,128)(2,1)S(1)}, bf16[512,512]{1,0:T(8,128)(2,1)S(1)}, u32[]{:S(2)}, u32[]{:S(2)}) collective-permute-start(bf16[512,512]{1,0:T(8,128)(2,1)S(1)} %add_convert_fusion.1), channel_id=1, source_target_pairs={{0,16},{4,20},{8,24},{12,28},{16,0},{20,4},{24,8},{28,12},{1,17},{... | collective-permute-start | bytes 1572872 | tf_op jit(solution)/shard_map/ppermute | solution.py:1388
  268.9 20.2 %collective-permute-start.44 = (bf16[512,512]{1,0:T(8,128)(2,1)S(1)}, bf16[512,512]{1,0:T(8,128)(2,1)S(1)}, u32[]{:S(2)}, u32[]{:S(2)}) collective-permute-start(bf16[512,512]{1,0:T(8,128)(2,1)S(1)} %add_convert_fusion), channel_id=1, source_target_pairs={{0,8},{4,12},{8,0},{12,4},{16,24},{20,28},{24,16},{28,20},{1,9},{5... | collective-permute-start | bytes 1572872 | tf_op jit(solution)/shard_map/ppermute | solution.py:1388
  272.4 24.7 %collective-permute-start.45 = (f32[4,2,1024]{2,1,0:T(2,128)S(1)}, f32[4,2,1024]{2,1,0:T(2,128)S(1)}, u32[]{:S(2)}, u32[]{:S(2)}) collective-permute-start(f32[4,2,1024]{2,1,0:T(2,128)S(1)} %copy-done.77), channel_id=1, source_target_pairs={{0,2},{1,3},{2,0},{3,1},{4,6},{5,7},{6,4},{7,5},{8,10},{9,11},{10,... | collective-permute-start | bytes 98312 | tf_op jit(solution)/shard_map/ppermute | solution.py:1365
  273.9 72.0 %collective-permute-start.55 = (bf16[2,320,3584]{2,1,0:T(8,128)(2,1)}, bf16[2,320,3584]{2,1,0:T(8,128)(2,1)}, u32[]{:S(2)}, u32[]{:S(2)}) collective-permute-start(bf16[2,320,3584]{2,1,0:T(8,128)(2,1)} %get-tuple-element.161), channel_id=1, source_target_pairs={{0,1},{1,0},{2,3},{3,2},{4,5},{5,4},{6,7},{7,6},{8,9},{9,8},{10,11... | collective-permute-start | bytes 13762568 | tf_op jit(solution)/shard_map/ppermute | solution.py:1356
  313.0 32.9 %collective-permute-start.56 = (bf16[2,320,3584]{2,1,0:T(8,128)(2,1)}, bf16[2,320,3584]{2,1,0:T(8,128)(2,1)}, u32[]{:S(2)}, u32[]{:S(2)}) collective-permute-start(bf16[2,320,3584]{2,1,0:T(8,128)(2,1)} %get-tuple-element.162), channel_id=1, source_target_pairs={{0,1},{1,0},{2,3},{3,2},{4,5},{5,4},{6,7},{7,6},{8,9},{9,8},{10,11... | collective-permute-start | bytes 13762568 | tf_op jit(solution)/shard_map/ppermute | solution.py:1405
  313.1 23.0 %collective-permute-start.46 = (bf16[512,512]{1,0:T(8,128)(2,1)}, bf16[512,512]{1,0:T(8,128)(2,1)}, u32[]{:S(2)}, u32[]{:S(2)}) collective-permute-start(bf16[512,512]{1,0:T(8,128)(2,1)} %get-tuple-element.147), channel_id=1, source_target_pairs={{0,4},{4,0},{8,12},{12,8},{16,20},{20,16},{24,28},{28,24},{1,5},{5... | collective-permute-start | bytes 1572872 | tf_op jit(solution)/shard_map/ppermute | solution.py:1388
  320.5 55.5 %all-to-all-start = ((bf16[8,128,512]{2,1,0:T(8,128)(2,1)}), bf16[8,128,512]{2,1,0:T(8,128)(2,1)}, u32[]{:S(2)}, u32[]{:S(2)}) async-start(bf16[8,128,512]{2,1,0:T(8,128)(2,1)} %shard_map.234), calls=%async_computation | async-start | bytes 2097152 | tf_op jit(solution)/shard_map/all_to_all | solution.py:1229
  356.9 42.4 %collective-permute-start.57 = (bf16[1,3072,512]{2,1,0:T(8,128)(2,1)}, bf16[1,3072,512]{2,1,0:T(8,128)(2,1)}, u32[]{:S(2)}, u32[]{:S(2)}) collective-permute-start(bf16[1,3072,512]{2,1,0:T(8,128)(2,1)} %get-tuple-element.169), channel_id=1, source_target_pairs={{0,1},{1,0},{2,3},{3,2},{4,5},{5,4},{6,7},{7,6},{8,9},{9,8},{10,11... | collective-permute-start | bytes 9437192 | tf_op jit(solution)/shard_map/ppermute | solution.py:1418
  368.0 36.0 %collective-permute-start.58 = (bf16[1,3072,512]{2,1,0:T(8,128)(2,1)}, bf16[1,3072,512]{2,1,0:T(8,128)(2,1)}, u32[]{:S(2)}, u32[]{:S(2)}) collective-permute-start(bf16[1,3072,512]{2,1,0:T(8,128)(2,1)} %get-tuple-element.173), channel_id=1, source_target_pairs={{0,1},{1,0},{2,3},{3,2},{4,5},{5,4},{6,7},{7,6},{8,9},{9,8},{10,11... | collective-permute-start | bytes 9437192 | tf_op jit(solution)/shard_map/ppermute | solution.py:1418
  368.5 5.9 %collective-permute-start.48 = (bf16[128,1024]{1,0:T(8,128)(2,1)S(1)}, bf16[128,1024]{1,0:T(8,128)(2,1)S(1)}, u32[]{:S(2)}, u32[]{:S(2)}) collective-permute-start(bf16[128,1024]{1,0:T(8,128)(2,1)S(1)} %get-tuple-element.154), channel_id=1, source_target_pairs={{0,1},{1,0},{2,3},{3,2},{4,5},{5,4},{6,7},{7,6},{8,9},{9,8},{10,11... | collective-permute-start | bytes 786440 | tf_op jit(solution)/shard_map/ppermute | solution.py:415
  368.5 13.5 %collective-permute-start.50 = (f32[2,1024]{1,0:T(2,128)S(1)}, f32[2,1024]{1,0:T(2,128)S(1)}, u32[]{:S(2)}, u32[]{:S(2)}) collective-permute-start(f32[2,1024]{1,0:T(2,128)S(1)} %pad_maximum_fusion.1), channel_id=1, source_target_pairs={{0,1},{1,0},{2,3},{3,2},{4,5},{5,4},{6,7},{7,6},{8,9},{9,8},{10,11... | collective-permute-start | bytes 24584 | tf_op jit(solution)/shard_map/ppermute | solution.py:437
  369.1 18.8 %collective-permute-start.47 = (bf16[128,1024]{1,0:T(8,128)(2,1)}, bf16[128,1024]{1,0:T(8,128)(2,1)S(1)}, u32[]{:S(2)}, u32[]{:S(2)}) collective-permute-start(bf16[128,1024]{1,0:T(8,128)(2,1)} %get-tuple-element.152), channel_id=1, source_target_pairs={{0,1},{1,0},{2,3},{3,2},{4,5},{5,4},{6,7},{7,6},{8,9},{9,8},{10,11... | collective-permute-start | bytes 786440 | tf_op jit(solution)/shard_map/ppermute | solution.py:415
  374.5 11.3 %collective-permute-start.49 = (bf16[128,1024]{1,0:T(8,128)(2,1)S(1)}, bf16[128,1024]{1,0:T(8,128)(2,1)S(1)}, u32[]{:S(2)}, u32[]{:S(2)}) collective-permute-start(bf16[128,1024]{1,0:T(8,128)(2,1)S(1)} %add_convert_fusion.3), channel_id=1, source_target_pairs={{0,2},{1,3},{2,0},{3,1},{4,6},{5,7},{6,4},{7,5},{8,10},{9,11},{10,... | collective-permute-start | bytes 786440 | tf_op jit(solution)/shard_map/ppermute | solution.py:415
  376.0 22.5 %all-to-all-start.1 = ((bf16[8,128,256]{2,1,0:T(8,128)(2,1)}), bf16[8,128,256]{2,1,0:T(8,128)(2,1)S(1)}, u32[]{:S(2)}, u32[]{:S(2)}) async-start(bf16[8,128,256]{2,1,0:T(8,128)(2,1)} %get-tuple-element.158), calls=%async_computation.1 | async-start | bytes 1048576 | tf_op jit(solution)/shard_map/all_to_all | solution.py:1229
  382.0 3.7 collective-permute-start.51
  385.8 3.8 collective-permute-start.52
  389.6 3.8 collective-permute-start.53
  393.3 4.5 %collective-permute-start.54 = (f32[2,1024]{1,0:T(2,128)S(1)}, f32[2,1024]{1,0:T(2,128)S(1)}, u32[]{:S(2)}, u32[]{:S(2)}) collective-permute-start(f32[2,1024]{1,0:T(2,128)S(1)} %add.199), channel_id=1, source_target_pairs={{0,16},{4,20},{8,24},{12,28},{16,0},{20,4},{24,8},{28,12},{1,17},{... | collective-permute-start | bytes 24584 | tf_op jit(solution)/shard_map/ppermute | solution.py:437
  (82 other events, 1185.7 us)
Sparse Core Ops, SparseCore 0:
  76.7 55.8 all-gather.2

commit v2 on v1

--- a/solution.py
+++ b/solution.py
@@ -16,6 +16,7 @@
 masked = -1e30
 vmem_bytes = 56 * 2**20
 vmem_small = 20 * 2**20
+pace = 1.15e9
 
 
 def passed_along(value, axis, steps):
@@ -465,11 +466,9 @@
     return value.astype(jnp.float32)
 
 
-def call(body, outs, operands, scalars, flops, scratch=(), grid=None, in_specs=None,
-         out_specs=None, transcendentals=0, aliases=None):
+def call(body, outs, operands, scalars, micros, scratch=(), grid=None, in_specs=None,
+         out_specs=None, aliases=None):
     memory = vmem_small if grid is None else vmem_bytes
-    size = sum(x.size * x.dtype.itemsize for x in operands)
-    size += sum(x.size * x.dtype.itemsize for x in outs)
     if grid is None:
         in_specs = [pl.BlockSpec(memory_space=pltpu.SMEM)] * len(scalars)
         in_specs += [pl.BlockSpec(memory_space=pltpu.VMEM)] * len(operands)
@@ -494,7 +493,7 @@
         input_output_aliases=aliases or {},
         compiler_params=pltpu.CompilerParams(vmem_limit_bytes=memory),
         cost_estimate=pl.CostEstimate(
-            flops=int(flops // 256), bytes_accessed=int(size // 256), transcendentals=0
+            flops=int(micros * pace), bytes_accessed=0, transcendentals=0
         ),
         **layout,
     )(*scalars, *operands)
@@ -520,7 +519,7 @@
             out_ref[:, column(r, me_ref[0], chunk)] = normed[:, r * chunk : (r + 1) * chunk]
 
     return call(
-        body, [shape((rows, width), jnp.bfloat16)], [layer_input, gain], [me], 4 * rows * width
+        body, [shape((rows, width), jnp.bfloat16)], [layer_input, gain], [me], 2
     )[0]
 
 
@@ -577,7 +576,7 @@
         ],
         [*x_chunks, *w_chunks, cosine, sine],
         [],
-        2 * tokens * width * cols,
+        2,
     )
 
 
@@ -638,8 +637,7 @@
         [shape((kv_rows + 8, all_rows), jnp.float32)],
         operands if first else [state, *operands],
         [offset],
-        4 * all_rows * tokens * n * kv_rows,
-        transcendentals=all_rows * tokens * n,
+        3 * n,
         aliases=None if first else {1: 0},
     )
 
@@ -672,7 +670,7 @@
     outs = [shape((local_q * HEAD_SIZE, tokens), f32), shape((1, all_rows), f32)]
     outs += [shape((tokens // pieces, width), jnp.bfloat16)] * pieces
     return call(
-        body, outs, [state, *out_chunks], [], 2 * tokens * width * local_q * HEAD_SIZE
+        body, outs, [state, *out_chunks], [], 2
     )
 
 
@@ -696,7 +694,7 @@
         [shape((rows, width), jnp.float32), shape((rows, width), jnp.bfloat16)],
         [layer_input, gain, *branch_parts],
         [me],
-        6 * rows * width,
+        1,
     )
 
 
@@ -724,7 +722,7 @@
         [shape((pieces, 2, count * tokens), jnp.float32)],
         list(payloads),
         [chosen],
-        count * rows * tokens,
+        1,
         scratch=[pltpu.VMEM((count * rows, tokens), jnp.float32)],
     )[0]
 
@@ -737,11 +735,12 @@
             refs[count][k] = refs[k][...]
 
     outs = [shape((count,) + chunks[0].shape, chunks[0].dtype)]
-    return call(body, outs, list(chunks), [], chunks[0].size)[0]
+    return call(body, outs, list(chunks), [], 2)[0]
 
 
 def experts(selected, norms, gathered, tables, gate_w, up_w, down_w, most, pieces, whole):
-    rows, width = gathered.shape[1:]
+    rows, width = gathered[0].shape[1], gate_w.shape[1]
+    parts = len(gathered)
     count = selected.shape[0] - 1 - pieces
     half = pieces // 2
     nn = len(norms)
@@ -752,14 +751,14 @@
     slots = count * most
 
     def body(sel_ref, *refs):
-        n_refs, u_refs = refs[:nn], refs[nn : nn + count]
-        refs = refs[nn + count :]
+        n_refs, u_refs = refs[:nn], refs[nn : nn + parts * count]
+        refs = refs[nn + parts * count :]
         table_ref, g_ref, up_ref, d_ref = refs[:4]
         rest = refs[4:]
         keep_ref, send_ref, rest = *rest[:2], rest[2:]
         if whole:
-            mix_refs, dx_refs = rest[:count], rest[count : 2 * count]
-            xs, gs, ys, ds = rest[2 * count :]
+            mix_refs, dx_refs = rest[:2], rest[2 : 2 + count]
+            xs, gs, ys, ds = rest[2 + count :]
         else:
             xs, gs = rest
         p = pl.program_id(0)
@@ -772,6 +771,9 @@
         def weighted(q, picks):
             at = slice(q * pair, (q + 1) * pair)
             return [jnp.where(c, table_ref[k, 1:2, at], 0.0) for k, c in enumerate(picks)]
+
+        def grad_rows(r):
+            return jnp.concatenate([u_refs[k * count + r][0] for k in range(parts)], axis=1)
 
         def norm_pair(q):
             if nn == 1:
@@ -789,9 +791,7 @@
                 here = dot_nn(pick, norm_pair(q))
                 grads = dot_nn(
                     pick,
-                    jnp.concatenate(
-                        [u_refs[2 * q][0], u_refs[2 * q + 1][0]], axis=0
-                    ),
+                    jnp.concatenate([grad_rows(2 * q), grad_rows(2 * q + 1)], axis=0),
                 )
                 grads = grads * factor
                 for k in range(pieces):
@@ -835,7 +835,7 @@
                     back = low(dot_tn(low(pick), grads))
                     for s in range(2):
                         part = slice(s * rows, (s + 1) * rows)
-                        mix_refs[2 * q + s][...] = mixed[part]
+                        mix_refs[s][q] = mixed[part]
                         dx_refs[2 * q + s][...] = back[part]
 
     def weight_block(a, b):
@@ -853,19 +853,20 @@
         pl.BlockSpec((1,) + fields, lambda p, sel: (jnp.maximum(p - half, 0), 0, 0)),
     ]
     if whole:
-        outs += [shape((rows, width), bf)] * (2 * count)
-        out_specs += [fixed((rows, width))] * (2 * count)
+        outs += [shape((pairs, rows, width), bf)] * 2 + [shape((rows, width), bf)] * count
+        out_specs += [fixed((pairs, rows, width))] * 2 + [fixed((rows, width))] * count
         scratch += [pltpu.VMEM((pieces, slots, width), bf)] * 2
     blocks = [
-        pl.BlockSpec((1,) + gathered.shape[1:], lambda p, sel, r=r: (sel[r], 0, 0))
+        pl.BlockSpec((1,) + part.shape[1:], lambda p, sel, r=r: (sel[r], 0, 0))
+        for part in gathered
         for r in range(count)
     ]
     return call(
         body,
         outs,
-        [*norms, *([gathered] * count), tables, gate_w, up_w, down_w],
+        [*norms, *[part for part in gathered for _ in range(count)], tables, gate_w, up_w, down_w],
         [selected],
-        pieces * slots * width * ff * 2 * (6 if whole else 3),
+        23 if whole else 8,
         scratch=scratch,
         grid=(pieces,),
         in_specs=[fixed(n.shape) for n in norms]
@@ -876,76 +877,86 @@
     )
 
 
-def expert_weight_grads(places, groups, totals, pieces_dev, ff):
+def expert_weight_grads(places, pieces, groups, totals, pieces_dev, ff, rounded):
     n = len(groups)
     _, slots, cols = groups[0].shape
     width = (cols - 3 * ff) // 2
-    edges = [0, width, 2 * width, 2 * width + ff, 2 * width + 2 * ff, cols]
+    tiles = width // ff
     given = len(totals)
 
     def body(places_ref, *refs):
-        refs = refs[given:]
-        fields = [
-            jnp.concatenate([r[0, :, edges[f] : edges[f + 1]] for r in refs[:n]], axis=0)
-            for f in range(5)
+        before, refs = refs[:given], refs[given:]
+        x, produced_grad, hidden, gate_low, upper_low = [
+            jnp.concatenate([refs[5 * g + f][0] for g in range(n)], axis=0) for f in range(5)
         ]
-        wide_refs, low_ref = refs[n : n + 3], refs[n + 3]
-        x, produced_grad, hidden, gate_low, upper_low = fields
+        outs = refs[5 * n :]
         for k, (left, right) in enumerate(
             [(x, gate_low), (x, upper_low), (hidden, produced_grad)]
         ):
             total = dot_tn(left, right)
-            wide_refs[k][0] = total
-            store_packed(low_ref, k, low(total), ff)
-
+            if given:
+                total = total + before[k][0]
+            outs[k][0] = total
+            if rounded:
+                outs[3][0, k, 0] = low(total)
+
+    def field(block):
+        return pl.BlockSpec((1, slots, ff), lambda p, j, at: (at[1] + p, 0, block(j)))
+
+    in_specs = [
+        field(lambda j: j),
+        field(lambda j: tiles + j),
+        field(lambda j: 2 * tiles),
+        field(lambda j: 2 * tiles + 1),
+        field(lambda j: 2 * tiles + 2),
+    ] * n
+    blocks = [
+        pl.BlockSpec((1, ff, ff), lambda p, j, at: (at[0] + p, j, 0)),
+        pl.BlockSpec((1, ff, ff), lambda p, j, at: (at[0] + p, j, 0)),
+        pl.BlockSpec((1, ff, ff), lambda p, j, at: (at[0] + p, 0, j)),
+    ]
     dims = [(width, ff), (width, ff), (ff, width)]
+    outs = [shape((pieces_dev,) + d, jnp.float32) for d in dims]
+    out_specs = list(blocks)
+    if rounded:
+        outs.append(shape((pieces, 3, tiles, ff, ff), jnp.bfloat16))
+        out_specs.append(pl.BlockSpec((1, 3, 1, ff, ff), lambda p, j, at: (p, 0, j, 0, 0)))
     return call(
         body,
-        [shape((pieces_dev,) + d, jnp.float32) for d in dims]
-        + [shape((1, 3 * width, ff), jnp.bfloat16)],
-        [*totals, *groups],
+        outs,
+        [*totals, *[group for group in groups for _ in range(5)]],
         [places],
-        6 * n * slots * width * ff,
-        grid=(1,),
-        in_specs=[pl.BlockSpec(memory_space=pl.ANY)] * given
-        + [pl.BlockSpec((1, slots, cols), lambda p, at: (at[1], 0, 0))] * n,
-        out_specs=[pl.BlockSpec((1,) + d, lambda p, at: (at[0], 0, 0)) for d in dims]
-        + [pl.BlockSpec((1, 3 * width, ff), lambda p, at: (0, 0, 0))],
+        pieces,
+        grid=(pieces, tiles),
+        in_specs=blocks[:given] + in_specs,
+        out_specs=out_specs,
         aliases={1 + k: k for k in range(given)},
     )
 
 
-def store_packed(ref, k, value, ff):
-    rows, cols = value.shape
-    start = k * rows * cols // ff
-    for cut in range(cols // ff):
-        at = slice(start + cut * rows, start + (cut + 1) * rows)
-        ref[0, at, :] = value[:, cut * ff : (cut + 1) * ff]
-
-
-def fill_piece(place, totals, received):
+def fill_pieces(place, totals, received):
     n = len(totals)
-    ff = received.shape[2]
+    pieces, _, tiles, ff, _ = received.shape
 
     def body(place_ref, *refs):
         packed, outs = refs[n], refs[n + 1 :]
-        start = 0
-        for out in outs:
-            _, rows, cols = out.shape
-            for cut in range(cols // ff):
-                out[0, :, cut * ff : (cut + 1) * ff] = wide(packed[0, start : start + rows, :])
-                start += rows
+        for k, out in enumerate(outs):
+            out[0] = wide(packed[0, k, 0])
 
     return call(
         body,
         [shape(t.shape, t.dtype) for t in totals],
         [*totals, received],
         [place],
-        received.size,
-        grid=(1,),
+        4 * pieces,
+        grid=(pieces, tiles),
         in_specs=[pl.BlockSpec(memory_space=pl.ANY)] * n
-        + [pl.BlockSpec(received.shape, lambda p, at: (0, 0, 0))],
-        out_specs=[pl.BlockSpec((1,) + t.shape[1:], lambda p, at: (at[0], 0, 0)) for t in totals],
+        + [pl.BlockSpec((1, 3, 1, ff, ff), lambda p, j, at: (p, 0, j, 0, 0))],
+        out_specs=[
+            pl.BlockSpec((1, ff, ff), lambda p, j, at: (at[0] + p, j, 0)),
+            pl.BlockSpec((1, ff, ff), lambda p, j, at: (at[0] + p, j, 0)),
+            pl.BlockSpec((1, ff, ff), lambda p, j, at: (at[0] + p, 0, j)),
+        ],
         aliases={1 + k: k for k in range(n)},
     )
 
@@ -980,7 +991,7 @@
         ],
         [middle, gain, upstream, *parts],
         [me],
-        12 * rows * width,
+        2,
     )
 
 
@@ -1018,25 +1029,21 @@
         ],
         [queries, attended, *branch_chunks, *out_chunks],
         [],
-        2 * tokens * width * local_q * HEAD_SIZE,
-    )
-
-
-def attention_backward_part(offset, total, queries, kv_chunks, extras, numbers, key_pos, query_pos,
-                            lse, started, local_q, rotation_table=()):
+        1,
+    )
+
+
+def attention_backward_part(offset, total, queries, kv_chunks, numbers, key_pos, query_pos, lse,
+                            started, local_q, rotation_table=()):
     kv_rows, all_rows = queries.shape
     tokens = all_rows // local_q
     group = local_q // (kv_rows // HEAD_SIZE)
     n = len(kv_chunks)
     first, final = total is None, len(rotation_table) > 0
-    extra_rows, width = extras[0].shape
-    cuts = width // tokens
-    kv_end = 2 * kv_rows
 
     def body(off_ref, *refs):
         if not first:
             before_ref, refs = refs[0], refs[1:]
-        extra_refs, refs = refs[:n], refs[n:]
         q_ref, kv_refs = refs[0], refs[1 : 1 + n]
         kpos_ref, qpos_ref, lse_ref = refs[1 + n : 4 + n]
         qn_ref, dot_ref, don_ref, delta_ref = refs[4 + n : 8 + n]
@@ -1074,11 +1081,7 @@
 
                 lax.fori_loop(0, local_q, head, 0)
                 kv_outs[index][:kv_rows, :] = low(dk_ref[...].T)
-                kv_outs[index][kv_rows:kv_end, :] = low(dv_ref[...].T)
-
-            for cut in range(cuts):
-                at = slice(kv_end + cut * extra_rows, kv_end + (cut + 1) * extra_rows)
-                kv_outs[index][at, :] = extra_refs[index][:, cut * tokens : (cut + 1) * tokens]
+                kv_outs[index][kv_rows:, :] = low(dv_ref[...].T)
 
             if r == 0:
                 block()
@@ -1088,7 +1091,7 @@
 
                 @pl.when(jnp.logical_not(live))
                 def _(index=index):
-                    kv_outs[index][:kv_end, :] = jnp.zeros((kv_end, tokens), jnp.bfloat16)
+                    kv_outs[index][...] = jnp.zeros_like(kv_outs[index])
 
         if not final:
             return
@@ -1100,32 +1103,30 @@
             dq_out[h * HEAD_SIZE : (h + 1) * HEAD_SIZE, :] = low(rope_rows(part, cosine, sine))
 
     bf, f32 = jnp.bfloat16, jnp.float32
-    operands = [*extras, queries, *kv_chunks, key_pos, query_pos, lse, *started, *rotation_table]
+    operands = [queries, *kv_chunks, key_pos, query_pos, lse, *started, *rotation_table]
     operands = operands if first else [total, *operands]
     outs = [shape((local_q * HEAD_SIZE, tokens), bf) if final else shape((kv_rows, all_rows), f32)]
     scratch = [pltpu.VMEM((kv_rows, all_rows), f32)] if final else []
     scratch += [pltpu.VMEM((tokens, kv_rows), f32)] * 2
     return call(
         body,
-        outs + [shape((kv_end + cuts * extra_rows, tokens), bf)] * n,
+        outs + [shape((2 * kv_rows, tokens), bf)] * n,
         operands,
         [offset],
-        10 * all_rows * tokens * n * kv_rows,
+        n,
         scratch=scratch,
-        transcendentals=all_rows * tokens * n,
         aliases={1: 0} if not first and not final else None,
     )
 
 
-def row_grads(me, pairs, count):
-    tokens = pairs[0][1].shape[1]
+def row_grads(pairs, count):
     width = pairs[0][0][0].shape[1]
     cols = sum(columns.shape[0] for _, columns in pairs)
     chunk = width // count
     counts = [len(x_chunks) + 1 for x_chunks, _ in pairs]
 
-    def body(me_ref, *refs):
-        out_ref, refs, left = refs[-1], list(refs[:-1]), 0
+    def body(*refs):
+        out_refs, refs, left = refs[-2:], list(refs[:-2]), 0
         for n in counts:
             mine, refs = refs[:n], refs[n:]
             x = jnp.concatenate([r[...] for r in mine[:-1]], axis=0)
@@ -1133,45 +1134,33 @@
             right = left + total.shape[1]
             for r in range(count):
                 part = total[r * chunk : (r + 1) * chunk]
-                out_ref[pl.ds(r ^ me_ref[0], 1), :, left:right] = part[None]
+                out_refs[r % 2][r // 2, :, left:right] = part
             left = right
 
     operands = [x for x_chunks, columns in pairs for x in (*x_chunks, columns)]
-    outs = [shape((count, chunk, cols), jnp.bfloat16)]
-    return call(body, outs, operands, [me], 2 * tokens * width * cols)[0]
-
-
-def input_parts(me, kv_parts, middle, query_grad, x_chunks, w_chunks, cosine, sine, gain, local_kv, count):
+    outs = [shape((count // 2, chunk, cols), jnp.bfloat16)] * 2
+    return call(body, outs, operands, [], 2)
+
+
+def input_parts(me, kv_parts, query_grad, x_chunks, w_chunks, cosine, sine, gain, local_kv, count):
     w_chunks, w_cols = w_chunks
     n, nx, nw = len(kv_parts), len(x_chunks), len(w_chunks)
     rows, width = x_chunks[0].shape
-    tokens = query_grad.shape[1]
     kv_rows = local_kv * HEAD_SIZE
     chunk = width // count
 
-    def body(*refs):
-        me_ref = refs[0]
-        parts = refs[1 : 1 + n]
-        middle_ref = refs[1 + n]
-        refs = refs[1:]
-        dq_ref = refs[1 + n]
-        x_refs = refs[2 + n : 2 + n + nx]
-        w_refs = refs[2 + n + nx : 2 + n + nx + nw]
-        cos_ref, sin_ref, gain_ref = refs[2 + n + nx + nw : 5 + n + nx + nw]
-        outs = refs[5 + n + nx + nw :]
-        in_refs, grad_ref, sum_ref, out_ref = outs[:nx], *outs[nx:]
+    def body(me_ref, *refs):
+        parts, dq_ref, refs = refs[:n], refs[n], refs[n + 1 :]
+        x_refs, w_refs, refs = refs[:nx], refs[nx : nx + nw], refs[nx + nw :]
+        cos_ref, sin_ref, gain_ref, refs = *refs[:3], refs[3:]
+        in_refs, even_ref, odd_ref, sum_ref = refs[:nx], *refs[nx:]
         total = sum_parts([p[...] for p in parts])
         cosine, sine = cos_ref[...], -sin_ref[...]
         blocks = [
             low(rope_rows(total[h * HEAD_SIZE : (h + 1) * HEAD_SIZE], cosine, sine))
             for h in range(local_kv)
         ]
-        for cut in range(width // tokens):
-            at = slice(cut * tokens, (cut + 1) * tokens)
-            mixed = total[2 * kv_rows + cut * rows : 2 * kv_rows + (cut + 1) * rows]
-            out_ref[:, at] = low(middle_ref[:, at] + mixed)
-        values = low(total[kv_rows : 2 * kv_rows])
-        columns = jnp.concatenate([dq_ref[...], *blocks, values], axis=0).T
+        columns = jnp.concatenate([dq_ref[...], *blocks, low(total[kv_rows:])], axis=0).T
         weight = jnp.concatenate([w[:, w_cols] for w in w_refs], axis=0)
         sums = jnp.zeros((1, width), jnp.float32)
         for m in range(nx):
@@ -1182,18 +1171,18 @@
             at = column(r, me_ref[0], chunk)
             sum_ref[:, at] = sums[:, r * chunk : (r + 1) * chunk] / gain_ref[:, at]
         x = jnp.concatenate([x[...] for x in x_refs], axis=0)
-        grads = dot_tn(x, columns[:, -2 * kv_rows :])
+        grads = low(dot_tn(x, columns[:, -2 * kv_rows :]))
         for r in range(count):
-            grad_ref[pl.ds(r ^ me_ref[0], 1)] = low(grads[r * chunk : (r + 1) * chunk])[None]
+            (even_ref, odd_ref)[r % 2][r // 2] = grads[r * chunk : (r + 1) * chunk]
 
     return call(
         body,
         [shape((rows, width), jnp.bfloat16)] * nx
-        + [shape((count, chunk, 2 * kv_rows), jnp.bfloat16)]
-        + [shape((1, width), jnp.float32), shape((rows, width), jnp.bfloat16)],
-        [*kv_parts, middle, query_grad, *x_chunks, *w_chunks, cosine, sine, gain],
+        + [shape((count // 2, chunk, 2 * kv_rows), jnp.bfloat16)] * 2
+        + [shape((1, width), jnp.float32)],
+        [*kv_parts, query_grad, *x_chunks, *w_chunks, cosine, sine, gain],
         [me],
-        4 * tokens * width * w_chunks[0].shape[1],
+        1,
     )
 
 
@@ -1221,13 +1210,8 @@
         [shape((rows, width), jnp.float32)],
         [layer_input, gain, middle_grad, *parts],
         [me],
-        10 * rows * width,
+        1,
     )[0]
-
-
-def exchange_sum(chunks):
-    received = lax.all_to_all(chunks, "dp", split_axis=0, concat_axis=0, tiled=True)
-    return jnp.sum(received.astype(jnp.float32), axis=0)
 
 
 def after(value, *others):
@@ -1337,7 +1321,7 @@
         kv_chunks[r] = lax.ppermute(source, "dp", [(i, i ^ near) for i in range(devices)])
     for numbers in forward_order[len(done) :]:
         state = attend(numbers, state)
-    gathered = lax.all_gather(after(upstream, kv_chunks[-1]), "dp", axis=0, tiled=False)
+    gathered = lax.all_gather(after(upstream, kv_chunks[devices // 2]), "dp", axis=0, tiled=False)
     attended, lse, *branch_chunks = attention_end(state, out_chunks, local_q, kv_own.shape[0] // 2, groups)
 
     middle, second_norm = middle_rows(
@@ -1345,13 +1329,14 @@
     )
     norm_chunks = xor_gather(second_norm, "dp")
     far_pairs = [[(i, i ^ g) for i in range(groups)] for g in range(2, groups, 2)]
-    gathered_far = [lax.ppermute(after(gathered, second_norm), "mp", pairs) for pairs in far_pairs]
+    near_columns, later_columns = jnp.split(after(gathered, second_norm), 2, axis=2)
+    columns_far = [lax.ppermute(near_columns, "mp", pairs) for pairs in far_pairs]
     expert_weights = (gate_weight, up_weight, down_weight)
     own = experts(
-        selected, norm_chunks, gathered, tables,
+        selected, norm_chunks, [gathered], tables,
         *expert_weights, most, pieces_dev, True,
     )
-    mixture_chunks, back_chunks = own[2 : 2 + devices], own[2 + devices :]
+    mixture, mixture_odd, back_chunks = own[2], own[3], own[4:]
     swap = [(i, i ^ 1) for i in range(groups)]
     fields = [own[0], lax.ppermute(own[1], "mp", swap)]
     back_parts = xor_scatter(back_chunks, "dp")
@@ -1360,82 +1345,130 @@
     )
 
     branch_rows = xor_gather(branch_low, "mp")
-    norm_here = after(stacked(norm_chunks), branch_rows[-1], *gathered_far)
+    norm_here = after(stacked(norm_chunks), branch_rows[-1], *columns_far)
+    later_columns = after(later_columns, branch_rows[-1], *columns_far)
     far_groups = [
-        (rows_far, *[lax.ppermute(v, "mp", pairs) for v in (norm_here, tables)])
-        for rows_far, pairs in zip(gathered_far, far_pairs)
+        ([first, lax.ppermute(later_columns, "mp", pairs)],
+         *[lax.ppermute(v, "mp", pairs) for v in (norm_here, tables)])
+        for first, pairs in zip(columns_far, far_pairs)
     ]
-    started = attention_backward_start(queries, attended, branch_rows, out_chunks, local_q)
-    backward = sorted(range(devices), key=lambda r: (-bin(r).count("1"), -r))
-    backward_order = [tuple(backward[i : i + 2]) for i in range(0, devices - 2, 2)]
-    backward_order += [(r,) for r in backward[-2:]]
-    total, pending, arrived = None, [[] for _ in range(devices)], []
-    for numbers in backward_order:
+    def halved(odd, even, bit):
+        came = lax.ppermute(odd, "dp", [(i, i ^ bit) for i in range(devices)])
+        return (wide(even) + wide(came)).astype(jnp.bfloat16)
+
+    def halving(chunks):
+        sums, bit = [halved(chunks[1], chunks[0], 1)], 2
+        while bit < devices:
+            sums.append(halved(sums[-1][1::2], sums[-1][0::2], bit))
+            bit *= 2
+        return sums
+
+    mixture = halved(after(mixture_odd, branch_low), mixture, 1)
+    started = attention_backward_start(
+        queries, attended, [after(branch_rows[0], mixture), *branch_rows[1:]], out_chunks, local_q
+    )
+    odd = list(range(devices - 1, 0, -2))
+    even = sorted(range(0, devices, 2), key=lambda r: (-bin(r).count("1"), -r))
+    backward_order = [tuple(part[i : i + 2]) for part in (odd, even) for i in range(0, len(part), 2)]
+    total, pending, waiting = None, [[] for _ in range(devices)], set(range(1, devices))
+    computed, arrivals, bit = set(), [], 2
+    for step, numbers in enumerate(backward_order):
         last = numbers is backward_order[-1]
-        if len(arrived) > 1 and arrived[-2]:
-            total = after(total, *arrived[-2])
+        if step > 1:
+            total = after(total, arrivals[step - 2])
+            if bit < devices:
+                mixture = halved(mixture[1::2], mixture[0::2], bit)
+                total = after(total, mixture)
+                bit *= 2
         total, *parts = attention_backward_part(
-            offset, total, queries, [kv_chunks[r] for r in numbers],
-            [mixture_chunks[r] for r in numbers], numbers, key_pos, query_pos, lse, started, local_q,
-            (cosine, sine) if last else (),
+            offset, total, queries, [kv_chunks[r] for r in numbers], numbers, key_pos, query_pos,
+            lse, started, local_q, (cosine, sine) if last else (),
         )
         for r, part in zip(numbers, parts):
-            pending[r].append(part)
-        arrived.append([])
-        for r in numbers:
+            pending[r].insert(0, part)
+            computed.add(r)
+        for r in sorted(waiting, key=lambda r: (r % 2 == 0, -r)):
             near = r & -r
-            if r:
+            feeders = [r | bit for bit in range(1, near) if bin(bit).count("1") == 1]
+            if r in computed and not waiting.intersection(feeders):
+                waiting.remove(r)
                 came = lax.ppermute(
                     add_parts(pending[r]), "dp", [(i, i ^ near) for i in range(devices)]
                 )
                 pending[r ^ near].append(came)
-                arrived[-1].append(came)
+                arrivals.append(came)
     query_plain, kv_parts = total, pending[0]
-    rows_grad = exchange_sum(
-        row_grads(me, [(x_chunks, query_plain), (branch_rows, attended)], devices)
-    )
-    query_cols = local_q * HEAD_SIZE
-    query_grad, out_grad = rows_grad[:, :query_cols], rows_grad[:, query_cols:]
-
+    while bit < devices:
+        mixture = halved(mixture[1::2], mixture[0::2], bit)
+        bit *= 2
+    layer_output = (middle + wide(mixture[0])).astype(jnp.bfloat16)
+    row_weights = row_grads([(x_chunks, query_plain), (branch_rows, attended)], devices)
+    row_sums = halving(row_weights)
+    places = jnp.stack([first_piece, jnp.int32(0)])
+    fields[0] = after(fields[0], row_weights[0])
+    totals = expert_weight_grads(places, halves, fields, [], pieces_dev, FF // split, False)
+    kv_parts[0] = after(kv_parts[0], totals[0], row_sums[0])
+    outs = input_parts(
+        me, kv_parts, query_plain, x_chunks, qkv_chunks, cosine, sine, gain_one, local_kv, devices
+    )
+    in_chunks, kv_weights, first_sum = outs[:groups], outs[groups : groups + 2], outs[-1]
+    kv_sums = halving(kv_weights)
+    in_parts, hops = [in_chunks[0]], []
+    pending = [[chunk] for chunk in in_chunks]
+    for r in sorted(range(1, groups), key=lambda r: (-bin(r).count("1"), r & -r)):
+        near = r & -r
+        came = lax.ppermute(add_parts(pending[r]), "mp", [(i, i ^ near) for i in range(groups)])
+        pending[r ^ near].append(came)
+        hops.append(came)
+    in_parts = pending[0]
+    gains = jnp.concatenate([first_sum, second_sum], axis=0)
+
+    def gain_hop(gains, axis, bit):
+        count = lax.axis_size(axis)
+        return gains + lax.ppermute(gains, axis, [(i, i ^ bit) for i in range(count)])
+
+    steps = [(axis, 1 << i) for axis in ("mp", "dp") for i in range(8) if 1 << i < lax.axis_size(axis)]
+    far_fields = []
     for rows_far, norm_far, tables_far in far_groups:
         kept, sent = experts(
-            selected, [after(norm_far, query_plain)], rows_far, tables_far, *expert_weights,
-            most, pieces_dev, False,
+            selected, [after(norm_far, first_sum)], rows_far, tables_far,
+            *expert_weights, most, pieces_dev, False,
         )
-        fields += [kept, lax.ppermute(sent, "mp", swap)]
-        kv_parts[0] = after(kv_parts[0], kept)
-    outs = input_parts(
-        me, kv_parts, middle, query_plain, x_chunks, qkv_chunks, cosine, sine, gain_one, local_kv,
-        devices,
-    )
-    in_chunks, (kv_weights, first_sum, layer_output) = outs[:groups], outs[groups:]
-    fields[0] = after(fields[0], first_sum)
-    totals, received = [], []
+        gains = gain_hop(gains, *steps.pop(0))
+        far_fields += [kept, lax.ppermute(sent, "mp", swap)]
+    received = []
     for i in range(halves):
+        gains = gain_hop(gains, *steps.pop(0))
         places = jnp.stack([first_piece + i, jnp.int32(i)])
-        grads = expert_weight_grads(places, fields, totals, pieces_dev, FF // split)
-        totals = grads[:3]
-        received.append(lax.ppermute(grads[3], "mp", swap))
+        hold = [hops[0], row_sums[1], kv_sums[0]] if i == 0 else [hops[-1], row_sums[-1], kv_sums[1]]
+        far_fields[0] = after(far_fields[0], *hold, gains)
+        *totals, sent = expert_weight_grads(
+            places, 1, far_fields, totals, pieces_dev, FF // split, True
+        )
+        received.append(lax.ppermute(sent, "mp", swap))
+    input_grad = input_backward(me, in_parts, layer_input, gain_one, middle_grad, devices)
+    gains = gain_hop(after(gains, input_grad), *steps.pop(0))
+    received[0] = after(received[0], kv_sums[-1])
     for i in range(halves):
         place = jnp.full((1,), halves - first_piece + i, jnp.int32)
-        totals = fill_piece(place, totals, received[i])
+        totals = fill_pieces(place, totals, received[i])
+        if steps:
+            gains = gain_hop(after(gains, totals[0]), *steps.pop(0))
+    for step in steps:
+        gains = gain_hop(gains, *step)
     gate_grad, up_grad, down_grad = totals
-    in_parts = xor_scatter(in_chunks, "mp")
-    kv_grad = exchange_sum(kv_weights)
-    kv_cols = local_kv * HEAD_SIZE
-    input_grad = input_backward(me, in_parts, layer_input, gain_one, middle_grad, devices)
-    gains = butterfly_sum(jnp.concatenate([first_sum, second_sum], axis=0), "mp")
-    gains = butterfly_sum(after(gains, in_parts[-1]), "dp")
+    row_weight_grad, kv_grad = wide(row_sums[-1][0]), wide(kv_sums[-1][0])
+    query_cols, kv_cols = local_q * HEAD_SIZE, local_kv * HEAD_SIZE
     first_gain_grad, second_gain_grad = gains[0], gains[1]
     return (
         layer_output,
         input_grad,
         first_gain_grad,
         second_gain_grad,
-        query_grad,
+        row_weight_grad[:, :query_cols],
         kv_grad[:, :kv_cols],
         kv_grad[:, kv_cols:],
-        out_grad,
+        row_weight_grad[:, query_cols:],
         gate_grad,
         up_grad,
         down_grad,

time: 423 us -> 405 us (0.957)
  waiting for transfers between devices: 158 us -> 133 us
  Pallas kernels: 96.4 us -> 106 us
  local copies, waits for them, and re-layouts: 31.1 us -> 24.4 us
    ppermute x7, waiting for transfers between devices: 34.4 us -> 1.1 us  [layer_shards(): lax.ppermute(add_parts(pending[r]), 'dp', [(i, i ^ near) for i in range(d...]
    ppermute x9 -> x22, waiting for transfers between devices: 5.02 us -> 38.2 us  [the longest x9 30.4 us: halved(): came = lax.ppermute(odd, 'dp', [(i, i ^ bit) for i in range(devices)])]
    all_to_all x2 -> x0, starting transfers between devices: 20.5 us -> none  [exchange_sum(): lax.all_to_all(chunks, 'dp', split_axis=0, concat_axis=0, tiled=True)]
    ppermute x9 -> x22, starting transfers between devices: 10.2 us -> 29.4 us  [the longest x9 25.1 us: halved(): came = lax.ppermute(odd, 'dp', [(i, i ^ bit) for i in range(devices)])]
    ppermute x7, waiting for transfers between devices: 30 us -> 17.1 us  [layer_shards(): lax.ppermute(source, 'dp', [(i, i ^ near) for i in range(devices)])]
    pallas_call x27, Pallas kernels: 96.4 us -> 106 us  [call(): pl.pallas_call(body, out_shape=list(outs), input_output_aliases=aliases o...]
    unnamed x172 -> x102, local copies, waits for them, and re-layouts: 28.3 us -> 20.3 us
    ppermute x20, waiting for transfers between devices: 56.8 us -> 50.6 us  [xor_gather(): lax.ppermute(chunks[r ^ low], axis, [(i, i ^ low) for i in range(count)])]
  transfers between devices with their start and end apart: 62 -> 70, of which waited for: 34 -> 32; matrix products, arithmetic and copies ran while one was open for 2% -> 3% of each run, Pallas kernels for 22% -> 17%
where the time goes in v2:
time: 405 us; the launch traced here: 398 us
  waiting for transfers between devices  133 us (33%)
  starting transfers between devices  109 us (27%)
  Pallas kernels  106 us (26%)
  local copies, waits for them, and re-layouts  24.4 us (6%)
  between operations  15.3 us (4%)
  other arithmetic  9.88 us (2%)
    pallas_call x27, Pallas kernels, call(): pl.pallas_call(body, out_shape=list(outs), input_output_aliases=aliases o...  106 us
    ppermute x20, waiting for transfers between devices, xor_gather(): lax.ppermute(chunks[r ^ low], axis, [(i, i ^ low) for i in range(count)])  50.6 us
    ppermute x20, starting transfers between devices, xor_gather(): lax.ppermute(chunks[r ^ low], axis, [(i, i ^ low) for i in range(count)])  32.8 us
    ppermute x9, waiting for transfers between devices, halved(): came = lax.ppermute(odd, 'dp', [(i, i ^ bit) for i in range(devices)])  30.4 us
    ppermute x10, waiting for transfers between devices, xor_scatter(): lax.ppermute(total, axis, [(i, i ^ low) for i in range(count)])  26.6 us
    ppermute x9, starting transfers between devices, halved(): came = lax.ppermute(odd, 'dp', [(i, i ^ bit) for i in range(devices)])  25.1 us
    unnamed x102, local copies, waits for them, and re-layouts  20.3 us
    ppermute x7, starting transfers between devices, layer_shards(): lax.ppermute(add_parts(pending[r]), 'dp', [(i, i ^ near) for i in range(d...  20.2 us
  transfers between devices with their start and end apart: 70, of which 32 were waited for; matrix products, arithmetic and copies ran while one was open for 3% of the time, Pallas kernels for 17%

profile of v2, /device:TPU:0, one launch (start us, length us, event | category | flops | bytes accessed | tf_op | source)
XLA Modules:
  0.0 398.4 jit_solution(4955236800136520543)
XLA Ops:
  11.4 4.1 %collective-permute-start.6 = (bf16[128,896]{1,0:T(8,128)(2,1)S(1)}, bf16[128,896]{1,0:T(8,128)(2,1)S(1)}, u32[]{:S(2)}, u32[]{:S(2)}) collective-permute-start(bf16[128,896]{1,0:T(8,128)(2,1)S(1)} %constant_dynamic-update-slice_fusion.refs_4_.refs_0_.refs_9_), channel_id=1, source_target_pairs={{0,16},{4,20},{8,24},{12,28},{16,0},{20,4},{24,8},{28,12},{1,17},{... | collective-permute-start | bytes 688136 | tf_op jit(solution)/shard_map/ppermute | solution.py:404
  17.4 1.6 collective-permute-start.1
  20.5 1.6 collective-permute-start.4
  22.1 4.1 %collective-permute-done.6.refs_8_.refs_4_.refs_13_ = bf16[128,896]{1,0:T(8,128)(2,1)S(1)} collective-permute-done((bf16[128,896]{1,0:T(8,128)(2,1)S(1)}, bf16[128,896]{1,0:T(8,128)(2,1)S(1)}, u32[]{:S(2)}, u32[]{:S(2)}) %collective-permute-start.6) | collective-permute-done | bytes 229408 | tf_op jit(solution)/shard_map/ppermute | solution.py:404
  28.4 2.7 collective-permute-done.4.refs_6_.refs_2_.refs_11_
  32.6 3.3 collective-permute-done.8.refs_10_.refs_6_.refs_15_
  37.6 1.9 collective-permute-done.5.refs_7_.refs_3_.refs_12_
  39.6 4.4 %collective-permute-done.9.refs_11_.refs_7_.refs_16_ = bf16[128,896]{1,0:T(8,128)(2,1)S(1)} collective-permute-done((bf16[128,896]{1,0:T(8,128)(2,1)S(1)}, bf16[128,896]{1,0:T(8,128)(2,1)S(1)}, u32[]{:S(2)}, u32[]{:S(2)}) %collective-permute-start.9) | collective-permute-done | bytes 229408 | tf_op jit(solution)/shard_map/ppermute | solution.py:404
  44.0 1.6 shard_map.213
  45.6 3.4 collective-permute-start.13
  50.7 3.7 shard_map.214.refs_0_
  55.5 4.8 %collective-permute-done.13.refs_3_ = bf16[256,512]{1,0:T(8,128)(2,1)} collective-permute-done((bf16[256,512]{1,0:T(8,128)(2,1)}, bf16[256,512]{1,0:T(8,128)(2,1)}, u32[]{:S(2)}, u32[]{:S(2)}) %collective-permute-start.13) | collective-permute-done | bytes 262176 | tf_op jit(solution)/shard_map/ppermute | solution.py:1321
  66.7 2.1 collective-permute-done.15.refs_3_.refs_2_
  68.7 2.2 collective-permute-start.16
  71.0 7.1 %collective-permute-done.12.refs_2_ = bf16[256,512]{1,0:T(8,128)(2,1)S(1)} collective-permute-done((bf16[256,512]{1,0:T(8,128)(2,1)}, bf16[256,512]{1,0:T(8,128)(2,1)S(1)}, u32[]{:S(2)}, u32[]{:S(2)}) %collective-permute-start.12) | collective-permute-done | bytes 262176 | tf_op jit(solution)/shard_map/ppermute | solution.py:1321
  80.6 2.1 collective-permute-done.16.refs_2_.refs_1_
  89.9 6.4 %collective-permute-done.19.refs_2_ = bf16[128,1024]{1,0:T(8,128)(2,1)S(1)} collective-permute-done((bf16[128,1024]{1,0:T(8,128)(2,1)}, bf16[128,1024]{1,0:T(8,128)(2,1)S(1)}, u32[]{:S(2)}, u32[]{:S(2)}) %collective-permute-start.19) | collective-permute-done | bytes 262176 | tf_op jit(solution)/shard_map/ppermute | solution.py:416
  101.9 12.1 %collective-permute-start.23 = (bf16[128,1024]{1,0:T(8,128)(2,1)}, bf16[128,1024]{1,0:T(8,128)(2,1)}, u32[]{:S(2)}, u32[]{:S(2)}) collective-permute-start(bf16[128,1024]{1,0:T(8,128)(2,1)} %get-tuple-element.109.refs_0_), channel_id=1, source_target_pairs={{0,16},{4,20},{8,24},{12,28},{16,0},{20,4},{24,8},{28,12},{1,17},{... | collective-permute-start | bytes 786440 | tf_op jit(solution)/shard_map/ppermute | solution.py:404
  114.5 11.3 %collective-permute-done.23.refs_4_ = bf16[128,1024]{1,0:T(8,128)(2,1)} collective-permute-done((bf16[128,1024]{1,0:T(8,128)(2,1)}, bf16[128,1024]{1,0:T(8,128)(2,1)}, u32[]{:S(2)}, u32[]{:S(2)}) %collective-permute-start.23) | collective-permute-done | bytes 262176 | tf_op jit(solution)/shard_map/ppermute | solution.py:404
  126.5 2.0 collective-permute-start.20
  128.5 1.9 collective-permute-start.22
  130.5 3.8 collective-permute-done.25.refs_6_
  138.7 8.5 %collective-permute-done.22.refs_3_ = bf16[128,1024]{1,0:T(8,128)(2,1)} collective-permute-done((bf16[128,1024]{1,0:T(8,128)(2,1)}, bf16[128,1024]{1,0:T(8,128)(2,1)}, u32[]{:S(2)}, u32[]{:S(2)}) %collective-permute-start.22) | collective-permute-done | bytes 262176 | tf_op jit(solution)/shard_map/ppermute | solution.py:404
  147.2 4.6 %collective-permute-done.26.refs_7_ = bf16[128,1024]{1,0:T(8,128)(2,1)} collective-permute-done((bf16[128,1024]{1,0:T(8,128)(2,1)}, bf16[128,1024]{1,0:T(8,128)(2,1)}, u32[]{:S(2)}, u32[]{:S(2)}) %collective-permute-start.26) | collective-permute-done | bytes 262176 | tf_op jit(solution)/shard_map/ppermute | solution.py:404
  151.9 23.2 %shard_map.222 = (bf16[2,320,3584]{2,1,0:T(8,128)(2,1)}, bf16[2,320,3584]{2,1,0:T(8,128)(2,1)}, bf16[4,128,1024]{2,1,0:T(8,128)(2,1)}, bf16[4,128,1024]{2,1,0:T(...) custom-call(s32[13]{0:T(128)} %pad_add_fusion.sel_ref, ...), custom_call_target="tpu_custom_call" | custom-call | flops 26449999872 | tf_op jit(solution)/shard_map/pallas_call | solution.py:490
  178.7 5.9 %collective-permute-done.31 = bf16[128,1024]{1,0:T(8,128)(2,1)S(1)} collective-permute-done((bf16[128,1024]{1,0:T(8,128)(2,1)}, bf16[128,1024]{1,0:T(8,128)(2,1)S(1)}, u32[]{:S(2)}, u32[]{:S(2)}) %collective-permute-start.31) | collective-permute-done | bytes 262176 | tf_op jit(solution)/shard_map/ppermute | solution.py:416
  185.6 1.8 collective-permute-start.32
  188.1 2.1 collective-permute-done.28
  191.2 1.8 collective-permute-start.29
  193.0 2.8 collective-permute-done.30
  197.0 3.2 collective-permute-start.33
  200.2 8.0 %collective-permute-done.33.refs_3_ = bf16[128,1024]{1,0:T(8,128)(2,1)S(1)} collective-permute-done((bf16[128,1024]{1,0:T(8,128)(2,1)S(1)}, bf16[128,1024]{1,0:T(8,128)(2,1)S(1)}, u32[]{:S(2)}, u32[]{:S(2)}) %collective-permute-start.33) | collective-permute-done | bytes 262176 | tf_op jit(solution)/shard_map/ppermute | solution.py:416
  211.2 1.8 collective-permute-start.38
  214.4 6.0 %collective-permute-done.38.refs_2_.refs_7_ = bf16[128,1024]{1,0:T(8,128)(2,1)S(1)} collective-permute-done((bf16[128,1024]{1,0:T(8,128)(2,1)S(1)}, bf16[128,1024]{1,0:T(8,128)(2,1)S(1)}, u32[]{:S(2)}, u32[]{:S(2)}) %collective-permute-start.38) | collective-permute-done | bytes 262176 | tf_op jit(solution)/shard_map/ppermute | solution.py:404
  220.4 8.9 %collective-permute-done.34 = bf16[4,128,1024]{2,1,0:T(8,128)(2,1)S(1)} collective-permute-done((bf16[4,128,1024]{2,1,0:T(8,128)(2,1)S(1)}, bf16[4,128,1024]{2,1,0:T(8,128)(2,1)S(1)}, u32[]{:S(2)}, u32[]{:S(2)}) %collective-permute-start.34) | collective-permute-done | bytes 1048608 | tf_op jit(solution)/shard_map/ppermute | solution.py:1356
  229.8 4.2 %collective-permute-start.35 = (bf16[2,128,1024]{2,1,0:T(8,128)(2,1)S(1)}, bf16[2,128,1024]{2,1,0:T(8,128)(2,1)S(1)}, u32[]{:S(2)}, u32[]{:S(2)}) collective-permute-start(bf16[2,128,1024]{2,1,0:T(8,128)(2,1)S(1)} %slice.61), channel_id=1, source_target_pairs={{0,8},{4,12},{8,0},{12,4},{16,24},{20,28},{24,16},{28,20},{1,9},{5... | collective-permute-start | bytes 1572872 | tf_op jit(solution)/shard_map/ppermute | solution.py:1356
  236.4 1.6 shard_map.233
  238.4 2.0 collective-permute-start.57
  240.4 1.7 collective-permute-start.41
  242.1 1.8 shard_map.226
  245.0 2.6 collective-permute-start.47
  247.9 10.4 %collective-permute-start.36 = (bf16[1,128,1024]{2,1,0:T(8,128)(2,1)S(1)}, bf16[1,128,1024]{2,1,0:T(8,128)(2,1)S(1)}, u32[]{:S(2)}, u32[]{:S(2)}) collective-permute-start(bf16[1,128,1024]{2,1,0:T(8,128)(2,1)S(1)} %slice.81), channel_id=1, source_target_pairs={{0,16},{4,20},{8,24},{12,28},{16,0},{20,4},{24,8},{28,12},{1,17},{... | collective-permute-start | bytes 786440 | tf_op jit(solution)/shard_map/ppermute | solution.py:1356
  259.6 3.5 collective-permute-start.45
  263.0 4.0 %collective-permute-done.36 = bf16[1,128,1024]{2,1,0:T(8,128)(2,1)S(1)} collective-permute-done((bf16[1,128,1024]{2,1,0:T(8,128)(2,1)S(1)}, bf16[1,128,1024]{2,1,0:T(8,128)(2,1)S(1)}, u32[]{:S(2)}, u32[]{:S(2)}) %collective-permute-start.36) | collective-permute-done | bytes 262176 | tf_op jit(solution)/shard_map/ppermute | solution.py:1356
  267.9 5.2 %shard_map.228 = (bf16[256,512]{1,0:T(8,128)(2,1)S(1)}, bf16[256,512]{1,0:T(8,128)(2,1)S(1)}, bf16[256,512]{1,0:T(8,128)(2,1)S(1)}) custom-call(s32[1]{0:T(128)} %bitcast.2.off_ref, f32[128,2048]{1,0:T(8,128)S(1)} %get-tuple-element.139.refs_0_, bf16[128,2048]{1,0:T(8,128)(2,1)S(1)} %copy-done.32, bf16[256,512]{1,0:T(8,128)(2,1)} %collective-permute-done.11.refs_3_.refs_2_, ...), custom_call_target="tpu_custom_call" | custom-call | flops 2300000000 | tf_op jit(solution)/shard_map/pallas_call | solution.py:490
  275.4 1.8 collective-permute-start.44
  277.3 5.8 %collective-permute-done.43 = bf16[4,128,512]{2,1,0:T(8,128)(2,1)S(1)} collective-permute-done((bf16[4,128,512]{2,1,0:T(8,128)(2,1)S(1)}, bf16[4,128,512]{2,1,0:T(8,128)(2,1)S(1)}, u32[]{:S(2)}, u32[]{:S(2)}) %collective-permute-start.43) | collective-permute-done | bytes 524320 | tf_op jit(solution)/shard_map/ppermute | solution.py:1356
  283.1 6.5 %collective-permute-start.46 = (bf16[256,512]{1,0:T(8,128)(2,1)S(1)}, bf16[256,512]{1,0:T(8,128)(2,1)S(1)}, u32[]{:S(2)}, u32[]{:S(2)}) collective-permute-start(bf16[256,512]{1,0:T(8,128)(2,1)S(1)} %add_convert_fusion.7), channel_id=1, source_target_pairs={{0,16},{4,20},{8,24},{12,28},{16,0},{20,4},{24,8},{28,12},{1,17},{... | collective-permute-start | bytes 786440 | tf_op jit(solution)/shard_map/ppermute | solution.py:1395
  289.6 3.7 collective-permute-start.48
  294.3 12.2 %shard_map.230 = (f32[4,1024,512]{2,1,0:T(8,128)}, f32[4,1024,512]{2,1,0:T(8,128)}, f32[4,512,1024]{2,1,0:T(8,128)}) custom-call(s32[2]{0:T(128)} %pad_add_fusion.1.places_ref, bf16[2,320,3584]{2,1,0:T(8,128)(2,1)} %get-tuple-element.144.refs_0_.refs_1_.refs_2_.refs_3_.refs_4_, ...), custom_call_target="tpu_custom_call" | custom-call | flops 2300000000 | tf_op jit(solution)/shard_map/pallas_call | solution.py:490
  306.5 2.4 collective-permute-start.59
  308.9 1.8 shard_map.231
  313.5 15.2 %shard_map.234 = (bf16[2,320,3584]{2,1,0:T(8,128)(2,1)}, bf16[2,320,3584]{2,1,0:T(8,128)(2,1)}) custom-call(s32[13]{0:T(128)} %pad_add_fusion.sel_ref, bf16[8,128,1024]{2,1,0:T(8,128)(2,1)} %collective-permute-done.57.refs_0_, bf16[8,128,512]{2,1,0:T(8,128)(2,1)} %copy-done.46, bf16[8,128,512]{2,1,0:T(8,128)(2,1)} %copy-done.46, ...), custom_call_target="tpu_custom_call" | custom-call | flops 9200000000 | tf_op jit(solution)/shard_map/pallas_call | solution.py:490
  328.9 2.1 collective-permute-start.60
  332.1 4.4 %collective-permute-done.52 = f32[2,1024]{1,0:T(2,128)S(1)} collective-permute-done((f32[2,1024]{1,0:T(2,128)S(1)}, f32[2,1024]{1,0:T(2,128)S(1)}, u32[]{:S(2)}, u32[]{:S(2)}) %collective-permute-start.52) | collective-permute-done | bytes 8224 | tf_op jit(solution)/shard_map/ppermute | solution.py:1428
  338.0 4.0 collective-permute-start.63
  342.0 1.7 collective-permute-start.61
  345.6 4.7 %collective-permute-done.61 = bf16[4,128,256]{2,1,0:T(8,128)(2,1)S(1)} collective-permute-done((bf16[4,128,256]{2,1,0:T(8,128)(2,1)}, bf16[4,128,256]{2,1,0:T(8,128)(2,1)S(1)}, u32[]{:S(2)}, u32[]{:S(2)}) %collective-permute-start.61) | collective-permute-done | bytes 262176 | tf_op jit(solution)/shard_map/ppermute | solution.py:1356
  350.9 8.9 %shard_map.235 = (f32[4,1024,512]{2,1,0:T(8,128)}, f32[4,1024,512]{2,1,0:T(8,128)}, f32[4,512,1024]{2,1,0:T(8,128)}, bf16[1,3,2,512,512]{4,3,2,1,0:T(8,128)(2,1)}) custom-call(s32[2]{0:T(128)} %pad_add_fusion.1.places_ref, f32[4,1024,512]{2,1,0:T(8,128)} %get-tuple-element.146.refs_0_, ...), custom_call_target="tpu_custom_call", output_to_operand_aliasing={{0}: (1, {}), {1}: (2, {}), {2}: (3, {})} | custom-call | flops 1150000000 | tf_op jit(solution)/shard_map/pallas_call | solution.py:490
  360.0 9.3 %shard_map.236 = (f32[4,1024,512]{2,1,0:T(8,128)}, f32[4,1024,512]{2,1,0:T(8,128)}, f32[4,512,1024]{2,1,0:T(8,128)}, bf16[1,3,2,512,512]{4,3,2,1,0:T(8,128)(2,1)}) custom-call(s32[2]{0:T(128)} %pad_add_fusion.2.places_ref, f32[4,1024,512]{2,1,0:T(8,128)} %get-tuple-element.172.refs_0_, ...), custom_call_target="tpu_custom_call", output_to_operand_aliasing={{0}: (1, {}), {1}: (2, {}), {2}: (3, {})} | custom-call | flops 1150000000 | tf_op jit(solution)/shard_map/pallas_call | solution.py:490
  371.0 5.7 %collective-permute-done.66 = bf16[1,128,256]{2,1,0:T(8,128)(2,1)S(1)} collective-permute-done((bf16[1,128,256]{2,1,0:T(8,128)(2,1)S(1)}, bf16[1,128,256]{2,1,0:T(8,128)(2,1)S(1)}, u32[]{:S(2)}, u32[]{:S(2)}) %collective-permute-start.66) | collective-permute-done | bytes 65568 | tf_op jit(solution)/shard_map/ppermute | solution.py:1356
  378.9 2.7 collective-permute-done.55
  381.7 4.2 %shard_map.237 = (f32[4,1024,512]{2,1,0:T(8,128)}, f32[4,1024,512]{2,1,0:T(8,128)}, f32[4,512,1024]{2,1,0:T(8,128)}) custom-call(s32[1]{0:T(128)} %bitcast.16.place_ref, f32[4,1024,512]{2,1,0:T(8,128)} %get-tuple-element.176.refs_0_, f32[4,1024,512]{2,1,0:T(8,128)} %get-tuple-element.177.refs_1_, ...), custom_call_target="tpu_custom_call", output_to_operand_aliasing={{0}: (1, {}), {1}: (2, {}), {2}: (3, {})} | custom-call | flops 4600000000 | tf_op jit(solution)/shard_map/pallas_call | solution.py:490
  385.9 4.2 %shard_map.238 = (f32[4,1024,512]{2,1,0:T(8,128)}, f32[4,1024,512]{2,1,0:T(8,128)}, f32[4,512,1024]{2,1,0:T(8,128)}) custom-call(s32[1]{0:T(128)} %bitcast.24.place_ref, f32[4,1024,512]{2,1,0:T(8,128)} %get-tuple-element.181.refs_0_, f32[4,1024,512]{2,1,0:T(8,128)} %get-tuple-element.183.refs_1_, ...), custom_call_target="tpu_custom_call", output_to_operand_aliasing={{0}: (1, {}), {1}: (2, {}), {2}: (3, {})} | custom-call | flops 4600000000 | tf_op jit(solution)/shard_map/pallas_call | solution.py:490
  (259 shorter events, 77.8 us)
Async XLA Ops:
  7.2 144.7 %all-gather.3.cloned.1.call-start = ((), (), s32[]{:S(2)}) async-start(), calls=%async_computation | async-start | bytes 2359296 | tf_op jit(solution)/shard_map/all_gather | solution.py:1324
  11.4 14.7 %collective-permute-start.6 = (bf16[128,896]{1,0:T(8,128)(2,1)S(1)}, bf16[128,896]{1,0:T(8,128)(2,1)S(1)}, u32[]{:S(2)}, u32[]{:S(2)}) collective-permute-start(bf16[128,896]{1,0:T(8,128)(2,1)S(1)} %constant_dynamic-update-slice_fusion.refs_4_.refs_0_.refs_9_), channel_id=1, source_target_pairs={{0,16},{4,20},{8,24},{12,28},{16,0},{20,4},{24,8},{28,12},{1,17},{... | collective-permute-start | bytes 688136 | tf_op jit(solution)/shard_map/ppermute | solution.py:404
  17.4 20.3 %collective-permute-start = (bf16[128,1024]{1,0:T(8,128)(2,1)S(1)}, bf16[128,1024]{1,0:T(8,128)(2,1)S(1)}, u32[]{:S(2)}, u32[]{:S(2)}) collective-permute-start(bf16[128,1024]{1,0:T(8,128)(2,1)S(1)} %shard_map.212.refs_0_.refs_5_), channel_id=1, source_target_pairs={{0,1},{1,0},{2,3},{3,2},{4,5},{5,4},{6,7},{7,6},{8,9},{9,8},{10,11... | collective-permute-start | bytes 786440 | tf_op jit(solution)/shard_map/ppermute | solution.py:404
  17.4 15.2 %collective-permute-start.1 = (bf16[128,1024]{1,0:T(8,128)(2,1)S(1)}, bf16[128,1024]{1,0:T(8,128)(2,1)S(1)}, u32[]{:S(2)}, u32[]{:S(2)}) collective-permute-start(bf16[128,1024]{1,0:T(8,128)(2,1)S(1)} %shard_map.212.refs_0_.refs_5_), channel_id=1, source_target_pairs={{0,2},{1,3},{2,0},{3,1},{4,6},{5,7},{6,4},{7,5},{8,10},{9,11},{10,... | collective-permute-start | bytes 786440 | tf_op jit(solution)/shard_map/ppermute | solution.py:404
  19.0 7.9 %collective-permute-start.3 = (bf16[128,896]{1,0:T(8,128)(2,1)S(1)}, bf16[128,896]{1,0:T(8,128)(2,1)S(1)}, u32[]{:S(2)}, u32[]{:S(2)}) collective-permute-start(bf16[128,896]{1,0:T(8,128)(2,1)S(1)} %constant_dynamic-update-slice_fusion.refs_4_.refs_0_.refs_9_), channel_id=1, source_target_pairs={{0,4},{4,0},{8,12},{12,8},{16,20},{20,16},{24,28},{28,24},{1,5},{5... | collective-permute-start | bytes 688136 | tf_op jit(solution)/shard_map/ppermute | solution.py:404
  20.5 10.5 %collective-permute-start.4 = (bf16[128,896]{1,0:T(8,128)(2,1)S(1)}, bf16[128,896]{1,0:T(8,128)(2,1)S(1)}, u32[]{:S(2)}, u32[]{:S(2)}) collective-permute-start(bf16[128,896]{1,0:T(8,128)(2,1)S(1)} %constant_dynamic-update-slice_fusion.refs_4_.refs_0_.refs_9_), channel_id=1, source_target_pairs={{0,8},{4,12},{8,0},{12,4},{16,24},{20,28},{24,16},{28,20},{1,9},{5... | collective-permute-start | bytes 688136 | tf_op jit(solution)/shard_map/ppermute | solution.py:404
  26.1 9.7 %collective-permute-start.8 = (bf16[128,896]{1,0:T(8,128)(2,1)S(1)}, bf16[128,896]{1,0:T(8,128)(2,1)S(1)}, u32[]{:S(2)}, u32[]{:S(2)}) collective-permute-start(bf16[128,896]{1,0:T(8,128)(2,1)S(1)} %collective-permute-done.6.refs_8_.refs_4_.refs_13_), channel_id=1, source_target_pairs={{0,8},{4,12},{8,0},{12,4},{16,24},{20,28},{24,16},{28,20},{1,9},{5... | collective-permute-start | bytes 688136 | tf_op jit(solution)/shard_map/ppermute | solution.py:404
  26.9 12.7 %collective-permute-start.7 = (bf16[128,896]{1,0:T(8,128)(2,1)S(1)}, bf16[128,896]{1,0:T(8,128)(2,1)S(1)}, u32[]{:S(2)}, u32[]{:S(2)}) collective-permute-start(bf16[128,896]{1,0:T(8,128)(2,1)S(1)} %collective-permute-done.6.refs_8_.refs_4_.refs_13_), channel_id=1, source_target_pairs={{0,4},{4,0},{8,12},{12,8},{16,20},{20,16},{24,28},{28,24},{1,5},{5... | collective-permute-start | bytes 688136 | tf_op jit(solution)/shard_map/ppermute | solution.py:404
  31.1 8.5 %collective-permute-start.5 = (bf16[128,896]{1,0:T(8,128)(2,1)S(1)}, bf16[128,896]{1,0:T(8,128)(2,1)S(1)}, u32[]{:S(2)}, u32[]{:S(2)}) collective-permute-start(bf16[128,896]{1,0:T(8,128)(2,1)S(1)} %collective-permute-done.4.refs_6_.refs_2_.refs_11_), channel_id=1, source_target_pairs={{0,4},{4,0},{8,12},{12,8},{16,20},{20,16},{24,28},{28,24},{1,5},{5... | collective-permute-start | bytes 688136 | tf_op jit(solution)/shard_map/ppermute | solution.py:404
  32.6 7.0 %collective-permute-start.2 = (bf16[128,1024]{1,0:T(8,128)(2,1)S(1)}, bf16[128,1024]{1,0:T(8,128)(2,1)S(1)}, u32[]{:S(2)}, u32[]{:S(2)}) collective-permute-start(bf16[128,1024]{1,0:T(8,128)(2,1)S(1)} %collective-permute-done.1.refs_2_.refs_7_), channel_id=1, source_target_pairs={{0,1},{1,0},{2,3},{3,2},{4,5},{5,4},{6,7},{7,6},{8,9},{9,8},{10,11... | collective-permute-start | bytes 786440 | tf_op jit(solution)/shard_map/ppermute | solution.py:404
  35.9 8.1 %collective-permute-start.9 = (bf16[128,896]{1,0:T(8,128)(2,1)S(1)}, bf16[128,896]{1,0:T(8,128)(2,1)S(1)}, u32[]{:S(2)}, u32[]{:S(2)}) collective-permute-start(bf16[128,896]{1,0:T(8,128)(2,1)S(1)} %collective-permute-done.8.refs_10_.refs_6_.refs_15_), channel_id=1, source_target_pairs={{0,4},{4,0},{8,12},{12,8},{16,20},{20,16},{24,28},{28,24},{1,5},{5... | collective-permute-start | bytes 688136 | tf_op jit(solution)/shard_map/ppermute | solution.py:404
  45.6 14.8 %collective-permute-start.13 = (bf16[256,512]{1,0:T(8,128)(2,1)}, bf16[256,512]{1,0:T(8,128)(2,1)}, u32[]{:S(2)}, u32[]{:S(2)}) collective-permute-start(bf16[256,512]{1,0:T(8,128)(2,1)} %get-tuple-element.101.refs_1_.refs_3_), channel_id=1, source_target_pairs={{0,16},{4,20},{8,24},{12,28},{16,0},{20,4},{24,8},{28,12},{1,17},{... | collective-permute-start | bytes 786440 | tf_op jit(solution)/shard_map/ppermute | solution.py:1321
  48.9 14.2 %collective-permute-start.10 = (bf16[256,512]{1,0:T(8,128)(2,1)}, bf16[256,512]{1,0:T(8,128)(2,1)}, u32[]{:S(2)}, u32[]{:S(2)}) collective-permute-start(bf16[256,512]{1,0:T(8,128)(2,1)} %get-tuple-element.101.refs_1_.refs_3_), channel_id=1, source_target_pairs={{0,4},{4,0},{8,12},{12,8},{16,20},{20,16},{24,28},{28,24},{1,5},{5... | collective-permute-start | bytes 786440 | tf_op jit(solution)/shard_map/ppermute | solution.py:1321
  50.4 12.2 %collective-permute-start.11 = (bf16[256,512]{1,0:T(8,128)(2,1)}, bf16[256,512]{1,0:T(8,128)(2,1)}, u32[]{:S(2)}, u32[]{:S(2)}) collective-permute-start(bf16[256,512]{1,0:T(8,128)(2,1)} %get-tuple-element.101.refs_1_.refs_3_), channel_id=1, source_target_pairs={{0,8},{4,12},{8,0},{12,4},{16,24},{20,28},{24,16},{28,20},{1,9},{5... | collective-permute-start | bytes 786440 | tf_op jit(solution)/shard_map/ppermute | solution.py:1321
  60.3 8.4 %collective-permute-start.15 = (bf16[256,512]{1,0:T(8,128)(2,1)}, bf16[256,512]{1,0:T(8,128)(2,1)}, u32[]{:S(2)}, u32[]{:S(2)}) collective-permute-start(bf16[256,512]{1,0:T(8,128)(2,1)} %collective-permute-done.13.refs_3_), channel_id=1, source_target_pairs={{0,8},{4,12},{8,0},{12,4},{16,24},{20,28},{24,16},{28,20},{1,9},{5... | collective-permute-start | bytes 786440 | tf_op jit(solution)/shard_map/ppermute | solution.py:1321
  60.3 19.0 %collective-permute-start.14 = (bf16[256,512]{1,0:T(8,128)(2,1)}, bf16[256,512]{1,0:T(8,128)(2,1)}, u32[]{:S(2)}, u32[]{:S(2)}) collective-permute-start(bf16[256,512]{1,0:T(8,128)(2,1)} %collective-permute-done.13.refs_3_), channel_id=1, source_target_pairs={{0,4},{4,0},{8,12},{12,8},{16,20},{20,16},{24,28},{28,24},{1,5},{5... | collective-permute-start | bytes 786440 | tf_op jit(solution)/shard_map/ppermute | solution.py:1321
  62.6 15.5 %collective-permute-start.12 = (bf16[256,512]{1,0:T(8,128)(2,1)}, bf16[256,512]{1,0:T(8,128)(2,1)S(1)}, u32[]{:S(2)}, u32[]{:S(2)}) collective-permute-start(bf16[256,512]{1,0:T(8,128)(2,1)} %collective-permute-done.11.refs_3_.refs_2_), channel_id=1, source_target_pairs={{0,4},{4,0},{8,12},{12,8},{16,20},{20,16},{24,28},{28,24},{1,5},{5... | collective-permute-start | bytes 786440 | tf_op jit(solution)/shard_map/ppermute | solution.py:1321
  68.7 13.9 %collective-permute-start.16 = (bf16[256,512]{1,0:T(8,128)(2,1)}, bf16[256,512]{1,0:T(8,128)(2,1)S(1)}, u32[]{:S(2)}, u32[]{:S(2)}) collective-permute-start(bf16[256,512]{1,0:T(8,128)(2,1)} %collective-permute-done.15.refs_3_.refs_2_), channel_id=1, source_target_pairs={{0,4},{4,0},{8,12},{12,8},{16,20},{20,16},{24,28},{28,24},{1,5},{5... | collective-permute-start | bytes 786440 | tf_op jit(solution)/shard_map/ppermute | solution.py:1321
  87.8 8.6 %collective-permute-start.19 = (bf16[128,1024]{1,0:T(8,128)(2,1)}, bf16[128,1024]{1,0:T(8,128)(2,1)S(1)}, u32[]{:S(2)}, u32[]{:S(2)}) collective-permute-start(bf16[128,1024]{1,0:T(8,128)(2,1)} %add_convert_fusion.13), channel_id=1, source_target_pairs={{0,2},{1,3},{2,0},{3,1},{4,6},{5,7},{6,4},{7,5},{8,10},{9,11},{10,... | collective-permute-start | bytes 786440 | tf_op jit(solution)/shard_map/ppermute | solution.py:416
  101.9 23.8 %collective-permute-start.23 = (bf16[128,1024]{1,0:T(8,128)(2,1)}, bf16[128,1024]{1,0:T(8,128)(2,1)}, u32[]{:S(2)}, u32[]{:S(2)}) collective-permute-start(bf16[128,1024]{1,0:T(8,128)(2,1)} %get-tuple-element.109.refs_0_), channel_id=1, source_target_pairs={{0,16},{4,20},{8,24},{12,28},{16,0},{20,4},{24,8},{28,12},{1,17},{... | collective-permute-start | bytes 786440 | tf_op jit(solution)/shard_map/ppermute | solution.py:404
  114.1 14.5 %collective-permute-start.21 = (bf16[128,1024]{1,0:T(8,128)(2,1)}, bf16[128,1024]{1,0:T(8,128)(2,1)}, u32[]{:S(2)}, u32[]{:S(2)}) collective-permute-start(bf16[128,1024]{1,0:T(8,128)(2,1)} %get-tuple-element.109.refs_0_), channel_id=1, source_target_pairs={{0,8},{4,12},{8,0},{12,4},{16,24},{20,28},{24,16},{28,20},{1,9},{5... | collective-permute-start | bytes 786440 | tf_op jit(solution)/shard_map/ppermute | solution.py:404
  125.8 8.5 %collective-permute-start.25 = (bf16[128,1024]{1,0:T(8,128)(2,1)}, bf16[128,1024]{1,0:T(8,128)(2,1)}, u32[]{:S(2)}, u32[]{:S(2)}) collective-permute-start(bf16[128,1024]{1,0:T(8,128)(2,1)} %collective-permute-done.23.refs_4_), channel_id=1, source_target_pairs={{0,8},{4,12},{8,0},{12,4},{16,24},{20,28},{24,16},{28,20},{1,9},{5... | collective-permute-start | bytes 786440 | tf_op jit(solution)/shard_map/ppermute | solution.py:404
  126.5 12.3 %collective-permute-start.20 = (bf16[128,1024]{1,0:T(8,128)(2,1)}, bf16[128,1024]{1,0:T(8,128)(2,1)}, u32[]{:S(2)}, u32[]{:S(2)}) collective-permute-start(bf16[128,1024]{1,0:T(8,128)(2,1)} %get-tuple-element.109.refs_0_), channel_id=1, source_target_pairs={{0,4},{4,0},{8,12},{12,8},{16,20},{20,16},{24,28},{28,24},{1,5},{5... | collective-permute-start | bytes 786440 | tf_op jit(solution)/shard_map/ppermute | solution.py:404
  128.4 18.8 %collective-permute-start.24 = (bf16[128,1024]{1,0:T(8,128)(2,1)}, bf16[128,1024]{1,0:T(8,128)(2,1)}, u32[]{:S(2)}, u32[]{:S(2)}) collective-permute-start(bf16[128,1024]{1,0:T(8,128)(2,1)} %collective-permute-done.23.refs_4_), channel_id=1, source_target_pairs={{0,4},{4,0},{8,12},{12,8},{16,20},{20,16},{24,28},{28,24},{1,5},{5... | collective-permute-start | bytes 786440 | tf_op jit(solution)/shard_map/ppermute | solution.py:404
  128.5 18.7 %collective-permute-start.22 = (bf16[128,1024]{1,0:T(8,128)(2,1)}, bf16[128,1024]{1,0:T(8,128)(2,1)}, u32[]{:S(2)}, u32[]{:S(2)}) collective-permute-start(bf16[128,1024]{1,0:T(8,128)(2,1)} %collective-permute-done.21.refs_2_), channel_id=1, source_target_pairs={{0,4},{4,0},{8,12},{12,8},{16,20},{20,16},{24,28},{28,24},{1,5},{5... | collective-permute-start | bytes 786440 | tf_op jit(solution)/shard_map/ppermute | solution.py:404
  134.3 17.6 %collective-permute-start.26 = (bf16[128,1024]{1,0:T(8,128)(2,1)}, bf16[128,1024]{1,0:T(8,128)(2,1)}, u32[]{:S(2)}, u32[]{:S(2)}) collective-permute-start(bf16[128,1024]{1,0:T(8,128)(2,1)} %collective-permute-done.25.refs_6_), channel_id=1, source_target_pairs={{0,4},{4,0},{8,12},{12,8},{16,20},{20,16},{24,28},{28,24},{1,5},{5... | collective-permute-start | bytes 786440 | tf_op jit(solution)/shard_map/ppermute | solution.py:404
  175.1 9.5 %collective-permute-start.31 = (bf16[128,1024]{1,0:T(8,128)(2,1)}, bf16[128,1024]{1,0:T(8,128)(2,1)S(1)}, u32[]{:S(2)}, u32[]{:S(2)}) collective-permute-start(bf16[128,1024]{1,0:T(8,128)(2,1)} %get-tuple-element.120), channel_id=1, source_target_pairs={{0,4},{4,0},{8,12},{12,8},{16,20},{20,16},{24,28},{28,24},{1,5},{5... | collective-permute-start | bytes 786440 | tf_op jit(solution)/shard_map/ppermute | solution.py:416
  176.6 13.6 %collective-permute-start.28 = (bf16[128,1024]{1,0:T(8,128)(2,1)}, bf16[128,1024]{1,0:T(8,128)(2,1)S(1)}, u32[]{:S(2)}, u32[]{:S(2)}) collective-permute-start(bf16[128,1024]{1,0:T(8,128)(2,1)} %get-tuple-element.116), channel_id=1, source_target_pairs={{0,4},{4,0},{8,12},{12,8},{16,20},{20,16},{24,28},{28,24},{1,5},{5... | collective-permute-start | bytes 786440 | tf_op jit(solution)/shard_map/ppermute | solution.py:416
  177.2 18.7 %collective-permute-start.30 = (bf16[128,1024]{1,0:T(8,128)(2,1)}, bf16[128,1024]{1,0:T(8,128)(2,1)S(1)}, u32[]{:S(2)}, u32[]{:S(2)}) collective-permute-start(bf16[128,1024]{1,0:T(8,128)(2,1)} %get-tuple-element.118), channel_id=1, source_target_pairs={{0,4},{4,0},{8,12},{12,8},{16,20},{20,16},{24,28},{28,24},{1,5},{5... | collective-permute-start | bytes 786440 | tf_op jit(solution)/shard_map/ppermute | solution.py:416
  185.6 10.2 %collective-permute-start.32 = (bf16[128,1024]{1,0:T(8,128)(2,1)S(1)}, bf16[128,1024]{1,0:T(8,128)(2,1)S(1)}, u32[]{:S(2)}, u32[]{:S(2)}) collective-permute-start(bf16[128,1024]{1,0:T(8,128)(2,1)S(1)} %add_convert_fusion.11), channel_id=1, source_target_pairs={{0,8},{4,12},{8,0},{12,4},{16,24},{20,28},{24,16},{28,20},{1,9},{5... | collective-permute-start | bytes 786440 | tf_op jit(solution)/shard_map/ppermute | solution.py:416
  187.4 12.8 %collective-permute-start.27 = (bf16[128,1024]{1,0:T(8,128)(2,1)}, bf16[128,1024]{1,0:T(8,128)(2,1)S(1)}, u32[]{:S(2)}, u32[]{:S(2)}) collective-permute-start(bf16[128,1024]{1,0:T(8,128)(2,1)} %get-tuple-element.114), channel_id=1, source_target_pairs={{0,4},{4,0},{8,12},{12,8},{16,20},{20,16},{24,28},{28,24},{1,5},{5... | collective-permute-start | bytes 786440 | tf_op jit(solution)/shard_map/ppermute | solution.py:416
  191.2 9.0 %collective-permute-start.29 = (bf16[128,1024]{1,0:T(8,128)(2,1)S(1)}, bf16[128,1024]{1,0:T(8,128)(2,1)S(1)}, u32[]{:S(2)}, u32[]{:S(2)}) collective-permute-start(bf16[128,1024]{1,0:T(8,128)(2,1)S(1)} %add_convert_fusion.12), channel_id=1, source_target_pairs={{0,8},{4,12},{8,0},{12,4},{16,24},{20,28},{24,16},{28,20},{1,9},{5... | collective-permute-start | bytes 786440 | tf_op jit(solution)/shard_map/ppermute | solution.py:416
  197.0 11.2 %collective-permute-start.33 = (bf16[128,1024]{1,0:T(8,128)(2,1)S(1)}, bf16[128,1024]{1,0:T(8,128)(2,1)S(1)}, u32[]{:S(2)}, u32[]{:S(2)}) collective-permute-start(bf16[128,1024]{1,0:T(8,128)(2,1)S(1)} %add_convert_fusion.10), channel_id=1, source_target_pairs={{0,16},{4,20},{8,24},{12,28},{16,0},{20,4},{24,8},{28,12},{1,17},{... | collective-permute-start | bytes 786440 | tf_op jit(solution)/shard_map/ppermute | solution.py:416
  200.2 89.4 %collective-permute-start.42 = (bf16[2,320,3584]{2,1,0:T(8,128)(2,1)}, bf16[2,320,3584]{2,1,0:T(8,128)(2,1)S(1)}, u32[]{:S(2)}, u32[]{:S(2)}) collective-permute-start(bf16[2,320,3584]{2,1,0:T(8,128)(2,1)} %get-tuple-element.145), channel_id=1, source_target_pairs={{0,1},{1,0},{2,3},{3,2},{4,5},{5,4},{6,7},{7,6},{8,9},{9,8},{10,11... | collective-permute-start | bytes 13762568 | tf_op jit(solution)/shard_map/ppermute | solution.py:1341
  209.7 19.6 %collective-permute-start.34 = (bf16[4,128,1024]{2,1,0:T(8,128)(2,1)S(1)}, bf16[4,128,1024]{2,1,0:T(8,128)(2,1)S(1)}, u32[]{:S(2)}, u32[]{:S(2)}) collective-permute-start(bf16[4,128,1024]{2,1,0:T(8,128)(2,1)S(1)} %copy-done.47), channel_id=1, source_target_pairs={{0,4},{4,0},{8,12},{12,8},{16,20},{20,16},{24,28},{28,24},{1,5},{5... | collective-permute-start | bytes 3145736 | tf_op jit(solution)/shard_map/ppermute | solution.py:1356
  211.2 9.2 %collective-permute-start.38 = (bf16[128,1024]{1,0:T(8,128)(2,1)S(1)}, bf16[128,1024]{1,0:T(8,128)(2,1)S(1)}, u32[]{:S(2)}, u32[]{:S(2)}) collective-permute-start(bf16[128,1024]{1,0:T(8,128)(2,1)S(1)} %get-tuple-element.126.refs_0_.refs_5_), channel_id=1, source_target_pairs={{0,2},{1,3},{2,0},{3,1},{4,6},{5,7},{6,4},{7,5},{8,10},{9,11},{10,... | collective-permute-start | bytes 786440 | tf_op jit(solution)/shard_map/ppermute | solution.py:404
  214.2 24.2 %collective-permute-start.56 = (bf16[8,128,512]{2,1,0:T(8,128)(2,1)S(1)}, bf16[8,128,512]{2,1,0:T(8,128)(2,1)S(1)}, u32[]{:S(2)}, u32[]{:S(2)}) collective-permute-start(bf16[8,128,512]{2,1,0:T(8,128)(2,1)S(1)} %get-tuple-element.198), channel_id=1, source_target_pairs={{0,2},{1,3},{2,0},{3,1},{4,6},{5,7},{6,4},{7,5},{8,10},{9,11},{10,... | collective-permute-start | bytes 3145736 | tf_op jit(solution)/shard_map/ppermute | solution.py:1333
  214.4 19.6 %collective-permute-start.37 = (bf16[128,1024]{1,0:T(8,128)(2,1)S(1)}, bf16[128,1024]{1,0:T(8,128)(2,1)S(1)}, u32[]{:S(2)}, u32[]{:S(2)}) collective-permute-start(bf16[128,1024]{1,0:T(8,128)(2,1)S(1)} %get-tuple-element.126.refs_0_.refs_5_), channel_id=1, source_target_pairs={{0,1},{1,0},{2,3},{3,2},{4,5},{5,4},{6,7},{7,6},{8,9},{9,8},{10,11... | collective-permute-start | bytes 786440 | tf_op jit(solution)/shard_map/ppermute | solution.py:404
  220.4 13.6 %collective-permute-start.39 = (bf16[128,1024]{1,0:T(8,128)(2,1)S(1)}, bf16[128,1024]{1,0:T(8,128)(2,1)S(1)}, u32[]{:S(2)}, u32[]{:S(2)}) collective-permute-start(bf16[128,1024]{1,0:T(8,128)(2,1)S(1)} %collective-permute-done.38.refs_2_.refs_7_), channel_id=1, source_target_pairs={{0,1},{1,0},{2,3},{3,2},{4,5},{5,4},{6,7},{7,6},{8,9},{9,8},{10,11... | collective-permute-start | bytes 786440 | tf_op jit(solution)/shard_map/ppermute | solution.py:404
  229.8 17.8 %collective-permute-start.35 = (bf16[2,128,1024]{2,1,0:T(8,128)(2,1)S(1)}, bf16[2,128,1024]{2,1,0:T(8,128)(2,1)S(1)}, u32[]{:S(2)}, u32[]{:S(2)}) collective-permute-start(bf16[2,128,1024]{2,1,0:T(8,128)(2,1)S(1)} %slice.61), channel_id=1, source_target_pairs={{0,8},{4,12},{8,0},{12,4},{16,24},{20,28},{24,16},{28,20},{1,9},{5... | collective-permute-start | bytes 1572872 | tf_op jit(solution)/shard_map/ppermute | solution.py:1356
  236.0 9.0 %collective-permute-start.40 = (bf16[256,512]{1,0:T(8,128)(2,1)S(1)}, bf16[256,512]{1,0:T(8,128)(2,1)S(1)}, u32[]{:S(2)}, u32[]{:S(2)}) collective-permute-start(bf16[256,512]{1,0:T(8,128)(2,1)S(1)} %get-tuple-element.133), channel_id=1, source_target_pairs={{0,4},{4,0},{8,12},{12,8},{16,20},{20,16},{24,28},{28,24},{1,5},{5... | collective-permute-start | bytes 786440 | tf_op jit(solution)/shard_map/ppermute | solution.py:1395
  238.4 74.5 %collective-permute-start.57 = (bf16[8,128,1024]{2,1,0:T(8,128)(2,1)S(1)}, bf16[8,128,1024]{2,1,0:T(8,128)(2,1)}, u32[]{:S(2)}, u32[]{:S(2)}) collective-permute-start(bf16[8,128,1024]{2,1,0:T(8,128)(2,1)S(1)} %shard_map.233), channel_id=1, source_target_pairs={{0,2},{1,3},{2,0},{3,1},{4,6},{5,7},{6,4},{7,5},{8,10},{9,11},{10,... | collective-permute-start | bytes 6291464 | tf_op jit(solution)/shard_map/ppermute | solution.py:1352
  240.4 19.1 %collective-permute-start.41 = (bf16[256,512]{1,0:T(8,128)(2,1)S(1)}, bf16[256,512]{1,0:T(8,128)(2,1)S(1)}, u32[]{:S(2)}, u32[]{:S(2)}) collective-permute-start(bf16[256,512]{1,0:T(8,128)(2,1)S(1)} %get-tuple-element.137), channel_id=1, source_target_pairs={{0,4},{4,0},{8,12},{12,8},{16,20},{20,16},{24,28},{28,24},{1,5},{5... | collective-permute-start | bytes 786440 | tf_op jit(solution)/shard_map/ppermute | solution.py:1395
  245.0 29.8 %collective-permute-start.47 = (bf16[256,512]{1,0:T(8,128)(2,1)S(1)}, bf16[256,512]{1,0:T(8,128)(2,1)S(1)}, u32[]{:S(2)}, u32[]{:S(2)}) collective-permute-start(bf16[256,512]{1,0:T(8,128)(2,1)S(1)} %get-tuple-element.153), channel_id=1, source_target_pairs={{0,4},{4,0},{8,12},{12,8},{16,20},{20,16},{24,28},{28,24},{1,5},{5... | collective-permute-start | bytes 786440 | tf_op jit(solution)/shard_map/ppermute | solution.py:1395
  247.9 19.2 %collective-permute-start.36 = (bf16[1,128,1024]{2,1,0:T(8,128)(2,1)S(1)}, bf16[1,128,1024]{2,1,0:T(8,128)(2,1)S(1)}, u32[]{:S(2)}, u32[]{:S(2)}) collective-permute-start(bf16[1,128,1024]{2,1,0:T(8,128)(2,1)S(1)} %slice.81), channel_id=1, source_target_pairs={{0,16},{4,20},{8,24},{12,28},{16,0},{20,4},{24,8},{28,12},{1,17},{... | collective-permute-start | bytes 786440 | tf_op jit(solution)/shard_map/ppermute | solution.py:1356
  259.6 15.9 %collective-permute-start.45 = (bf16[256,512]{1,0:T(8,128)(2,1)S(1)}, bf16[256,512]{1,0:T(8,128)(2,1)S(1)}, u32[]{:S(2)}, u32[]{:S(2)}) collective-permute-start(bf16[256,512]{1,0:T(8,128)(2,1)S(1)} %add_convert_fusion.8), channel_id=1, source_target_pairs={{0,8},{4,12},{8,0},{12,4},{16,24},{20,28},{24,16},{28,20},{1,9},{5... | collective-permute-start | bytes 786440 | tf_op jit(solution)/shard_map/ppermute | solution.py:1395
  273.9 9.2 %collective-permute-start.43 = (bf16[4,128,512]{2,1,0:T(8,128)(2,1)S(1)}, bf16[4,128,512]{2,1,0:T(8,128)(2,1)S(1)}, u32[]{:S(2)}, u32[]{:S(2)}) collective-permute-start(bf16[4,128,512]{2,1,0:T(8,128)(2,1)S(1)} %get-tuple-element.147), channel_id=1, source_target_pairs={{0,4},{4,0},{8,12},{12,8},{16,20},{20,16},{24,28},{28,24},{1,5},{5... | collective-permute-start | bytes 1572872 | tf_op jit(solution)/shard_map/ppermute | solution.py:1356
  274.8 38.1 %collective-permute-start.58 = (bf16[8,128,512]{2,1,0:T(8,128)(2,1)}, bf16[8,128,512]{2,1,0:T(8,128)(2,1)}, u32[]{:S(2)}, u32[]{:S(2)}) collective-permute-start(bf16[8,128,512]{2,1,0:T(8,128)(2,1)} %get-tuple-element.166), channel_id=1, source_target_pairs={{0,2},{1,3},{2,0},{3,1},{4,6},{5,7},{6,4},{7,5},{8,10},{9,11},{10,... | collective-permute-start | bytes 3145736 | tf_op jit(solution)/shard_map/ppermute | solution.py:1351
  275.4 31.1 %collective-permute-start.44 = (bf16[256,512]{1,0:T(8,128)(2,1)}, bf16[256,512]{1,0:T(8,128)(2,1)S(1)}, u32[]{:S(2)}, u32[]{:S(2)}) collective-permute-start(bf16[256,512]{1,0:T(8,128)(2,1)} %get-tuple-element.149), channel_id=1, source_target_pairs={{0,4},{4,0},{8,12},{12,8},{16,20},{20,16},{24,28},{28,24},{1,5},{5... | collective-permute-start | bytes 786440 | tf_op jit(solution)/shard_map/ppermute | solution.py:1395
  283.1 25.8 %collective-permute-start.46 = (bf16[256,512]{1,0:T(8,128)(2,1)S(1)}, bf16[256,512]{1,0:T(8,128)(2,1)S(1)}, u32[]{:S(2)}, u32[]{:S(2)}) collective-permute-start(bf16[256,512]{1,0:T(8,128)(2,1)S(1)} %add_convert_fusion.7), channel_id=1, source_target_pairs={{0,16},{4,20},{8,24},{12,28},{16,0},{20,4},{24,8},{28,12},{1,17},{... | collective-permute-start | bytes 786440 | tf_op jit(solution)/shard_map/ppermute | solution.py:1395
  289.6 19.3 %collective-permute-start.48 = (bf16[256,512]{1,0:T(8,128)(2,1)S(1)}, bf16[256,512]{1,0:T(8,128)(2,1)S(1)}, u32[]{:S(2)}, u32[]{:S(2)}) collective-permute-start(bf16[256,512]{1,0:T(8,128)(2,1)S(1)} %add_convert_fusion.6), channel_id=1, source_target_pairs={{0,8},{4,12},{8,0},{12,4},{16,24},{20,28},{24,16},{28,20},{1,9},{5... | collective-permute-start | bytes 786440 | tf_op jit(solution)/shard_map/ppermute | solution.py:1395
  328.7 22.1 %collective-permute-start.62 = (bf16[2,320,3584]{2,1,0:T(8,128)(2,1)}, bf16[2,320,3584]{2,1,0:T(8,128)(2,1)}, u32[]{:S(2)}, u32[]{:S(2)}) collective-permute-start(bf16[2,320,3584]{2,1,0:T(8,128)(2,1)} %get-tuple-element.171), channel_id=1, source_target_pairs={{0,1},{1,0},{2,3},{3,2},{4,5},{5,4},{6,7},{7,6},{8,9},{9,8},{10,11... | collective-permute-start | bytes 13762568 | tf_op jit(solution)/shard_map/ppermute | solution.py:1438
  328.9 9.1 %collective-permute-start.60 = (bf16[2,128,512]{2,1,0:T(8,128)(2,1)S(1)}, bf16[2,128,512]{2,1,0:T(8,128)(2,1)S(1)}, u32[]{:S(2)}, u32[]{:S(2)}) collective-permute-start(bf16[2,128,512]{2,1,0:T(8,128)(2,1)S(1)} %slice.65), channel_id=1, source_target_pairs={{0,8},{4,12},{8,0},{12,4},{16,24},{20,28},{24,16},{28,20},{1,9},{5... | collective-permute-start | bytes 786440 | tf_op jit(solution)/shard_map/ppermute | solution.py:1356
  331.8 12.3 %collective-permute-start.50 = (bf16[128,1024]{1,0:T(8,128)(2,1)S(1)}, bf16[128,1024]{1,0:T(8,128)(2,1)S(1)}, u32[]{:S(2)}, u32[]{:S(2)}) collective-permute-start(bf16[128,1024]{1,0:T(8,128)(2,1)S(1)} %copy-done.22), channel_id=1, source_target_pairs={{0,1},{1,0},{2,3},{3,2},{4,5},{5,4},{6,7},{7,6},{8,9},{9,8},{10,11... | collective-permute-start | bytes 786440 | tf_op jit(solution)/shard_map/ppermute | solution.py:1420
  336.6 7.2 %collective-permute-start.53 = (f32[2,1024]{1,0:T(2,128)S(1)}, f32[2,1024]{1,0:T(2,128)S(1)}, u32[]{:S(2)}, u32[]{:S(2)}) collective-permute-start(f32[2,1024]{1,0:T(2,128)S(1)} %fusion.9), channel_id=1, source_target_pairs={{0,2},{1,3},{2,0},{3,1},{4,6},{5,7},{6,4},{7,5},{8,10},{9,11},{10,... | collective-permute-start | bytes 24584 | tf_op jit(solution)/shard_map/ppermute | solution.py:1428
  338.0 21.8 %collective-permute-start.63 = (bf16[1,128,512]{2,1,0:T(8,128)(2,1)S(1)}, bf16[1,128,512]{2,1,0:T(8,128)(2,1)S(1)}, u32[]{:S(2)}, u32[]{:S(2)}) collective-permute-start(bf16[1,128,512]{2,1,0:T(8,128)(2,1)S(1)} %slice.83), channel_id=1, source_target_pairs={{0,16},{4,20},{8,24},{12,28},{16,0},{20,4},{24,8},{28,12},{1,17},{... | collective-permute-start | bytes 393224 | tf_op jit(solution)/shard_map/ppermute | solution.py:1356
  342.0 8.3 %collective-permute-start.61 = (bf16[4,128,256]{2,1,0:T(8,128)(2,1)}, bf16[4,128,256]{2,1,0:T(8,128)(2,1)S(1)}, u32[]{:S(2)}, u32[]{:S(2)}) collective-permute-start(bf16[4,128,256]{2,1,0:T(8,128)(2,1)} %copy-done.20), channel_id=1, source_target_pairs={{0,4},{4,0},{8,12},{12,8},{16,20},{20,16},{24,28},{28,24},{1,5},{5... | collective-permute-start | bytes 786440 | tf_op jit(solution)/shard_map/ppermute | solution.py:1356
  343.7 16.2 %collective-permute-start.54 = (f32[2,1024]{1,0:T(2,128)S(1)}, f32[2,1024]{1,0:T(2,128)S(1)}, u32[]{:S(2)}, u32[]{:S(2)}) collective-permute-start(f32[2,1024]{1,0:T(2,128)S(1)} %fusion.14), channel_id=1, source_target_pairs={{0,4},{4,0},{8,12},{12,8},{16,20},{20,16},{24,28},{28,24},{1,5},{5... | collective-permute-start | bytes 24584 | tf_op jit(solution)/shard_map/ppermute | solution.py:1428
  344.2 15.8 %collective-permute-start.51 = (bf16[128,1024]{1,0:T(8,128)(2,1)S(1)}, bf16[128,1024]{1,0:T(8,128)(2,1)S(1)}, u32[]{:S(2)}, u32[]{:S(2)}) collective-permute-start(bf16[128,1024]{1,0:T(8,128)(2,1)S(1)} %add_convert_fusion.5), channel_id=1, source_target_pairs={{0,2},{1,3},{2,0},{3,1},{4,6},{5,7},{6,4},{7,5},{8,10},{9,11},{10,... | collective-permute-start | bytes 786440 | tf_op jit(solution)/shard_map/ppermute | solution.py:1420
  350.4 9.5 %collective-permute-start.64 = (bf16[2,128,256]{2,1,0:T(8,128)(2,1)S(1)}, bf16[2,128,256]{2,1,0:T(8,128)(2,1)S(1)}, u32[]{:S(2)}, u32[]{:S(2)}) collective-permute-start(bf16[2,128,256]{2,1,0:T(8,128)(2,1)S(1)} %slice.69), channel_id=1, source_target_pairs={{0,8},{4,12},{8,0},{12,4},{16,24},{20,28},{24,16},{28,20},{1,9},{5... | collective-permute-start | bytes 393224 | tf_op jit(solution)/shard_map/ppermute | solution.py:1356
  359.8 21.9 %collective-permute-start.65 = (bf16[1,3,2,512,512]{4,3,2,1,0:T(8,128)(2,1)}, bf16[1,3,2,512,512]{4,3,2,1,0:T(8,128)(2,1)}, u32[]{:S(2)}, u32[]{:S(2)}) collective-permute-start(bf16[1,3,2,512,512]{4,3,2,1,0:T(8,128)(2,1)} %get-tuple-element.179), channel_id=1, source_target_pairs={{0,1},{1,0},{2,3},{3,2},{4,5},{5,4},{6,7},{7,6},{8,9},{9,8},{10,11... | collective-permute-start | bytes 9437192 | tf_op jit(solution)/shard_map/ppermute | solution.py:1448
  369.3 16.6 %collective-permute-start.68 = (bf16[1,3,2,512,512]{4,3,2,1,0:T(8,128)(2,1)}, bf16[1,3,2,512,512]{4,3,2,1,0:T(8,128)(2,1)}, u32[]{:S(2)}, u32[]{:S(2)}) collective-permute-start(bf16[1,3,2,512,512]{4,3,2,1,0:T(8,128)(2,1)} %get-tuple-element.185), channel_id=1, source_target_pairs={{0,1},{1,0},{2,3},{3,2},{4,5},{5,4},{6,7},{7,6},{8,9},{9,8},{10,11... | collective-permute-start | bytes 9437192 | tf_op jit(solution)/shard_map/ppermute | solution.py:1448
  369.9 6.9 %collective-permute-start.49 = (bf16[128,1024]{1,0:T(8,128)(2,1)S(1)}, bf16[128,1024]{1,0:T(8,128)(2,1)S(1)}, u32[]{:S(2)}, u32[]{:S(2)}) collective-permute-start(bf16[128,1024]{1,0:T(8,128)(2,1)S(1)} %copy-done.19), channel_id=1, source_target_pairs={{0,1},{1,0},{2,3},{3,2},{4,5},{5,4},{6,7},{7,6},{8,9},{9,8},{10,11... | collective-permute-start | bytes 786440 | tf_op jit(solution)/shard_map/ppermute | solution.py:1420
  370.0 6.7 %collective-permute-start.66 = (bf16[1,128,256]{2,1,0:T(8,128)(2,1)S(1)}, bf16[1,128,256]{2,1,0:T(8,128)(2,1)S(1)}, u32[]{:S(2)}, u32[]{:S(2)}) collective-permute-start(bf16[1,128,256]{2,1,0:T(8,128)(2,1)S(1)} %slice.85), channel_id=1, source_target_pairs={{0,16},{4,20},{8,24},{12,28},{16,0},{20,4},{24,8},{28,12},{1,17},{... | collective-permute-start | bytes 196616 | tf_op jit(solution)/shard_map/ppermute | solution.py:1356
  (55 other events, 548.6 us)
Sparse Core Ops, SparseCore 0:
  61.9 51.6 all-gather.2
